TPU v7x, 128 devices: a whole 4x4x4 slice. The times are simulated.
128 devices in a mesh: grp: 4 (over z), dom: 32 (over x, y, core).
Axes of the slice: x: 4, y: 4, z: 4, core: 2. Of those that a mesh axis runs over, the one named last changes fastest.
Arguments:
- operator_blocks: float32 [512, 16, 4096], P(('grp', 'dom')), may hold values from -0.75 to 0.75
- operator_cols: int32 [512, 16], P(('grp', 'dom')), may hold values from 0 to 31, as said below
- halo_count: int32 [512], P(('grp', 'dom')), may hold values from 2 to 4, as said below
- prolong_blocks: float32 [512, 8, 4096], P(('grp', 'dom')), may hold values from -0.75 to 0.75
- prolong_cols: int32 [512, 8], P(('grp', 'dom')), may hold values from 0 to 255, as said below
- prolong_slot: int32 [512, 8], P(('grp', 'dom')), may hold values from 0 to 63, as said below
- send_lists: int32 [128, 32], P(('grp', 'dom')), may hold values from 0 to 3
- slot_owner_row: int32 [128, 64], P(('grp', 'dom')), may hold values from 0 to 2, as said below
- coarse_pattern: int32 [256, 16], P(('grp', 'dom')), may hold values from 0 to 255, as said below
Outputs:
- coarse_blocks: float32 [256, 16, 4096], P(('grp', 'dom'))
Inputs may be any that keep to these rules, and one draw needn't show every extreme that they name: `operator_cols`: slots below 12 hold values below 16, the others values below 32. Slots at or beyond a row's live count hold valid values whose blocks do not count. `halo_count`: the first fine row of every device has 4. `prolong_cols`: the 8 values of a row are different. A row on grp index g names coarse rows owned by devices of grp index g only. Slot t of device v stands for owner dom index t // 2 and owner coarse row slot_owner_row[v, t]; prolong_cols[i, j] = ((v // 32) * 32 + s // 2) * 2 + slot_owner_row[v, s] for s = prolong_slot[i, j]; the slots of a row are different and never empty. `slot_owner_row`: the value 2 marks an empty slot; the live values of one device for one owner are different; every device fills all 2 slots of its own dom index and the first slot of every owner, and no other slot. `coarse_pattern`: the 16 values of a row are different.
All inputs are finite; a program needn't handle non-finite values.
Results may differ from a plain program's by a relative error of at most 0.0003.
Values sent between devices are 32-bit elements; how exact they have to be, the bound alone decides.
No kernel may reach another device: no remote copies, remote signals or barrier semaphores. Data moves between devices by JAX's collectives and lax.ppermute only.
A program may use at most 128 MiB of HBM per device.

v0:
```python
import functools

import jax
import jax.numpy as jnp
from jax import lax
from jax.experimental import pallas as pl
from jax.experimental.pallas import tpu as pltpu
from jax.sharding import PartitionSpec as P

BS = 64
KG = 12
KH = 4
KA = 16
KP = 8
KC = 16
RB = 4
PAIRS = RB * KP
NEAR_E = KG * KP
FAR_E = KH * KP
LANES = 128
STEP = 4
ROW_T = KP * BS * BS // LANES


def split(x):
    hi = x.astype(jnp.bfloat16)
    lo = (x - hi.astype(jnp.float32)).astype(jnp.bfloat16)
    return hi, lo


def paired(blocks):
    rows, n, _ = blocks.shape
    view = blocks.reshape(rows, n // 2, 2, BS, BS)
    return view.transpose(0, 1, 3, 2, 4).reshape(rows, n // 2, BS, LANES)


def first_half(shape):
    return lax.broadcasted_iota(jnp.int32, shape, 1) < BS


def put_right(right_ref, slot, table):
    for s in range(4):
        hi, lo = split(table(s))
        cols = slice(s * LANES, (s + 1) * LANES)
        right_ref[slot, 0:64, cols] = hi
        right_ref[slot, 64:128, cols] = hi
        right_ref[slot, 128:192, cols] = lo
        right_ref[slot, 192:256, cols] = lo


def spread_rows(a_ref, spread_ref):
    for t in range(a_ref.shape[1] // 8):
        for k in range(BS // 2):
            part = a_ref[0, t * 8 : (t + 1) * 8, k * LANES : (k + 1) * LANES]
            spread_ref[pl.ds(t * 8 * (BS // 2) + k, 8, stride=BS // 2), :] = part


def left_of(two):
    hi = two.astype(jnp.bfloat16).astype(jnp.float32)
    lo = pltpu.roll(two - hi, BS, axis=1)
    first = first_half(two.shape)
    rows = jnp.concatenate([jnp.where(first, hi, lo), jnp.where(first, lo, hi)], axis=0).astype(jnp.bfloat16)
    return jnp.concatenate([rows, rows], axis=1)


def put_weights(w_ref, m, w):
    for s in range(4):
        pair = w[:, s * LANES : (s + 1) * LANES]
        w_ref[0, m * 4 + s] = pair
        w_ref[1, m * 4 + s] = pltpu.roll(pair, BS, axis=1)


def add_matches(list_ref, base, count, w_ref, m_ref):
    half = lax.broadcasted_iota(jnp.int32, (BS, LANES), 1) // BS

    def body(k, carry):
        codes = [list_ref[base + k * STEP + t] for t in range(STEP)]
        parts = []
        for code in codes:
            e = code >> 4
            odd = code & 1
            parts.append(jnp.where(half == odd, w_ref[(e ^ code) & 1, e >> 1], 0.0))
        for code, part in zip(codes, parts):
            m_ref[(code & 15) >> 1] += part
        return carry

    lax.fori_loop(0, (count + STEP - 1) // STEP, body, 0)


def near_kernel(
    cols_ref, list_ref, count_ref, a_ref, p0, p1, p2, p3, m_ref, left_ref, right_ref, w_ref, spread_ref
):
    i = pl.program_id(0)

    @pl.when(i == 0)
    def _():
        for k, ref in enumerate((p0, p1, p2, p3)):

            def put(r, carry, k=k, ref=ref):
                def table(s):
                    return ref[pl.ds(pl.multiple_of(r * ROW_T + s * BS, BS), BS), :]

                put_right(right_ref, k * RB + r, table)
                return carry

            lax.fori_loop(0, RB, put, 0)

    for s in range(4):
        base = pl.multiple_of(i * ROW_T + s * BS, BS)
        slab = jnp.concatenate(
            [p0[pl.ds(base, BS // 2, stride=2), :], p0[pl.ds(base + 1, BS // 2, stride=2), :]], axis=0
        )
        hi = slab.astype(jnp.bfloat16).astype(jnp.float32)
        lo = slab - hi
        high = jnp.concatenate([hi, hi], axis=0).T.astype(jnp.bfloat16)
        low = jnp.concatenate([lo, lo], axis=0).T.astype(jnp.bfloat16)
        for t in range(2):
            left_ref[0, 2 * s + t, 0:BS, :] = high[t * BS : (t + 1) * BS]
            left_ref[0, 2 * s + t, BS : 2 * BS, :] = low[t * BS : (t + 1) * BS]

    for t in range(2):
        w_ref[t, NEAR_E // 2] = jnp.zeros((BS, LANES), jnp.float32)
    spread_rows(a_ref, spread_ref)
    for m in range(KG):
        left = left_of(spread_ref[m * (BS // 2) : (m + 1) * (BS // 2), :])
        w = jnp.dot(left, right_ref[cols_ref[i * KG + m]], preferred_element_type=jnp.float32)
        put_weights(w_ref, m, w)

    def per_target(j, carry):
        m_ref[0, j] = jnp.zeros((KC // 2, BS, LANES), jnp.float32)
        add_matches(list_ref, (i * KP + j) * NEAR_E, count_ref[i * KP + j], w_ref, m_ref.at[0, j])
        return carry

    lax.fori_loop(0, KP, per_target, 0)


def far_kernel(
    cols_ref, list_ref, count_ref, pos_ref, a_ref, f0, f1, f2, f3, m_ref, left_ref,
    out0, out1, out2, out3, out4, right_ref, w_ref, wide_ref, acc_ref, spread_ref, sems,
):
    i = pl.program_id(0)
    n_pos = acc_ref.shape[0]

    @pl.when(i == 0)
    def _():
        def clear(k, carry):
            acc_ref[k] = jnp.zeros(acc_ref.shape[1:], jnp.float32)
            return carry

        lax.fori_loop(0, n_pos, clear, 0)

    far = (f0, f1, f2, f3)
    for t in range(2):
        w_ref[t, FAR_E // 2] = jnp.zeros((BS, LANES), jnp.float32)
    spread_rows(a_ref, spread_ref)
    for m in range(KH):
        here = (KG % 8 + m) * (BS // 2)
        left = left_of(spread_ref[here : here + BS // 2, :])

        def table(s, m=m):
            return far[m][0, s * BS : (s + 1) * BS, :]

        put_right(right_ref, m, table)
        w = jnp.dot(left, right_ref[m], preferred_element_type=jnp.float32)
        put_weights(w_ref, m, w)

    def per_two(jj, carry):
        for t in range(2):
            j = jj * 2 + t
            here = i * KP + j
            add_matches(list_ref, here * FAR_E, count_ref[here], w_ref, m_ref.at[0, j])
        outs = []
        for t in range(2):
            j = jj * 2 + t
            for s in range(KC // 2):
                hi, lo = split(m_ref[0, j, s])
                cols = slice(s * LANES, (s + 1) * LANES)
                wide_ref[t, 0:64, cols] = hi
                wide_ref[t, 64:128, cols] = lo
            outs.append(jnp.dot(left_ref[0, j], wide_ref[t], preferred_element_type=jnp.float32))
        for t in range(2):
            pos = pos_ref[i * KP + jj * 2 + t]
            for s in range(KC // 2):
                cols = slice(s * LANES, (s + 1) * LANES)
                acc_ref[pos, s * BS : (s + 1) * BS, :] += outs[t][0:BS, cols] + outs[t][BS : 2 * BS, cols]
        return carry

    lax.fori_loop(0, KP // 2, per_two, 0)

    @pl.when(i == pl.num_programs(0) - 1)
    def _():
        copies = [
            pltpu.make_async_copy(acc_ref.at[pl.ds(k * 8, out.shape[0])], out, sems.at[k])
            for k, out in enumerate((out0, out1, out2, out3, out4))
        ]
        for copy in copies:
            copy.start()
        for copy in copies:
            copy.wait()


def final_kernel(mine_ref, got_ref, out_ref, spread_ref):
    half = BS // 2
    first = first_half((half, LANES))
    for s in range(KC // 2):
        even, odd = (pl.ds(s * BS + o, half, stride=2) for o in range(2))
        even = mine_ref[0, even, :] + got_ref[0, even, :]
        odd = mine_ref[0, odd, :] + got_ref[0, odd, :]
        spread_ref[2 * s * half : (2 * s + 1) * half, :] = jnp.where(first, even, pltpu.roll(odd, BS, axis=1))
        spread_ref[(2 * s + 1) * half : (2 * s + 2) * half, :] = jnp.where(first, pltpu.roll(even, BS, axis=1), odd)
    for t in range(KC // 8):
        for k in range(half):
            out_ref[0, t * 8 : (t + 1) * 8, k * LANES : (k + 1) * LANES] = spread_ref[
                pl.ds(t * 8 * half + k, 8, stride=half), :
            ]


def outgoing_kernel(pick_ref, p_ref, out_ref, sem):
    n = out_ref.shape[0]

    def copy(k):
        src = p_ref.at[pl.ds(pl.multiple_of(pick_ref[k] * ROW_T, ROW_T), ROW_T)]
        return pltpu.make_async_copy(src, out_ref.at[k], sem.at[k])

    def start(k, carry):
        copy(k).start()
        return carry

    def wait(k, carry):
        copy(k).wait()
        return carry

    lax.fori_loop(0, n, start, 0)
    lax.fori_loop(0, n, wait, 0)


def match_lists(wanted, ids, live):
    n = ids.shape[1]
    eq = wanted[:, :, None] == ids[:, None, :]
    c_of = jnp.sum(jnp.where(eq, jnp.arange(KC, dtype=jnp.int32)[None, :, None], 0), axis=1)
    hit = jnp.any(eq, axis=1) & live
    number = jnp.arange(n, dtype=jnp.int32)
    before = jnp.sum(jnp.where((number[:, None] < number[None, :])[None], hit[:, :, None].astype(jnp.int32), 0), axis=1)
    code = number[None, :] * KC + c_of
    here = hit[:, None, :] & (before[:, None, :] == number[None, :, None])
    count = jnp.sum(hit.astype(jnp.int32), axis=1)
    lists = jnp.sum(jnp.where(here, code[:, None, :], 0), axis=2)
    lists = jnp.where(number[None, :] < count[:, None], lists, n * KC)
    return lists.reshape(-1), count


def pick_rows(table, index):
    n = table.shape[0]
    one = index[:, None] == jnp.arange(n, dtype=jnp.int32)[None, :]
    return jnp.sum(jnp.where(one[:, :, None], table[None], 0), axis=1)


def near_call(cols, lists, counts, operator_blocks, near_rows):
    row_block = pl.BlockSpec((RB * ROW_T, LANES), lambda i, *_: (0, 0))
    return pl.pallas_call(
        near_kernel,
        out_shape=(
            jax.ShapeDtypeStruct((RB, KP, KC // 2, BS, LANES), jnp.float32),
            jax.ShapeDtypeStruct((RB, KP, LANES, LANES), jnp.bfloat16),
        ),
        grid_spec=pltpu.PrefetchScalarGridSpec(
            num_scalar_prefetch=3,
            grid=(RB,),
            in_specs=[pl.BlockSpec((1, KA, BS * BS), lambda i, *_: (i, 0, 0))] + [row_block] * 4,
            out_specs=(
                pl.BlockSpec((1, KP, KC // 2, BS, LANES), lambda i, *_: (i, 0, 0, 0, 0)),
                pl.BlockSpec((1, KP, LANES, LANES), lambda i, *_: (i, 0, 0, 0)),
            ),
            scratch_shapes=[
                pltpu.VMEM((4 * RB, 256, KP * BS), jnp.bfloat16),
                pltpu.VMEM((2, NEAR_E // 2 + 1, BS, LANES), jnp.float32),
                pltpu.VMEM((KA * BS // 2, LANES), jnp.float32),
            ],
        ),
        compiler_params=pltpu.CompilerParams(vmem_limit_bytes=40 * 2**20),
        cost_estimate=pl.CostEstimate(flops=10**10, bytes_accessed=16 * 2**20, transcendentals=0),
        name="near",
    )(cols, lists, counts, operator_blocks, *near_rows)


def far_call(cols, lists, counts, position, operator_blocks, far_rows, matched, left, n_dom):
    far_spec = lambda m: pl.BlockSpec((1, ROW_T, LANES), lambda i, cols, *_: (cols[i * KH + m], 0, 0))
    slot_shape = (KC // 2 * BS, LANES)
    return pl.pallas_call(
        far_kernel,
        out_shape=tuple(jax.ShapeDtypeStruct((n,) + slot_shape, jnp.float32) for n in (8, 8, 8, 8, 1)),
        grid_spec=pltpu.PrefetchScalarGridSpec(
            num_scalar_prefetch=4,
            grid=(RB,),
            in_specs=[pl.BlockSpec((1, 8, BS * BS), lambda i, *_: (i, 1, 0))]
            + [far_spec(m) for m in range(KH)]
            + [
                pl.BlockSpec((1, KP, KC // 2, BS, LANES), lambda i, *_: (i, 0, 0, 0, 0)),
                pl.BlockSpec((1, KP, LANES, LANES), lambda i, *_: (i, 0, 0, 0)),
            ],
            out_specs=(pl.BlockSpec(memory_space=pltpu.HBM),) * 5,
            scratch_shapes=[
                pltpu.VMEM((KH, 256, KP * BS), jnp.bfloat16),
                pltpu.VMEM((2, FAR_E // 2 + 1, BS, LANES), jnp.float32),
                pltpu.VMEM((2, LANES, KC * BS), jnp.bfloat16),
                pltpu.VMEM((n_dom + 1,) + slot_shape, jnp.float32),
                pltpu.VMEM((8 * BS // 2, LANES), jnp.float32),
                pltpu.SemaphoreType.DMA((5,)),
            ],
        ),
        compiler_params=pltpu.CompilerParams(vmem_limit_bytes=40 * 2**20),
        cost_estimate=pl.CostEstimate(flops=10**10, bytes_accessed=24 * 2**20, transcendentals=0),
        name="far",
    )(cols, lists, counts, position, operator_blocks, *([far_rows] * KH), matched, left)


SIDE = 4


def places(device, me):
    x, y, k = device // (2 * SIDE), device // 2 % SIDE, device % 2
    return jnp.where(me % 2 == 0, x, y), jnp.where(me % 2 == 0, y, x), k


def device_at(u, v, k, me):
    u, v, k = u % SIDE, v % SIDE, k % 2
    return (jnp.where(me % 2 == 0, u, v) * SIDE + jnp.where(me % 2 == 0, v, u)) * 2 + k


def shift_pairs(shift, phase):
    pairs = []
    for x in range(SIDE):
        for y in range(SIDE):
            for k in range(2):
                along_x = (k == 0) == (phase == 0)
                to_x, to_y = ((x + shift) % SIDE, y) if along_x else (x, (y + shift) % SIDE)
                pairs.append(((x * SIDE + y) * 2 + k, (to_x * SIDE + to_y) * 2 + k))
    return pairs


def per_device(
    operator_blocks,
    operator_cols,
    halo_count,
    prolong_blocks,
    prolong_cols,
    prolong_slot,
    send_lists,
    slot_owner_row,
    coarse_pattern,
):
    n_dom = lax.axis_size("dom")
    n_grp = lax.axis_size("grp")
    g = lax.axis_index("grp")
    d = lax.axis_index("dom")
    owner = slot_owner_row.reshape(-1)

    panels = paired(prolong_blocks).reshape(RB * ROW_T, LANES)
    outgoing = pl.pallas_call(
        outgoing_kernel,
        out_shape=jax.ShapeDtypeStruct((n_dom, ROW_T, LANES), jnp.float32),
        grid_spec=pltpu.PrefetchScalarGridSpec(
            num_scalar_prefetch=1,
            grid=(1,),
            in_specs=[pl.BlockSpec((RB * ROW_T, LANES), lambda i, *_: (0, 0))],
            out_specs=pl.BlockSpec(memory_space=pltpu.HBM),
            scratch_shapes=[pltpu.SemaphoreType.DMA((n_dom,))],
        ),
        name="outgoing",
    )(send_lists.reshape(-1), panels)
    far_rows = lax.all_to_all(outgoing, "dom", split_axis=0, concat_axis=0, tiled=True)

    id_tile = jnp.pad(prolong_cols.reshape(1, PAIRS).astype(jnp.float32), ((0, 7), (0, LANES - PAIRS)))
    carried = jnp.concatenate([panels, id_tile], axis=0)
    near_rows = [carried]
    for k in range(1, n_grp):
        near_rows.append(lax.ppermute(carried, "grp", [((z + k) % n_grp, z) for z in range(n_grp)]))

    mine = jnp.concatenate(
        [prolong_cols.reshape(-1), coarse_pattern.reshape(-1), send_lists.reshape(-1), owner.reshape(n_dom, 2)[:, 0]]
    )
    told = lax.all_to_all(
        jnp.broadcast_to(mine[None], (n_dom, mine.shape[0])), "dom", split_axis=0, concat_axis=0, tiled=True
    )
    all_cols = told[:, :PAIRS].reshape(n_dom, RB, KP)
    patterns = told[:, PAIRS : 2 * PAIRS].reshape(2 * n_dom, KC)
    here = jnp.arange(n_dom, dtype=jnp.int32)[None, :] == d
    picked = jnp.sum(jnp.where(here, told[:, 2 * PAIRS : 2 * PAIRS + n_dom], 0), axis=1)
    first_rows = told[:, 2 * PAIRS + n_dom :]
    far_ids = jnp.sum(
        jnp.where((picked[:, None] == jnp.arange(RB, dtype=jnp.int32))[:, :, None], all_cols, 0), axis=1
    )

    slots = prolong_slot.reshape(-1)
    slot_row = pick_rows(owner[:, None], slots)[:, 0]
    wanted = pick_rows(patterns, (slots // 2) * 2 + slot_row)
    u, v, k = places(d, d)
    to_u, to_v, to_k = places(slots // 2, d)
    position = ((to_u - u) % SIDE) * 8 + ((to_v - v) % SIDE) * 2 + (to_k - k) % 2
    position = jnp.where(slots % 2 == 1, n_dom, position)

    near_ids_table = jnp.concatenate(
        [rows[RB * ROW_T, :PAIRS].astype(jnp.int32).reshape(RB, KP) for rows in near_rows], axis=0
    )
    near_slots = operator_cols[:, :KG]
    near_cols = (((near_slots // RB) - g) % n_grp * RB + near_slots % RB).reshape(-1)
    far_cols = operator_cols[:, KG:].reshape(-1)
    near_ids = pick_rows(near_ids_table, near_cols).reshape(RB, NEAR_E)
    far_ids = pick_rows(far_ids, far_cols).reshape(RB, FAR_E)
    live = jnp.arange(KH, dtype=jnp.int32)[None, :] < halo_count[:, None]
    spread = lambda x: jnp.repeat(x, KP, axis=0)
    near_list, near_count = match_lists(wanted, spread(near_ids), jnp.ones((PAIRS, NEAR_E), bool))
    far_list, far_count = match_lists(wanted, spread(far_ids), spread(jnp.repeat(live, KP, axis=1)))

    matched, left = near_call(near_cols, near_list, near_count, operator_blocks, near_rows)
    chunks = far_call(far_cols, far_list, far_count, position, operator_blocks, far_rows, matched, left, n_dom)
    slot_shape = (KC // 2 * BS, LANES)

    arriving = [chunks[0]] + [lax.ppermute(chunks[t], "dom", shift_pairs(t, 0)) for t in range(1, SIDE)]
    sources = jnp.stack([device_at(u - t, v, k, d) for t in range(SIDE)])
    owners = jnp.stack([device_at(u, v + p // 2, k + p % 2, d) for p in range(8)])
    rows_from = pick_rows(first_rows, sources)
    row_of = pick_rows(rows_from.T, owners).T
    own_first = row_of[0, 0]

    def owned(t2):
        total = 0.0
        for t in range(SIDE):
            part = arriving[t][2 * t2 : 2 * t2 + 2][:, None]
            to_row = row_of[t, 2 * t2 : 2 * t2 + 2][:, None] == jnp.arange(2, dtype=jnp.int32)
            total = total + jnp.where(to_row[:, :, None, None], part, 0.0)
        if t2 == 0:
            to_row = (jnp.arange(2, dtype=jnp.int32) == 1 - own_first)[None] & (jnp.arange(2) == 0)[:, None]
            total = total + jnp.where(to_row[:, :, None, None], chunks[4][:, None], 0.0)
        return total

    sent = {t2: lax.ppermute(owned(t2), "dom", shift_pairs(t2, 1)) for t2 in (2, 1, 3)}
    kept = owned(0)
    sums = [kept[kk] + sent[1][kk] + sent[2][kk] + sent[3][kk] for kk in (1, 0)]
    swapped = lax.ppermute(sums[0], "dom", [(n, n ^ 1) for n in range(n_dom)])

    row_spec = pl.BlockSpec((1,) + slot_shape, lambda i: (i, 0, 0))
    return pl.pallas_call(
        final_kernel,
        out_shape=jax.ShapeDtypeStruct((2, KC, BS * BS), jnp.float32),
        grid=(2,),
        in_specs=[row_spec, row_spec],
        out_specs=pl.BlockSpec((1, KC, BS * BS), lambda i: (i, 0, 0)),
        scratch_shapes=[pltpu.VMEM((KC * BS // 2, LANES), jnp.float32)],
        name="final",
    )(sums[1], swapped)


def solution(mesh):
    return jax.shard_map(
        per_device,
        mesh=mesh,
        in_specs=(
            P(("grp", "dom"), None, None),
            P(("grp", "dom"), None),
            P(("grp", "dom")),
            P(("grp", "dom"), None, None),
            P(("grp", "dom"), None),
            P(("grp", "dom"), None),
            P(("grp", "dom"), None),
            P(("grp", "dom"), None),
            P(("grp", "dom"), None),
        ),
        out_specs=P(("grp", "dom"), None, None),
        check_vma=False,
    )
```

profile of v0, /device:TPU:1, one launch (start us, length us, event | category | flops | bytes accessed | tf_op | source)
XLA Modules:
  0.0 195.2 jit_solution(6701905893404682233)
XLA Ops:
  0.0 0.7 convert_convert_fusion
  0.8 1.5 reshape.876
  2.3 0.8 copy.26
  3.1 0.6 reshape_reshape.7.p_ref
  3.8 2.5 %collective-permute-start.2 = (f32[1032,128]{1,0:T(8,128)S(1)}, f32[1032,128]{1,0:T(8,128)S(1)}, u32[]{:S(2)}, u32[]{:S(2)}) collective-permute-start(f32[1032,128]{1,0:T(8,128)S(1)} %select_maximum_fusion.p0), channel_id=1, source_target_pairs={{96,0},{0,32},{32,64},{64,96},{97,1},{1,33},{33,65},{65,97},{98,2}... | collective-permute-start | bytes 1585160 | tf_op jit(solution)/shard_map/ppermute | solution.py:377
  6.3 3.3 %collective-permute-start.1 = (f32[1032,128]{1,0:T(8,128)S(1)}, f32[1032,128]{1,0:T(8,128)S(1)}, u32[]{:S(2)}, u32[]{:S(2)}) collective-permute-start(f32[1032,128]{1,0:T(8,128)S(1)} %select_maximum_fusion.p0), channel_id=1, source_target_pairs={{64,0},{96,32},{0,64},{32,96},{65,1},{97,33},{1,65},{33,97},{66,2}... | collective-permute-start | bytes 1585160 | tf_op jit(solution)/shard_map/ppermute | solution.py:377
  9.6 0.7 collective-permute-start
  10.5 0.5 broadcast.587
  11.0 0.6 reduce.22
  11.9 0.6 broadcast_in_dim.566
  12.5 8.6 %all-to-all-start = ((s32[32,1,128]{2,1,0:T(1,128)}), s32[32,1,128]{2,1,0:T(1,128)S(1)}, u32[]{:S(2)}, u32[]{:S(2)}) async-start(s32[32,1,128]{2,1,0:T(1,128)} %broadcast_in_dim.566), calls=%async_computation | async-start | bytes 32768 | tf_op jit(solution)/shard_map/all_to_all | solution.py:382
  22.6 4.0 %outgoing.1 = f32[32,256,128]{2,1,0:T(8,128)} custom-call(s32[32]{0:T(128)} %bitcast.77, f32[1024,128]{1,0:T(8,128)} %copy-done.9), custom_call_target="tpu_custom_call" | custom-call | tf_op jit(solution)/shard_map/outgoing/pallas_call | solution.py:359
  26.7 1.3 all-to-all-done
  28.1 6.2 %all-to-all-start.1 = ((f32[32,256,128]{2,1,0:T(8,128)}), f32[32,256,128]{2,1,0:T(8,128)}, u32[]{:S(2)}, u32[]{:S(2)}) async-start(f32[32,256,128]{2,1,0:T(8,128)} %outgoing.1), calls=%async_computation.1 | async-start | bytes 8388608 | tf_op jit(solution)/shard_map/all_to_all | solution.py:371
  35.2 0.6 select_reduce_fusion.4
  36.5 0.6 select_reduce_fusion.2
  37.4 0.8 copy-done.4
  38.3 0.7 fusion.29
  39.9 0.6 select_reduce_fusion.1
  40.5 0.6 select_reduce_fusion
  41.3 1.1 copy-done.5
  42.3 11.0 %near.1 = (f32[4,8,8,64,128]{4,3,2,1,0:T(8,128)S(1)}, bf16[4,8,128,128]{3,2,1,0:T(8,128)(2,1)S(1)}) custom-call(s32[48]{0:T(128)S(1)} %reshape.877.cols_ref, s32[3072]{0:T(1024)S(1)} %select_n.493.list_ref, s32[32]{0:T(128)S(1)} %convert_reduce_fusion.count_ref, f32[4,16,4096]{2,1,0:T(8,128)S(1)} %copy-done.2, f32[1032,128]{1,0:T(8,128)S(1)} %select_maximum_fusion.p0, ...), custom_call_target="tpu_custom_call" | custom-call | flops 10000000000 | bytes 16777216 | tf_op jit(solution)/shard_map/near/pallas_call | solution.py:260
  53.4 3.2 %copy-done.6 = f32[4,8,8,64,128]{4,3,2,1,0:T(8,128)} copy-done((f32[4,8,8,64,128]{4,3,2,1,0:T(8,128)}, f32[4,8,8,64,128]{4,3,2,1,0:T(8,128)S(1)}, u32[]{:S(2)}) %copy-start.6) | copy-done | bytes 8388632
  56.6 1.0 copy-done.7
  57.6 28.9 %all-to-all-done.1.f0.f1.f2.f3 = f32[32,256,128]{2,1,0:T(8,128)} async-done(((f32[32,256,128]{2,1,0:T(8,128)}), f32[32,256,128]{2,1,0:T(8,128)}, u32[]{:S(2)}, u32[]{:S(2)}) %all-to-all-start.1) | async-done | bytes 4194336 | tf_op jit(solution)/shard_map/all_to_all | solution.py:371
  86.5 1.2 copy-done.3
  87.8 1.2 copy-done.8
  89.0 15.4 %far.1 = (f32[8,512,128]{2,1,0:T(8,128)S(1)}, f32[8,512,128]{2,1,0:T(8,128)}, f32[8,512,128]{2,1,0:T(8,128)S(1)}, f32[8,512,128]{2,1,0:T(8,128)S(1)}, f32[1,512,128]{2,1,0:T(8,128)S(1)}) custom-call(s32[16]{0:T(128)S(1)} %reshape.871.cols_ref, s32[1024]{0:T(1024)S(1)} %select_n.472.list_ref, s32[32]{0:T(128)S(1)} %get-tuple-element.21.count_ref, ...), custom_call_target="tpu_custom_call" | custom-call | flops 10000000000 | bytes 25165824 | tf_op jit(solution)/shard_map/far/pallas_call | solution.py:289
  104.4 1.3 copy-done
  105.8 1.3 copy-done.1
  107.1 2.3 %collective-permute-start.3 = (f32[8,512,128]{2,1,0:T(8,128)}, f32[8,512,128]{2,1,0:T(8,128)}, u32[]{:S(2)}, u32[]{:S(2)}) collective-permute-start(f32[8,512,128]{2,1,0:T(8,128)} %get-tuple-element.15), channel_id=1, source_target_pairs={{0,8},{1,3},{2,10},{3,5},{4,12},{5,7},{6,14},{7,1},{8,16},{9,11},{... | collective-permute-start | bytes 6291464 | tf_op jit(solution)/shard_map/ppermute | solution.py:419
  109.8 1.4 collective-permute-start.4
  111.3 1.2 collective-permute-start.5
  112.6 0.5 slice.172
  114.3 19.5 %collective-permute-done.3 = f32[8,512,128]{2,1,0:T(8,128)} collective-permute-done((f32[8,512,128]{2,1,0:T(8,128)}, f32[8,512,128]{2,1,0:T(8,128)}, u32[]{:S(2)}, u32[]{:S(2)}) %collective-permute-start.3) | collective-permute-done | bytes 2097184 | tf_op jit(solution)/shard_map/ppermute | solution.py:419
  133.8 1.7 fusion.31
  135.4 21.4 %collective-permute-done.4 = f32[8,512,128]{2,1,0:T(8,128)S(1)} collective-permute-done((f32[8,512,128]{2,1,0:T(8,128)}, f32[8,512,128]{2,1,0:T(8,128)S(1)}, u32[]{:S(2)}, u32[]{:S(2)}) %collective-permute-start.4) | collective-permute-done | bytes 2097184 | tf_op jit(solution)/shard_map/ppermute | solution.py:419
  157.7 0.8 collective-permute-start.8
  158.8 0.9 collective-permute-start.7
  160.1 0.9 collective-permute-start.6
  161.6 10.1 %collective-permute-done.8 = f32[2,2,512,128]{3,2,1,0:T(8,128)S(1)} collective-permute-done((f32[2,2,512,128]{3,2,1,0:T(8,128)S(1)}, f32[2,2,512,128]{3,2,1,0:T(8,128)S(1)}, u32[]{:S(2)}, u32[]{:S(2)}) %collective-permute-start.8) | collective-permute-done | bytes 1048608 | tf_op jit(solution)/shard_map/ppermute | solution.py:437
  171.7 2.7 %collective-permute-done.7 = f32[2,2,512,128]{3,2,1,0:T(8,128)S(1)} collective-permute-done((f32[2,2,512,128]{3,2,1,0:T(8,128)S(1)}, f32[2,2,512,128]{3,2,1,0:T(8,128)S(1)}, u32[]{:S(2)}, u32[]{:S(2)}) %collective-permute-start.7) | collective-permute-done | bytes 1048608 | tf_op jit(solution)/shard_map/ppermute | solution.py:437
  174.4 11.2 %collective-permute-done.6 = f32[2,2,512,128]{3,2,1,0:T(8,128)S(1)} collective-permute-done((f32[2,2,512,128]{3,2,1,0:T(8,128)S(1)}, f32[2,2,512,128]{3,2,1,0:T(8,128)S(1)}, u32[]{:S(2)}, u32[]{:S(2)}) %collective-permute-start.6) | collective-permute-done | bytes 1048608 | tf_op jit(solution)/shard_map/ppermute | solution.py:437
  185.6 1.0 fusion.1
  186.6 3.9 %collective-permute-start.9 = (f32[2,512,128]{2,1,0:T(8,128)S(1)}, f32[2,512,128]{2,1,0:T(8,128)S(1)}, u32[]{:S(2)}, u32[]{:S(2)}) collective-permute-start(f32[2,512,128]{2,1,0:T(8,128)S(1)} %get-tuple-element.23), channel_id=1, source_target_pairs={{0,1},{1,0},{2,3},{3,2},{4,5},{5,4},{6,7},{7,6},{8,9},{9,8},{10,11... | collective-permute-start | bytes 1572872 | tf_op jit(solution)/shard_map/ppermute | solution.py:440
  190.5 1.5 collective-permute-done.9.got_ref
  192.1 0.8 copy-done.10
  192.9 2.3 %final.1 = f32[2,16,4096]{2,1,0:T(8,128)} custom-call(f32[2,512,128]{2,1,0:T(8,128)} %get-tuple-element.24.mine_ref, f32[2,512,128]{2,1,0:T(8,128)} %copy-done.10), custom_call_target="tpu_custom_call" | custom-call | tf_op jit(solution)/shard_map/final/pallas_call | solution.py:443
  (117 shorter events, 7.9 us)
Async XLA Ops:
  2.2 8.1 %copy-start.11 = (s32[4,8]{1,0:T(4,128)S(1)}, s32[4,8]{1,0:T(4,128)}, u32[]{:S(2)}) copy-start(s32[4,8]{1,0:T(4,128)} %param.13) | copy-start | bytes 388
  2.2 8.2 %copy-start.15 = (s32[2,16]{1,0:T(2,128)S(1)}, s32[2,16]{1,0:T(2,128)}, u32[]{:S(2)}) copy-start(s32[2,16]{1,0:T(2,128)} %param.17) | copy-start | bytes 388
  2.3 8.8 %copy-start.16 = (s32[1,64]{1,0:T(1,128)S(1)}, s32[1,64]{1,0:T(1,128)}, u32[]{:S(2)}) copy-start(s32[1,64]{1,0:T(1,128)} %param.16) | copy-start | bytes 772
  2.3 9.6 %copy-start.13 = (s32[1,32]{1,0:T(1,128)S(1)}, s32[1,32]{1,0:T(1,128)}, u32[]{:S(2)}) copy-start(s32[1,32]{1,0:T(1,128)} %param.15) | copy-start | bytes 388
  3.1 18.4 %copy-start.14 = (s32[4,8]{1,0:T(4,128)S(1)}, s32[4,8]{1,0:T(4,128)}, u32[]{:S(2)}) copy-start(s32[4,8]{1,0:T(4,128)} %param.14) | copy-start | bytes 388
  3.1 18.7 %copy-start.17 = (s32[4]{0:T(128)S(1)}, s32[4]{0:T(128)}, u32[]{:S(2)}) copy-start(s32[4]{0:T(128)} %param.11) | copy-start | bytes 52
  3.1 19.0 %copy-start.12 = (s32[4,16]{1,0:T(4,128)S(1)}, s32[4,16]{1,0:T(4,128)}, u32[]{:S(2)}) copy-start(s32[4,16]{1,0:T(4,128)} %param.10) | copy-start | bytes 772
  3.7 18.9 %copy-start.9 = (f32[1024,128]{1,0:T(8,128)}, f32[1024,128]{1,0:T(8,128)S(1)}, u32[]{:S(2)}) copy-start(f32[1024,128]{1,0:T(8,128)S(1)} %reshape_reshape.7.p_ref) | copy-start | bytes 1572868
  3.8 33.5 %collective-permute-start.2 = (f32[1032,128]{1,0:T(8,128)S(1)}, f32[1032,128]{1,0:T(8,128)S(1)}, u32[]{:S(2)}, u32[]{:S(2)}) collective-permute-start(f32[1032,128]{1,0:T(8,128)S(1)} %select_maximum_fusion.p0), channel_id=1, source_target_pairs={{96,0},{0,32},{32,64},{64,96},{97,1},{1,33},{33,65},{65,97},{98,2}... | collective-permute-start | bytes 1585160 | tf_op jit(solution)/shard_map/ppermute | solution.py:377
  6.3 31.1 %collective-permute-start.1 = (f32[1032,128]{1,0:T(8,128)S(1)}, f32[1032,128]{1,0:T(8,128)S(1)}, u32[]{:S(2)}, u32[]{:S(2)}) collective-permute-start(f32[1032,128]{1,0:T(8,128)S(1)} %select_maximum_fusion.p0), channel_id=1, source_target_pairs={{64,0},{96,32},{0,64},{32,96},{65,1},{97,33},{1,65},{33,97},{66,2}... | collective-permute-start | bytes 1585160 | tf_op jit(solution)/shard_map/ppermute | solution.py:377
  9.6 28.7 %collective-permute-start = (f32[1032,128]{1,0:T(8,128)S(1)}, f32[1032,128]{1,0:T(8,128)}, u32[]{:S(2)}, u32[]{:S(2)}) collective-permute-start(f32[1032,128]{1,0:T(8,128)S(1)} %select_maximum_fusion.p0), channel_id=1, source_target_pairs={{32,0},{64,32},{96,64},{0,96},{33,1},{65,33},{97,65},{1,97},{34,2}... | collective-permute-start | bytes 1585160 | tf_op jit(solution)/shard_map/ppermute | solution.py:377
  12.5 15.5 %all-to-all-start = ((s32[32,1,128]{2,1,0:T(1,128)}), s32[32,1,128]{2,1,0:T(1,128)S(1)}, u32[]{:S(2)}, u32[]{:S(2)}) async-start(s32[32,1,128]{2,1,0:T(1,128)} %broadcast_in_dim.566), calls=%async_computation | async-start | bytes 32768 | tf_op jit(solution)/shard_map/all_to_all | solution.py:382
  26.7 14.5 %copy-start.2 = (f32[4,16,4096]{2,1,0:T(8,128)S(1)}, f32[4,16,4096]{2,1,0:T(8,128)}, u32[]{:S(2)}) copy-start(f32[4,16,4096]{2,1,0:T(8,128)} %a_ref.3) | copy-start | bytes 3145732
  28.1 58.5 %all-to-all-start.1 = ((f32[32,256,128]{2,1,0:T(8,128)}), f32[32,256,128]{2,1,0:T(8,128)}, u32[]{:S(2)}, u32[]{:S(2)}) async-start(f32[32,256,128]{2,1,0:T(8,128)} %outgoing.1), calls=%async_computation.1 | async-start | bytes 8388608 | tf_op jit(solution)/shard_map/all_to_all | solution.py:371
  37.4 0.8 copy-start.4
  41.3 1.1 copy-start.5
  53.4 3.2 %copy-start.6 = (f32[4,8,8,64,128]{4,3,2,1,0:T(8,128)}, f32[4,8,8,64,128]{4,3,2,1,0:T(8,128)S(1)}, u32[]{:S(2)}) copy-start(f32[4,8,8,64,128]{4,3,2,1,0:T(8,128)S(1)} %get-tuple-element.12.m_ref) | copy-start | bytes 25165828
  56.6 1.0 copy-start.7
  86.5 1.2 copy-start.3
  87.8 1.2 copy-start.8
  104.4 1.4 copy-start
  105.8 1.3 copy-start.1
  107.1 26.7 %collective-permute-start.3 = (f32[8,512,128]{2,1,0:T(8,128)}, f32[8,512,128]{2,1,0:T(8,128)}, u32[]{:S(2)}, u32[]{:S(2)}) collective-permute-start(f32[8,512,128]{2,1,0:T(8,128)} %get-tuple-element.15), channel_id=1, source_target_pairs={{0,8},{1,3},{2,10},{3,5},{4,12},{5,7},{6,14},{7,1},{8,16},{9,11},{... | collective-permute-start | bytes 6291464 | tf_op jit(solution)/shard_map/ppermute | solution.py:419
  109.8 47.1 %collective-permute-start.4 = (f32[8,512,128]{2,1,0:T(8,128)}, f32[8,512,128]{2,1,0:T(8,128)S(1)}, u32[]{:S(2)}, u32[]{:S(2)}) collective-permute-start(f32[8,512,128]{2,1,0:T(8,128)} %copy-done.1), channel_id=1, source_target_pairs={{0,16},{1,5},{2,18},{3,7},{4,20},{5,1},{6,22},{7,3},{8,24},{9,13},... | collective-permute-start | bytes 6291464 | tf_op jit(solution)/shard_map/ppermute | solution.py:419
  111.3 45.9 %collective-permute-start.5 = (f32[8,512,128]{2,1,0:T(8,128)}, f32[8,512,128]{2,1,0:T(8,128)S(1)}, u32[]{:S(2)}, u32[]{:S(2)}) collective-permute-start(f32[8,512,128]{2,1,0:T(8,128)} %copy-done), channel_id=1, source_target_pairs={{0,24},{1,7},{2,26},{3,1},{4,28},{5,3},{6,30},{7,5},{8,0},{9,15},{... | collective-permute-start | bytes 6291464 | tf_op jit(solution)/shard_map/ppermute | solution.py:419
  157.7 14.0 %collective-permute-start.8 = (f32[2,2,512,128]{3,2,1,0:T(8,128)S(1)}, f32[2,2,512,128]{3,2,1,0:T(8,128)S(1)}, u32[]{:S(2)}, u32[]{:S(2)}) collective-permute-start(f32[2,2,512,128]{3,2,1,0:T(8,128)S(1)} %select_add_fusion), channel_id=1, source_target_pairs={{0,6},{1,25},{2,0},{3,27},{4,2},{5,29},{6,4},{7,31},{8,14},{9,1},{... | collective-permute-start | bytes 3145736 | tf_op jit(solution)/shard_map/ppermute | solution.py:437
  158.8 15.6 %collective-permute-start.7 = (f32[2,2,512,128]{3,2,1,0:T(8,128)S(1)}, f32[2,2,512,128]{3,2,1,0:T(8,128)S(1)}, u32[]{:S(2)}, u32[]{:S(2)}) collective-permute-start(f32[2,2,512,128]{3,2,1,0:T(8,128)S(1)} %select_add_fusion.1), channel_id=1, source_target_pairs={{0,4},{1,17},{2,6},{3,19},{4,0},{5,21},{6,2},{7,23},{8,12},{9,25},... | collective-permute-start | bytes 3145736 | tf_op jit(solution)/shard_map/ppermute | solution.py:437
  160.1 25.5 %collective-permute-start.6 = (f32[2,2,512,128]{3,2,1,0:T(8,128)S(1)}, f32[2,2,512,128]{3,2,1,0:T(8,128)S(1)}, u32[]{:S(2)}, u32[]{:S(2)}) collective-permute-start(f32[2,2,512,128]{3,2,1,0:T(8,128)S(1)} %select_add_fusion.2), channel_id=1, source_target_pairs={{0,2},{1,9},{2,4},{3,11},{4,6},{5,13},{6,0},{7,15},{8,10},{9,17},{... | collective-permute-start | bytes 3145736 | tf_op jit(solution)/shard_map/ppermute | solution.py:437
  186.6 5.5 %collective-permute-start.9 = (f32[2,512,128]{2,1,0:T(8,128)S(1)}, f32[2,512,128]{2,1,0:T(8,128)S(1)}, u32[]{:S(2)}, u32[]{:S(2)}) collective-permute-start(f32[2,512,128]{2,1,0:T(8,128)S(1)} %get-tuple-element.23), channel_id=1, source_target_pairs={{0,1},{1,0},{2,3},{3,2},{4,5},{5,4},{6,7},{7,6},{8,9},{9,8},{10,11... | collective-permute-start | bytes 1572872 | tf_op jit(solution)/shard_map/ppermute | solution.py:440
  192.1 0.8 copy-start.10
where the time goes:
time: 196 us; the launch traced here: 195 us
  waiting for transfers between devices  96.9 us (49%)
  starting transfers between devices  33 us (17%)
  Pallas kernels  32.7 us (17%)
  local copies, waits for them, and re-layouts  20.7 us (11%)
  other arithmetic  10.5 us (5%)
    ppermute x3, waiting for transfers between devices, per_device(): lax.ppermute(chunks[t], 'dom', shift_pairs(t, 0))  41.1 us
    all_to_all x1, waiting for transfers between devices, per_device(): lax.all_to_all(outgoing, 'dom', split_axis=0, concat_axis=0, tiled=True)  28.9 us
    ppermute x3, waiting for transfers between devices, per_device(): lax.ppermute(owned(t2), 'dom', shift_pairs(t2, 1))  23.9 us
    pallas_call x1, Pallas kernels, far_call(): pl.pallas_call(far_kernel, out_shape=tuple((jax.ShapeDtypeStruct((n,) + s...  15.4 us
    unnamed x37, local copies, waits for them, and re-layouts  12.5 us
    pallas_call x1, Pallas kernels, near_call(): pl.pallas_call(near_kernel, out_shape=(jax.ShapeDtypeStruct((RB, KP, KC /...  11 us
    all_to_all x1, starting transfers between devices, per_device(): lax.all_to_all(jnp.broadcast_to(mine[None], (n_dom, mine.shape[0])), 'dom...  8.6 us
    ppermute x3, starting transfers between devices, per_device(): lax.ppermute(carried, 'grp', [((z + k) % n_grp, z) for z in range(n_grp)])  6.57 us
  transfers between devices with their start and end apart: 12, of which 9 were waited for; matrix products, arithmetic and copies ran while one was open for 7% of the time, Pallas kernels for 8%

commit v1 on v0

--- a/solution.py
+++ b/solution.py
@@ -13,6 +13,10 @@
 KA = 16
 KP = 8
 KC = 16
+HALVES = 2
+OUT_SPACE = pl.ANY
+FAR_VMEM = 24
+HALF_C = KC // HALVES
 RB = 4
 PAIRS = RB * KP
 NEAR_E = KG * KP
@@ -172,7 +176,7 @@
         outs = []
         for t in range(2):
             j = jj * 2 + t
-            for s in range(KC // 2):
+            for s in range(HALF_C // 2):
                 hi, lo = split(m_ref[0, j, s])
                 cols = slice(s * LANES, (s + 1) * LANES)
                 wide_ref[t, 0:64, cols] = hi
@@ -180,7 +184,7 @@
             outs.append(jnp.dot(left_ref[0, j], wide_ref[t], preferred_element_type=jnp.float32))
         for t in range(2):
             pos = pos_ref[i * KP + jj * 2 + t]
-            for s in range(KC // 2):
+            for s in range(HALF_C // 2):
                 cols = slice(s * LANES, (s + 1) * LANES)
                 acc_ref[pos, s * BS : (s + 1) * BS, :] += outs[t][0:BS, cols] + outs[t][BS : 2 * BS, cols]
         return carry
@@ -199,11 +203,13 @@
             copy.wait()
 
 
-def final_kernel(mine_ref, got_ref, out_ref, spread_ref):
+def final_kernel(*refs):
+    *parts, out_ref, spread_ref = refs
     half = BS // 2
     first = first_half((half, LANES))
     for s in range(KC // 2):
-        even, odd = (pl.ds(s * BS + o, half, stride=2) for o in range(2))
+        mine_ref, got_ref = parts[2 * (s // (HALF_C // 2)) : 2 * (s // (HALF_C // 2)) + 2]
+        even, odd = (pl.ds(s % (HALF_C // 2) * BS + o, half, stride=2) for o in range(2))
         even = mine_ref[0, even, :] + got_ref[0, even, :]
         odd = mine_ref[0, odd, :] + got_ref[0, odd, :]
         spread_ref[2 * s * half : (2 * s + 1) * half, :] = jnp.where(first, even, pltpu.roll(odd, BS, axis=1))
@@ -237,7 +243,7 @@
 def match_lists(wanted, ids, live):
     n = ids.shape[1]
     eq = wanted[:, :, None] == ids[:, None, :]
-    c_of = jnp.sum(jnp.where(eq, jnp.arange(KC, dtype=jnp.int32)[None, :, None], 0), axis=1)
+    c_of = jnp.sum(jnp.where(eq, jnp.arange(wanted.shape[1], dtype=jnp.int32)[None, :, None], 0), axis=1)
     hit = jnp.any(eq, axis=1) & live
     number = jnp.arange(n, dtype=jnp.int32)
     before = jnp.sum(jnp.where((number[:, None] < number[None, :])[None], hit[:, :, None].astype(jnp.int32), 0), axis=1)
@@ -283,9 +289,10 @@
     )(cols, lists, counts, operator_blocks, *near_rows)
 
 
-def far_call(cols, lists, counts, position, operator_blocks, far_rows, matched, left, n_dom):
+def far_call(half, cols, lists, counts, position, operator_blocks, far_rows, matched, left, n_dom):
     far_spec = lambda m: pl.BlockSpec((1, ROW_T, LANES), lambda i, cols, *_: (cols[i * KH + m], 0, 0))
-    slot_shape = (KC // 2 * BS, LANES)
+    slot_shape = (HALF_C // 2 * BS, LANES)
+    hbm = lambda x: pltpu.with_memory_space_constraint(x, pltpu.HBM)
     return pl.pallas_call(
         far_kernel,
         out_shape=tuple(jax.ShapeDtypeStruct((n,) + slot_shape, jnp.float32) for n in (8, 8, 8, 8, 1)),
@@ -295,23 +302,23 @@
             in_specs=[pl.BlockSpec((1, 8, BS * BS), lambda i, *_: (i, 1, 0))]
             + [far_spec(m) for m in range(KH)]
             + [
-                pl.BlockSpec((1, KP, KC // 2, BS, LANES), lambda i, *_: (i, 0, 0, 0, 0)),
+                pl.BlockSpec((1, KP, HALF_C // 2, BS, LANES), lambda i, *_: (i, 0, half, 0, 0)),
                 pl.BlockSpec((1, KP, LANES, LANES), lambda i, *_: (i, 0, 0, 0)),
             ],
-            out_specs=(pl.BlockSpec(memory_space=pltpu.HBM),) * 5,
+            out_specs=(pl.BlockSpec(memory_space=OUT_SPACE),) * 5,
             scratch_shapes=[
                 pltpu.VMEM((KH, 256, KP * BS), jnp.bfloat16),
                 pltpu.VMEM((2, FAR_E // 2 + 1, BS, LANES), jnp.float32),
-                pltpu.VMEM((2, LANES, KC * BS), jnp.bfloat16),
+                pltpu.VMEM((2, LANES, HALF_C * BS), jnp.bfloat16),
                 pltpu.VMEM((n_dom + 1,) + slot_shape, jnp.float32),
                 pltpu.VMEM((8 * BS // 2, LANES), jnp.float32),
                 pltpu.SemaphoreType.DMA((5,)),
             ],
         ),
-        compiler_params=pltpu.CompilerParams(vmem_limit_bytes=40 * 2**20),
-        cost_estimate=pl.CostEstimate(flops=10**10, bytes_accessed=24 * 2**20, transcendentals=0),
+        compiler_params=pltpu.CompilerParams(vmem_limit_bytes=FAR_VMEM * 2**20),
+        cost_estimate=pl.CostEstimate(flops=5 * 10**9, bytes_accessed=12 * 2**20, transcendentals=0),
         name="far",
-    )(cols, lists, counts, position, operator_blocks, *([far_rows] * KH), matched, left)
+    )(cols, lists, counts, position, operator_blocks, *([far_rows] * KH), hbm(matched), hbm(left))
 
 
 SIDE = 4
@@ -325,6 +332,15 @@
 def device_at(u, v, k, me):
     u, v, k = u % SIDE, v % SIDE, k % 2
     return (jnp.where(me % 2 == 0, u, v) * SIDE + jnp.where(me % 2 == 0, v, u)) * 2 + k
+
+
+def plane_pairs(dx, dy, dk):
+    return [
+        ((((x + dx) % SIDE) * SIDE + (y + dy) % SIDE) * 2 + (k + dk) % 2, (x * SIDE + y) * 2 + k)
+        for x in range(SIDE)
+        for y in range(SIDE)
+        for k in range(2)
+    ]
 
 
 def shift_pairs(shift, phase):
@@ -368,6 +384,7 @@
         ),
         name="outgoing",
     )(send_lists.reshape(-1), panels)
+    outgoing, prolong_cols, panels = lax.optimization_barrier((outgoing, prolong_cols, panels))
     far_rows = lax.all_to_all(outgoing, "dom", split_axis=0, concat_axis=0, tiled=True)
 
     id_tile = jnp.pad(prolong_cols.reshape(1, PAIRS).astype(jnp.float32), ((0, 7), (0, LANES - PAIRS)))
@@ -379,9 +396,16 @@
     mine = jnp.concatenate(
         [prolong_cols.reshape(-1), coarse_pattern.reshape(-1), send_lists.reshape(-1), owner.reshape(n_dom, 2)[:, 0]]
     )
-    told = lax.all_to_all(
-        jnp.broadcast_to(mine[None], (n_dom, mine.shape[0])), "dom", split_axis=0, concat_axis=0, tiled=True
-    )
+    told = mine[None]
+    told = jnp.concatenate([told, lax.ppermute(told, "dom", plane_pairs(0, 0, 1))], axis=0)
+    told = jnp.concatenate([told] + [lax.ppermute(told, "dom", plane_pairs(0, n, 0)) for n in range(1, SIDE)], axis=0)
+    told = jnp.concatenate([told] + [lax.ppermute(told, "dom", plane_pairs(n, 0, 0)) for n in range(1, SIDE)], axis=0)
+
+    def relative(device):
+        dx = device // (2 * SIDE) - d // (2 * SIDE)
+        dy = device // 2 % SIDE - d // 2 % SIDE
+        return ((dx % SIDE) * SIDE + dy % SIDE) * 2 + (device - d) % 2
+
     all_cols = told[:, :PAIRS].reshape(n_dom, RB, KP)
     patterns = told[:, PAIRS : 2 * PAIRS].reshape(2 * n_dom, KC)
     here = jnp.arange(n_dom, dtype=jnp.int32)[None, :] == d
@@ -393,7 +417,7 @@
 
     slots = prolong_slot.reshape(-1)
     slot_row = pick_rows(owner[:, None], slots)[:, 0]
-    wanted = pick_rows(patterns, (slots // 2) * 2 + slot_row)
+    wanted = pick_rows(patterns, relative(slots // 2) * 2 + slot_row)
     u, v, k = places(d, d)
     to_u, to_v, to_k = places(slots // 2, d)
     position = ((to_u - u) % SIDE) * 8 + ((to_v - v) % SIDE) * 2 + (to_k - k) % 2
@@ -406,49 +430,74 @@
     near_cols = (((near_slots // RB) - g) % n_grp * RB + near_slots % RB).reshape(-1)
     far_cols = operator_cols[:, KG:].reshape(-1)
     near_ids = pick_rows(near_ids_table, near_cols).reshape(RB, NEAR_E)
-    far_ids = pick_rows(far_ids, far_cols).reshape(RB, FAR_E)
+    far_ids = pick_rows(far_ids, relative(far_cols)).reshape(RB, FAR_E)
     live = jnp.arange(KH, dtype=jnp.int32)[None, :] < halo_count[:, None]
     spread = lambda x: jnp.repeat(x, KP, axis=0)
     near_list, near_count = match_lists(wanted, spread(near_ids), jnp.ones((PAIRS, NEAR_E), bool))
-    far_list, far_count = match_lists(wanted, spread(far_ids), spread(jnp.repeat(live, KP, axis=1)))
+    far_live = spread(jnp.repeat(live, KP, axis=1))
 
     matched, left = near_call(near_cols, near_list, near_count, operator_blocks, near_rows)
-    chunks = far_call(far_cols, far_list, far_count, position, operator_blocks, far_rows, matched, left, n_dom)
-    slot_shape = (KC // 2 * BS, LANES)
-
-    arriving = [chunks[0]] + [lax.ppermute(chunks[t], "dom", shift_pairs(t, 0)) for t in range(1, SIDE)]
+    slot_shape = (HALF_C // 2 * BS, LANES)
     sources = jnp.stack([device_at(u - t, v, k, d) for t in range(SIDE)])
     owners = jnp.stack([device_at(u, v + p // 2, k + p % 2, d) for p in range(8)])
-    rows_from = pick_rows(first_rows, sources)
+    rows_from = pick_rows(first_rows, relative(sources))
     row_of = pick_rows(rows_from.T, owners).T
-    own_first = row_of[0, 0]
-
-    def owned(t2):
-        total = 0.0
-        for t in range(SIDE):
-            part = arriving[t][2 * t2 : 2 * t2 + 2][:, None]
-            to_row = row_of[t, 2 * t2 : 2 * t2 + 2][:, None] == jnp.arange(2, dtype=jnp.int32)
-            total = total + jnp.where(to_row[:, :, None, None], part, 0.0)
-        if t2 == 0:
-            to_row = (jnp.arange(2, dtype=jnp.int32) == 1 - own_first)[None] & (jnp.arange(2) == 0)[:, None]
-            total = total + jnp.where(to_row[:, :, None, None], chunks[4][:, None], 0.0)
-        return total
-
-    sent = {t2: lax.ppermute(owned(t2), "dom", shift_pairs(t2, 1)) for t2 in (2, 1, 3)}
-    kept = owned(0)
-    sums = [kept[kk] + sent[1][kk] + sent[2][kk] + sent[3][kk] for kk in (1, 0)]
-    swapped = lax.ppermute(sums[0], "dom", [(n, n ^ 1) for n in range(n_dom)])
+    two = jnp.arange(2, dtype=jnp.int32)
+    second_row = (two == 1 - row_of[0, 0])[None] & (two == 0)[:, None]
+
+    def first_phase(half, before):
+        far_list, far_count = match_lists(
+            wanted[:, half * HALF_C : (half + 1) * HALF_C], spread(far_ids), far_live
+        )
+        chunks = far_call(
+            half, far_cols, far_list, far_count, position, operator_blocks, far_rows, matched, left, n_dom
+        )
+        far_two = lax.ppermute(chunks[2], "dom", shift_pairs(2, 0))
+        one, three, before = lax.optimization_barrier((chunks[1], chunks[3], before))
+        sent = [lax.ppermute(chunk, "dom", shift_pairs(t, 0)) for t, chunk in ((1, one), (3, three))]
+        return [chunks[0], sent[0], far_two, sent[1]], chunks[4], before
+
+    def second_phase(arriving, second):
+        def owned(t2):
+            total = 0.0
+            for t in range(SIDE):
+                part = arriving[t][2 * t2 : 2 * t2 + 2][:, None]
+                to_row = row_of[t, 2 * t2 : 2 * t2 + 2][:, None] == two
+                total = total + jnp.where(to_row[:, :, None, None], part, 0.0)
+            if t2 == 0:
+                total = total + jnp.where(second_row[:, :, None, None], second[:, None], 0.0)
+            return total
+
+        sent = [lax.ppermute(owned(t2), "dom", shift_pairs(t2, 1)) for t2 in (2, 1, 3)]
+        return owned(0), sent
+
+    def swap(kept, sent):
+        sums = [kept[kk] + sent[1][kk] + sent[0][kk] + sent[2][kk] for kk in (1, 0)]
+        return sums[1], lax.ppermute(sums[0], "dom", [(n, n ^ 1) for n in range(n_dom)])
+
+    arrived = []
+    for half in range(HALVES):
+        here, second, before = first_phase(half, arrived[-1][0] if arrived else [])
+        if arrived:
+            arrived[-1] = (before, arrived[-1][1])
+        arrived.append((here, second))
+    halves = []
+    for here, second in arrived:
+        if halves:
+            here, _ = lax.optimization_barrier((here, halves[-1][1]))
+        halves.append(second_phase(here, second))
+    parts = [swap(*half) for half in halves]
 
     row_spec = pl.BlockSpec((1,) + slot_shape, lambda i: (i, 0, 0))
     return pl.pallas_call(
         final_kernel,
         out_shape=jax.ShapeDtypeStruct((2, KC, BS * BS), jnp.float32),
         grid=(2,),
-        in_specs=[row_spec, row_spec],
+        in_specs=[row_spec] * (2 * HALVES),
         out_specs=pl.BlockSpec((1, KC, BS * BS), lambda i: (i, 0, 0)),
         scratch_shapes=[pltpu.VMEM((KC * BS // 2, LANES), jnp.float32)],
         name="final",
-    )(sums[1], swapped)
+    )(*[x for pair in parts for x in pair])
 
 
 def solution(mesh):

time: 196 us -> 210 us (1.071)
  starting transfers between devices: 33 us -> 46.3 us
  Pallas kernels: 32.7 us -> 38.9 us
  local copies, waits for them, and re-layouts: 20.7 us -> 15.1 us
    all_to_all x1, waiting for transfers between devices: 28.9 us -> 0.01 us  [per_device(): lax.all_to_all(outgoing, 'dom', split_axis=0, concat_axis=0, tiled=True)]
    ppermute x7 -> x21, waiting for transfers between devices: 66.6 us -> 91.5 us  [the longest x3 39.8 us: per_device(): lax.ppermute(told, 'dom', plane_pairs(0, n, 0))]
    ppermute x7 -> x21, starting transfers between devices: 11.6 us -> 31.1 us  [the longest x6 6.35 us: second_phase(): lax.ppermute(owned(t2), 'dom', shift_pairs(t2, 1))]
    all_to_all x1 -> x0, starting transfers between devices: 8.6 us -> none  [per_device(): lax.all_to_all(jnp.broadcast_to(mine[None], (n_dom, mine.shape[0])), 'dom...]
    unnamed x37 -> x27, local copies, waits for them, and re-layouts: 12.5 us -> 5.48 us
    pallas_call x1 -> x2, Pallas kernels: 15.4 us -> 22.1 us  [far_call(): pl.pallas_call(far_kernel, out_shape=tuple((jax.ShapeDtypeStruct((n,) + s...]
    ppermute x3, waiting for transfers between devices: 0.01 us -> 5.66 us  [per_device(): lax.ppermute(carried, 'grp', [((z + k) % n_grp, z) for z in range(n_grp)])]
    all_to_all x1, starting transfers between devices: 6.24 us -> 8.37 us  [per_device(): lax.all_to_all(outgoing, 'dom', split_axis=0, concat_axis=0, tiled=True)]
  transfers between devices with their start and end apart: 12 -> 25, of which waited for: 9 -> 12; matrix products, arithmetic and copies ran while one was open for 7% -> 8% of each run, Pallas kernels for 8% -> 10%
where the time goes in v1:
time: 210 us
  waiting for transfers between devices  97.2 us (46%)
  starting transfers between devices  46.3 us (22%)
  Pallas kernels  38.9 us (19%)
  local copies, waits for them, and re-layouts  15.1 us (7%)
  other arithmetic  11.1 us (5%)
    ppermute x3, waiting for transfers between devices, per_device(): lax.ppermute(told, 'dom', plane_pairs(0, n, 0))  39.8 us
    ppermute x6, waiting for transfers between devices, second_phase(): lax.ppermute(owned(t2), 'dom', shift_pairs(t2, 1))  30.4 us
    pallas_call x2, Pallas kernels, far_call(): pl.pallas_call(far_kernel, out_shape=tuple((jax.ShapeDtypeStruct((n,) + s...  22.1 us
    ppermute x4, waiting for transfers between devices, first_phase(): lax.ppermute(chunk, 'dom', shift_pairs(t, 0))  19 us
    pallas_call x1, Pallas kernels, near_call(): pl.pallas_call(near_kernel, out_shape=(jax.ShapeDtypeStruct((RB, KP, KC /...  10.3 us
    all_to_all x1, starting transfers between devices, per_device(): lax.all_to_all(outgoing, 'dom', split_axis=0, concat_axis=0, tiled=True)  8.37 us
    ppermute x3, starting transfers between devices, per_device(): lax.ppermute(carried, 'grp', [((z + k) % n_grp, z) for z in range(n_grp)])  6.76 us
    ppermute x6, starting transfers between devices, second_phase(): lax.ppermute(owned(t2), 'dom', shift_pairs(t2, 1))  6.35 us
  transfers between devices with their start and end apart: 25, of which 12 were waited for; matrix products, arithmetic and copies ran while one was open for 8% of the time, Pallas kernels for 10%

profile of v1, /device:TPU:1, one launch (start us, length us, event | category | flops | bytes accessed | tf_op | source)
XLA Modules:
  0.0 209.8 jit_solution(270405114577873250)
XLA Ops:
  0.0 1.5 reshape.1305
  1.5 0.8 copy.21
  2.3 1.4 reshape_reshape.6.p_ref
  3.7 4.1 %outgoing.1 = f32[32,256,128]{2,1,0:T(8,128)} custom-call(s32[32]{0:T(128)} %bitcast.82, f32[1024,128]{1,0:T(8,128)} %reshape_reshape.6.p_ref), custom_call_target="tpu_custom_call" | custom-call | tf_op jit(solution)/shard_map/outgoing/pallas_call | solution.py:375
  8.0 2.5 %collective-permute-start.9 = (f32[1032,128]{1,0:T(8,128)S(1)}, f32[1032,128]{1,0:T(8,128)S(1)}, u32[]{:S(2)}, u32[]{:S(2)}) collective-permute-start(f32[1032,128]{1,0:T(8,128)S(1)} %select_maximum_fusion.p0), channel_id=1, source_target_pairs={{96,0},{0,32},{32,64},{64,96},{97,1},{1,33},{33,65},{65,97},{98,2}... | collective-permute-start | bytes 1585160 | tf_op jit(solution)/shard_map/ppermute | solution.py:394
  10.5 3.3 %collective-permute-start.8 = (f32[1032,128]{1,0:T(8,128)S(1)}, f32[1032,128]{1,0:T(8,128)S(1)}, u32[]{:S(2)}, u32[]{:S(2)}) collective-permute-start(f32[1032,128]{1,0:T(8,128)S(1)} %select_maximum_fusion.p0), channel_id=1, source_target_pairs={{64,0},{96,32},{0,64},{32,96},{65,1},{97,33},{1,65},{33,97},{66,2}... | collective-permute-start | bytes 1585160 | tf_op jit(solution)/shard_map/ppermute | solution.py:394
  13.8 8.4 %all-to-all-start = ((f32[32,256,128]{2,1,0:T(8,128)}), f32[32,256,128]{2,1,0:T(8,128)}, u32[]{:S(2)}, u32[]{:S(2)}) async-start(f32[32,256,128]{2,1,0:T(8,128)} %outgoing.1), calls=%async_computation | async-start | bytes 8388608 | tf_op jit(solution)/shard_map/all_to_all | solution.py:388
  22.9 0.7 reduce.26
  25.5 1.5 collective-permute-start.3
  27.0 2.4 %collective-permute-start.2 = (s32[2,128]{1,0:T(2,128)S(1)}, s32[2,128]{1,0:T(2,128)S(1)}, u32[]{:S(2)}, u32[]{:S(2)}) collective-permute-start(s32[2,128]{1,0:T(2,128)S(1)} %pad_add_fusion.1), channel_id=1, source_target_pairs={{4,0},{5,1},{6,2},{7,3},{0,4},{1,5},{2,6},{3,7},{12,8},{13,9},{14,... | collective-permute-start | bytes 3080 | tf_op jit(solution)/shard_map/ppermute | solution.py:401
  29.4 1.2 collective-permute-start.1
  30.6 37.8 %collective-permute-done.3 = s32[2,128]{1,0:T(2,128)S(1)} collective-permute-done((s32[2,128]{1,0:T(2,128)S(1)}, s32[2,128]{1,0:T(2,128)S(1)}, u32[]{:S(2)}, u32[]{:S(2)}) %collective-permute-start.3) | collective-permute-done | bytes 1056 | tf_op jit(solution)/shard_map/ppermute | solution.py:401
  68.4 2.0 collective-permute-done.1
  70.4 2.8 %collective-permute-start.6 = (s32[8,128]{1,0:T(8,128)S(1)}, s32[8,128]{1,0:T(8,128)S(1)}, u32[]{:S(2)}, u32[]{:S(2)}) collective-permute-start(s32[8,128]{1,0:T(8,128)S(1)} %concatenate.38), channel_id=1, source_target_pairs={{24,0},{25,1},{26,2},{27,3},{28,4},{29,5},{30,6},{31,7},{0,8},{1,9... | collective-permute-start | bytes 12296 | tf_op jit(solution)/shard_map/ppermute | solution.py:402
  73.2 2.2 %collective-permute-start.5 = (s32[8,128]{1,0:T(8,128)S(1)}, s32[8,128]{1,0:T(8,128)S(1)}, u32[]{:S(2)}, u32[]{:S(2)}) collective-permute-start(s32[8,128]{1,0:T(8,128)S(1)} %concatenate.38), channel_id=1, source_target_pairs={{16,0},{17,1},{18,2},{19,3},{20,4},{21,5},{22,6},{23,7},{24,8},{25... | collective-permute-start | bytes 12296 | tf_op jit(solution)/shard_map/ppermute | solution.py:402
  76.0 0.9 collective-permute-start.7
  77.1 1.0 collective-permute-done.4
  79.0 0.6 select_reduce_fusion.6
  80.9 0.6 select_reduce_fusion.2
  81.9 0.6 select_reduce_fusion.4
  82.8 5.7 %collective-permute-done.7.p1 = f32[1032,128]{1,0:T(8,128)S(1)} collective-permute-done((f32[1032,128]{1,0:T(8,128)S(1)}, f32[1032,128]{1,0:T(8,128)S(1)}, u32[]{:S(2)}, u32[]{:S(2)}) %collective-permute-start.7) | collective-permute-done | bytes 528416 | tf_op jit(solution)/shard_map/ppermute | solution.py:394
  89.9 0.6 select_reduce_fusion
  90.7 10.3 %near.1 = (f32[4,8,8,64,128]{4,3,2,1,0:T(8,128)S(1)}, bf16[4,8,128,128]{3,2,1,0:T(8,128)(2,1)S(1)}) custom-call(s32[48]{0:T(128)S(1)} %reshape.1313.cols_ref, s32[3072]{0:T(1024)S(1)} %select_n.727.list_ref, s32[32]{0:T(128)S(1)} %convert_reduce_fusion.1.count_ref, f32[4,16,4096]{2,1,0:T(8,128)S(1)} %copy-done.1, f32[1032,128]{1,0:T(8,128)S(1)} %select_maximum_fusion.p0, ...), custom_call_target="tpu_custom_call" | custom-call | flops 10000000000 | bytes 16777216 | tf_op jit(solution)/shard_map/near/pallas_call | solution.py:266
  101.1 3.2 %copy-done = f32[4,8,8,64,128]{4,3,2,1,0:T(8,128)} copy-done((f32[4,8,8,64,128]{4,3,2,1,0:T(8,128)}, f32[4,8,8,64,128]{4,3,2,1,0:T(8,128)S(1)}, u32[]{:S(2)}) %copy-start) | copy-done | bytes 8388632
  104.3 1.0 copy-done.2
  105.3 11.6 %far.3 = (f32[8,256,128]{2,1,0:T(8,128)S(1)}, f32[8,256,128]{2,1,0:T(8,128)}, f32[8,256,128]{2,1,0:T(8,128)S(1)}, f32[8,256,128]{2,1,0:T(8,128)}, f32[1,256,128]{2,1,0:T(8,128)S(1)}) custom-call(s32[16]{0:T(128)S(1)} %reshape.1308.cols_ref, s32[1024]{0:T(1024)S(1)} %select_n.732.list_ref, s32[32]{0:T(128)S(1)} %get-tuple-element.136.count_ref, ...), custom_call_target="tpu_custom_call" | custom-call | flops 5000000000 | bytes 12582912 | tf_op jit(solution)/shard_map/far/pallas_call | solution.py:296
  117.0 2.7 %collective-permute-start.12 = (f32[8,256,128]{2,1,0:T(8,128)}, f32[8,256,128]{2,1,0:T(8,128)}, u32[]{:S(2)}, u32[]{:S(2)}) collective-permute-start(f32[8,256,128]{2,1,0:T(8,128)} %get-tuple-element.44), channel_id=1, source_target_pairs={{0,24},{1,7},{2,26},{3,1},{4,28},{5,3},{6,30},{7,5},{8,0},{9,15},{... | collective-permute-start | bytes 3145736 | tf_op jit(solution)/shard_map/ppermute | solution.py:457
  121.3 10.5 %far.2 = (f32[8,256,128]{2,1,0:T(8,128)S(1)}, f32[8,256,128]{2,1,0:T(8,128)S(1)}, f32[8,256,128]{2,1,0:T(8,128)S(1)}, f32[8,256,128]{2,1,0:T(8,128)S(1)}, f32[1,256,128]{2,1,0:T(8,128)S(1)}) custom-call(s32[16]{0:T(128)S(1)} %reshape.1308.cols_ref, s32[1024]{0:T(1024)S(1)} %select_n.709.list_ref, s32[32]{0:T(128)S(1)} %get-tuple-element.70.count_ref, ...), custom_call_target="tpu_custom_call" | custom-call | flops 5000000000 | bytes 12582912 | tf_op jit(solution)/shard_map/far/pallas_call | solution.py:296
  131.8 3.4 %collective-permute-start.18 = (f32[8,256,128]{2,1,0:T(8,128)S(1)}, f32[8,256,128]{2,1,0:T(8,128)S(1)}, u32[]{:S(2)}, u32[]{:S(2)}) collective-permute-start(f32[8,256,128]{2,1,0:T(8,128)S(1)} %get-tuple-element.52), channel_id=1, source_target_pairs={{0,16},{1,5},{2,18},{3,7},{4,20},{5,1},{6,22},{7,3},{8,24},{9,13},... | collective-permute-start | bytes 3145736 | tf_op jit(solution)/shard_map/ppermute | solution.py:455
  135.2 19.0 %collective-permute-done.12 = f32[8,256,128]{2,1,0:T(8,128)} collective-permute-done((f32[8,256,128]{2,1,0:T(8,128)}, f32[8,256,128]{2,1,0:T(8,128)}, u32[]{:S(2)}, u32[]{:S(2)}) %collective-permute-start.12) | collective-permute-done | bytes 1048608 | tf_op jit(solution)/shard_map/ppermute | solution.py:457
  154.2 3.3 %collective-permute-start.19 = (f32[8,256,128]{2,1,0:T(8,128)S(1)}, f32[8,256,128]{2,1,0:T(8,128)S(1)}, u32[]{:S(2)}, u32[]{:S(2)}) collective-permute-start(f32[8,256,128]{2,1,0:T(8,128)S(1)} %get-tuple-element.53), channel_id=1, source_target_pairs={{0,24},{1,7},{2,26},{3,1},{4,28},{5,3},{6,30},{7,5},{8,0},{9,15},{... | collective-permute-start | bytes 3145736 | tf_op jit(solution)/shard_map/ppermute | solution.py:457
  157.5 1.3 fusion.60
  158.9 1.7 fusion.62
  161.3 1.5 collective-permute-start.13
  163.1 11.7 %collective-permute-done.15 = f32[2,2,256,128]{3,2,1,0:T(8,128)S(1)} collective-permute-done((f32[2,2,256,128]{3,2,1,0:T(8,128)S(1)}, f32[2,2,256,128]{3,2,1,0:T(8,128)S(1)}, u32[]{:S(2)}, u32[]{:S(2)}) %collective-permute-start.15) | collective-permute-done | bytes 524320 | tf_op jit(solution)/shard_map/ppermute | solution.py:471
  174.8 1.8 collective-permute-done.14
  176.6 6.2 %collective-permute-done.13 = f32[2,2,256,128]{3,2,1,0:T(8,128)S(1)} collective-permute-done((f32[2,2,256,128]{3,2,1,0:T(8,128)S(1)}, f32[2,2,256,128]{3,2,1,0:T(8,128)S(1)}, u32[]{:S(2)}, u32[]{:S(2)}) %collective-permute-start.13) | collective-permute-done | bytes 524320 | tf_op jit(solution)/shard_map/ppermute | solution.py:471
  183.3 3.9 %collective-permute-start.22 = (f32[2,2,256,128]{3,2,1,0:T(8,128)S(1)}, f32[2,2,256,128]{3,2,1,0:T(8,128)S(1)}, u32[]{:S(2)}, u32[]{:S(2)}) collective-permute-start(f32[2,2,256,128]{3,2,1,0:T(8,128)S(1)} %select_add_fusion), channel_id=1, source_target_pairs={{0,6},{1,25},{2,0},{3,27},{4,2},{5,29},{6,4},{7,31},{8,14},{9,1},{... | collective-permute-start | bytes 1572872 | tf_op jit(solution)/shard_map/ppermute | solution.py:471
  187.8 0.6 collective-permute-start.20
  188.8 0.8 fusion.6
  189.6 2.7 %collective-permute-start.16 = (f32[2,256,128]{2,1,0:T(8,128)S(1)}, f32[2,256,128]{2,1,0:T(8,128)S(1)}, u32[]{:S(2)}, u32[]{:S(2)}) collective-permute-start(f32[2,256,128]{2,1,0:T(8,128)S(1)} %get-tuple-element.74), channel_id=1, source_target_pairs={{0,1},{1,0},{2,3},{3,2},{4,5},{5,4},{6,7},{7,6},{8,9},{9,8},{10,11... | collective-permute-start | bytes 786440 | tf_op jit(solution)/shard_map/ppermute | solution.py:476
  192.4 6.7 %collective-permute-done.22 = f32[2,2,256,128]{3,2,1,0:T(8,128)S(1)} collective-permute-done((f32[2,2,256,128]{3,2,1,0:T(8,128)S(1)}, f32[2,2,256,128]{3,2,1,0:T(8,128)S(1)}, u32[]{:S(2)}, u32[]{:S(2)}) %collective-permute-start.22) | collective-permute-done | bytes 524320 | tf_op jit(solution)/shard_map/ppermute | solution.py:471
  199.0 4.0 %collective-permute-done.20 = f32[2,2,256,128]{3,2,1,0:T(8,128)S(1)} collective-permute-done((f32[2,2,256,128]{3,2,1,0:T(8,128)S(1)}, f32[2,2,256,128]{3,2,1,0:T(8,128)S(1)}, u32[]{:S(2)}, u32[]{:S(2)}) %collective-permute-start.20) | collective-permute-done | bytes 524320 | tf_op jit(solution)/shard_map/ppermute | solution.py:471
  203.0 0.8 fusion.4
  203.8 1.7 collective-permute-start.23
  205.5 1.2 collective-permute-done.23.refs_3_
  206.7 0.7 copy-done.5
  207.4 2.4 %final.1 = f32[2,16,4096]{2,1,0:T(8,128)} custom-call(f32[2,256,128]{2,1,0:T(8,128)} %get-tuple-element.75.refs_0_, f32[2,256,128]{2,1,0:T(8,128)} %copy-done.4, f32[2,256,128]{2,1,0:T(8,128)} %get-tuple-element.73.refs_2_, f32[2,256,128]{2,1,0:T(8,128)} %copy-done.5), custom_call_target="tpu_custom_call" | custom-call | tf_op jit(solution)/shard_map/final/pallas_call | solution.py:492
  (146 shorter events, 11.2 us)
Async XLA Ops:
  3.7 4.1 %copy-start.6 = (s32[4,8]{1,0:T(4,128)S(1)}, s32[4,8]{1,0:T(4,128)}, u32[]{:S(2)}) copy-start(s32[4,8]{1,0:T(4,128)} %param.13) | copy-start | bytes 388
  3.7 4.2 %copy-start.3 = (f32[1024,128]{1,0:T(8,128)S(1)}, f32[1024,128]{1,0:T(8,128)}, u32[]{:S(2)}) copy-start(f32[1024,128]{1,0:T(8,128)} %reshape_reshape.6.p_ref) | copy-start | bytes 1572868
  7.9 14.4 %copy-start.10 = (s32[2,16]{1,0:T(2,128)S(1)}, s32[2,16]{1,0:T(2,128)}, u32[]{:S(2)}) copy-start(s32[2,16]{1,0:T(2,128)} %param.17) | copy-start | bytes 388
  7.9 15.0 %copy-start.11 = (s32[1,64]{1,0:T(1,128)S(1)}, s32[1,64]{1,0:T(1,128)}, u32[]{:S(2)}) copy-start(s32[1,64]{1,0:T(1,128)} %param.16) | copy-start | bytes 772
  7.9 15.9 %copy-start.8 = (s32[1,32]{1,0:T(1,128)S(1)}, s32[1,32]{1,0:T(1,128)}, u32[]{:S(2)}) copy-start(s32[1,32]{1,0:T(1,128)} %param.15) | copy-start | bytes 388
  8.0 16.5 %copy-start.9 = (s32[4,8]{1,0:T(4,128)S(1)}, s32[4,8]{1,0:T(4,128)}, u32[]{:S(2)}) copy-start(s32[4,8]{1,0:T(4,128)} %param.14) | copy-start | bytes 388
  8.0 16.8 %copy-start.12 = (s32[4]{0:T(128)S(1)}, s32[4]{0:T(128)}, u32[]{:S(2)}) copy-start(s32[4]{0:T(128)} %param.11) | copy-start | bytes 52
  8.0 17.0 %copy-start.7 = (s32[4,16]{1,0:T(4,128)S(1)}, s32[4,16]{1,0:T(4,128)}, u32[]{:S(2)}) copy-start(s32[4,16]{1,0:T(4,128)} %param.10) | copy-start | bytes 772
  8.0 74.6 %collective-permute-start.9 = (f32[1032,128]{1,0:T(8,128)S(1)}, f32[1032,128]{1,0:T(8,128)S(1)}, u32[]{:S(2)}, u32[]{:S(2)}) collective-permute-start(f32[1032,128]{1,0:T(8,128)S(1)} %select_maximum_fusion.p0), channel_id=1, source_target_pairs={{96,0},{0,32},{32,64},{64,96},{97,1},{1,33},{33,65},{65,97},{98,2}... | collective-permute-start | bytes 1585160 | tf_op jit(solution)/shard_map/ppermute | solution.py:394
  10.5 72.2 %collective-permute-start.8 = (f32[1032,128]{1,0:T(8,128)S(1)}, f32[1032,128]{1,0:T(8,128)S(1)}, u32[]{:S(2)}, u32[]{:S(2)}) collective-permute-start(f32[1032,128]{1,0:T(8,128)S(1)} %select_maximum_fusion.p0), channel_id=1, source_target_pairs={{64,0},{96,32},{0,64},{32,96},{65,1},{97,33},{1,65},{33,97},{66,2}... | collective-permute-start | bytes 1585160 | tf_op jit(solution)/shard_map/ppermute | solution.py:394
  13.8 91.5 %all-to-all-start = ((f32[32,256,128]{2,1,0:T(8,128)}), f32[32,256,128]{2,1,0:T(8,128)}, u32[]{:S(2)}, u32[]{:S(2)}) async-start(f32[32,256,128]{2,1,0:T(8,128)} %outgoing.1), calls=%async_computation | async-start | bytes 8388608 | tf_op jit(solution)/shard_map/all_to_all | solution.py:388
  22.2 68.5 %copy-start.1 = (f32[4,16,4096]{2,1,0:T(8,128)S(1)}, f32[4,16,4096]{2,1,0:T(8,128)}, u32[]{:S(2)}) copy-start(f32[4,16,4096]{2,1,0:T(8,128)} %a_ref.5) | copy-start | bytes 3145732
  23.9 1.6 collective-permute-start
  25.5 42.9 %collective-permute-start.3 = (s32[2,128]{1,0:T(2,128)S(1)}, s32[2,128]{1,0:T(2,128)S(1)}, u32[]{:S(2)}, u32[]{:S(2)}) collective-permute-start(s32[2,128]{1,0:T(2,128)S(1)} %pad_add_fusion.1), channel_id=1, source_target_pairs={{6,0},{7,1},{0,2},{1,3},{2,4},{3,5},{4,6},{5,7},{14,8},{15,9},{8,1... | collective-permute-start | bytes 3080 | tf_op jit(solution)/shard_map/ppermute | solution.py:401
  27.0 41.4 %collective-permute-start.2 = (s32[2,128]{1,0:T(2,128)S(1)}, s32[2,128]{1,0:T(2,128)S(1)}, u32[]{:S(2)}, u32[]{:S(2)}) collective-permute-start(s32[2,128]{1,0:T(2,128)S(1)} %pad_add_fusion.1), channel_id=1, source_target_pairs={{4,0},{5,1},{6,2},{7,3},{0,4},{1,5},{2,6},{3,7},{12,8},{13,9},{14,... | collective-permute-start | bytes 3080 | tf_op jit(solution)/shard_map/ppermute | solution.py:401
  29.4 40.9 %collective-permute-start.1 = (s32[2,128]{1,0:T(2,128)S(1)}, s32[2,128]{1,0:T(2,128)S(1)}, u32[]{:S(2)}, u32[]{:S(2)}) collective-permute-start(s32[2,128]{1,0:T(2,128)S(1)} %pad_add_fusion.1), channel_id=1, source_target_pairs={{2,0},{3,1},{4,2},{5,3},{6,4},{7,5},{0,6},{1,7},{10,8},{11,9},{12,... | collective-permute-start | bytes 3080 | tf_op jit(solution)/shard_map/ppermute | solution.py:401
  70.4 5.6 %collective-permute-start.6 = (s32[8,128]{1,0:T(8,128)S(1)}, s32[8,128]{1,0:T(8,128)S(1)}, u32[]{:S(2)}, u32[]{:S(2)}) collective-permute-start(s32[8,128]{1,0:T(8,128)S(1)} %concatenate.38), channel_id=1, source_target_pairs={{24,0},{25,1},{26,2},{27,3},{28,4},{29,5},{30,6},{31,7},{0,8},{1,9... | collective-permute-start | bytes 12296 | tf_op jit(solution)/shard_map/ppermute | solution.py:402
  73.2 4.0 %collective-permute-start.5 = (s32[8,128]{1,0:T(8,128)S(1)}, s32[8,128]{1,0:T(8,128)S(1)}, u32[]{:S(2)}, u32[]{:S(2)}) collective-permute-start(s32[8,128]{1,0:T(8,128)S(1)} %concatenate.38), channel_id=1, source_target_pairs={{16,0},{17,1},{18,2},{19,3},{20,4},{21,5},{22,6},{23,7},{24,8},{25... | collective-permute-start | bytes 12296 | tf_op jit(solution)/shard_map/ppermute | solution.py:402
  75.3 2.8 %collective-permute-start.4 = (s32[8,128]{1,0:T(8,128)S(1)}, s32[8,128]{1,0:T(8,128)S(1)}, u32[]{:S(2)}, u32[]{:S(2)}) collective-permute-start(s32[8,128]{1,0:T(8,128)S(1)} %concatenate.38), channel_id=1, source_target_pairs={{8,0},{9,1},{10,2},{11,3},{12,4},{13,5},{14,6},{15,7},{16,8},{17,9... | collective-permute-start | bytes 12296 | tf_op jit(solution)/shard_map/ppermute | solution.py:402
  76.0 12.5 %collective-permute-start.7 = (f32[1032,128]{1,0:T(8,128)S(1)}, f32[1032,128]{1,0:T(8,128)S(1)}, u32[]{:S(2)}, u32[]{:S(2)}) collective-permute-start(f32[1032,128]{1,0:T(8,128)S(1)} %select_maximum_fusion.p0), channel_id=1, source_target_pairs={{32,0},{64,32},{96,64},{0,96},{33,1},{65,33},{97,65},{1,97},{34,2}... | collective-permute-start | bytes 1585160 | tf_op jit(solution)/shard_map/ppermute | solution.py:394
  101.1 3.2 %copy-start = (f32[4,8,8,64,128]{4,3,2,1,0:T(8,128)}, f32[4,8,8,64,128]{4,3,2,1,0:T(8,128)S(1)}, u32[]{:S(2)}) copy-start(f32[4,8,8,64,128]{4,3,2,1,0:T(8,128)S(1)} %get-tuple-element.35.m_ref) | copy-start | bytes 25165828
  104.3 1.0 copy-start.2
  116.9 18.3 %collective-permute-start.10 = (f32[8,256,128]{2,1,0:T(8,128)}, f32[8,256,128]{2,1,0:T(8,128)}, u32[]{:S(2)}, u32[]{:S(2)}) collective-permute-start(f32[8,256,128]{2,1,0:T(8,128)} %get-tuple-element.42), channel_id=1, source_target_pairs={{0,8},{1,3},{2,10},{3,5},{4,12},{5,7},{6,14},{7,1},{8,16},{9,11},{... | collective-permute-start | bytes 3145736 | tf_op jit(solution)/shard_map/ppermute | solution.py:457
  117.0 37.2 %collective-permute-start.12 = (f32[8,256,128]{2,1,0:T(8,128)}, f32[8,256,128]{2,1,0:T(8,128)}, u32[]{:S(2)}, u32[]{:S(2)}) collective-permute-start(f32[8,256,128]{2,1,0:T(8,128)} %get-tuple-element.44), channel_id=1, source_target_pairs={{0,24},{1,7},{2,26},{3,1},{4,28},{5,3},{6,30},{7,5},{8,0},{9,15},{... | collective-permute-start | bytes 3145736 | tf_op jit(solution)/shard_map/ppermute | solution.py:457
  119.7 34.5 %collective-permute-start.11 = (f32[8,256,128]{2,1,0:T(8,128)S(1)}, f32[8,256,128]{2,1,0:T(8,128)}, u32[]{:S(2)}, u32[]{:S(2)}) collective-permute-start(f32[8,256,128]{2,1,0:T(8,128)S(1)} %get-tuple-element.43), channel_id=1, source_target_pairs={{0,16},{1,5},{2,18},{3,7},{4,20},{5,1},{6,22},{7,3},{8,24},{9,13},... | collective-permute-start | bytes 3145736 | tf_op jit(solution)/shard_map/ppermute | solution.py:455
  131.8 29.5 %collective-permute-start.18 = (f32[8,256,128]{2,1,0:T(8,128)S(1)}, f32[8,256,128]{2,1,0:T(8,128)S(1)}, u32[]{:S(2)}, u32[]{:S(2)}) collective-permute-start(f32[8,256,128]{2,1,0:T(8,128)S(1)} %get-tuple-element.52), channel_id=1, source_target_pairs={{0,16},{1,5},{2,18},{3,7},{4,20},{5,1},{6,22},{7,3},{8,24},{9,13},... | collective-permute-start | bytes 3145736 | tf_op jit(solution)/shard_map/ppermute | solution.py:455
  154.2 28.6 %collective-permute-start.17 = (f32[8,256,128]{2,1,0:T(8,128)S(1)}, f32[8,256,128]{2,1,0:T(8,128)S(1)}, u32[]{:S(2)}, u32[]{:S(2)}) collective-permute-start(f32[8,256,128]{2,1,0:T(8,128)S(1)} %get-tuple-element.51), channel_id=1, source_target_pairs={{0,8},{1,3},{2,10},{3,5},{4,12},{5,7},{6,14},{7,1},{8,16},{9,11},{... | collective-permute-start | bytes 3145736 | tf_op jit(solution)/shard_map/ppermute | solution.py:457
  154.2 28.6 %collective-permute-start.19 = (f32[8,256,128]{2,1,0:T(8,128)S(1)}, f32[8,256,128]{2,1,0:T(8,128)S(1)}, u32[]{:S(2)}, u32[]{:S(2)}) collective-permute-start(f32[8,256,128]{2,1,0:T(8,128)S(1)} %get-tuple-element.53), channel_id=1, source_target_pairs={{0,24},{1,7},{2,26},{3,1},{4,28},{5,3},{6,30},{7,5},{8,0},{9,15},{... | collective-permute-start | bytes 3145736 | tf_op jit(solution)/shard_map/ppermute | solution.py:457
  160.7 14.1 %collective-permute-start.15 = (f32[2,2,256,128]{3,2,1,0:T(8,128)S(1)}, f32[2,2,256,128]{3,2,1,0:T(8,128)S(1)}, u32[]{:S(2)}, u32[]{:S(2)}) collective-permute-start(f32[2,2,256,128]{3,2,1,0:T(8,128)S(1)} %select_add_fusion.4), channel_id=1, source_target_pairs={{0,6},{1,25},{2,0},{3,27},{4,2},{5,29},{6,4},{7,31},{8,14},{9,1},{... | collective-permute-start | bytes 1572872 | tf_op jit(solution)/shard_map/ppermute | solution.py:471
  161.0 15.6 %collective-permute-start.14 = (f32[2,2,256,128]{3,2,1,0:T(8,128)S(1)}, f32[2,2,256,128]{3,2,1,0:T(8,128)S(1)}, u32[]{:S(2)}, u32[]{:S(2)}) collective-permute-start(f32[2,2,256,128]{3,2,1,0:T(8,128)S(1)} %select_add_fusion.5), channel_id=1, source_target_pairs={{0,4},{1,17},{2,6},{3,19},{4,0},{5,21},{6,2},{7,23},{8,12},{9,25},... | collective-permute-start | bytes 1572872 | tf_op jit(solution)/shard_map/ppermute | solution.py:471
  161.3 21.5 %collective-permute-start.13 = (f32[2,2,256,128]{3,2,1,0:T(8,128)S(1)}, f32[2,2,256,128]{3,2,1,0:T(8,128)S(1)}, u32[]{:S(2)}, u32[]{:S(2)}) collective-permute-start(f32[2,2,256,128]{3,2,1,0:T(8,128)S(1)} %select_add_fusion.6), channel_id=1, source_target_pairs={{0,2},{1,9},{2,4},{3,11},{4,6},{5,13},{6,0},{7,15},{8,10},{9,17},{... | collective-permute-start | bytes 1572872 | tf_op jit(solution)/shard_map/ppermute | solution.py:471
  183.3 15.7 %collective-permute-start.22 = (f32[2,2,256,128]{3,2,1,0:T(8,128)S(1)}, f32[2,2,256,128]{3,2,1,0:T(8,128)S(1)}, u32[]{:S(2)}, u32[]{:S(2)}) collective-permute-start(f32[2,2,256,128]{3,2,1,0:T(8,128)S(1)} %select_add_fusion), channel_id=1, source_target_pairs={{0,6},{1,25},{2,0},{3,27},{4,2},{5,29},{6,4},{7,31},{8,14},{9,1},{... | collective-permute-start | bytes 1572872 | tf_op jit(solution)/shard_map/ppermute | solution.py:471
  187.5 11.6 %collective-permute-start.21 = (f32[2,2,256,128]{3,2,1,0:T(8,128)S(1)}, f32[2,2,256,128]{3,2,1,0:T(8,128)S(1)}, u32[]{:S(2)}, u32[]{:S(2)}) collective-permute-start(f32[2,2,256,128]{3,2,1,0:T(8,128)S(1)} %select_add_fusion.1), channel_id=1, source_target_pairs={{0,4},{1,17},{2,6},{3,19},{4,0},{5,21},{6,2},{7,23},{8,12},{9,25},... | collective-permute-start | bytes 1572872 | tf_op jit(solution)/shard_map/ppermute | solution.py:471
  187.8 15.2 %collective-permute-start.20 = (f32[2,2,256,128]{3,2,1,0:T(8,128)S(1)}, f32[2,2,256,128]{3,2,1,0:T(8,128)S(1)}, u32[]{:S(2)}, u32[]{:S(2)}) collective-permute-start(f32[2,2,256,128]{3,2,1,0:T(8,128)S(1)} %select_add_fusion.2), channel_id=1, source_target_pairs={{0,2},{1,9},{2,4},{3,11},{4,6},{5,13},{6,0},{7,15},{8,10},{9,17},{... | collective-permute-start | bytes 1572872 | tf_op jit(solution)/shard_map/ppermute | solution.py:471
  189.6 15.9 %collective-permute-start.16 = (f32[2,256,128]{2,1,0:T(8,128)S(1)}, f32[2,256,128]{2,1,0:T(8,128)S(1)}, u32[]{:S(2)}, u32[]{:S(2)}) collective-permute-start(f32[2,256,128]{2,1,0:T(8,128)S(1)} %get-tuple-element.74), channel_id=1, source_target_pairs={{0,1},{1,0},{2,3},{3,2},{4,5},{5,4},{6,7},{7,6},{8,9},{9,8},{10,11... | collective-permute-start | bytes 786440 | tf_op jit(solution)/shard_map/ppermute | solution.py:476
  203.8 2.8 %collective-permute-start.23 = (f32[2,256,128]{2,1,0:T(8,128)S(1)}, f32[2,256,128]{2,1,0:T(8,128)S(1)}, u32[]{:S(2)}, u32[]{:S(2)}) collective-permute-start(f32[2,256,128]{2,1,0:T(8,128)S(1)} %get-tuple-element.72), channel_id=1, source_target_pairs={{0,1},{1,0},{2,3},{3,2},{4,5},{5,4},{6,7},{7,6},{8,9},{9,8},{10,11... | collective-permute-start | bytes 786440 | tf_op jit(solution)/shard_map/ppermute | solution.py:476
  205.5 1.2 copy-start.4
  206.7 0.7 copy-start.5

commit v2 on v0

--- a/solution.py
+++ b/solution.py
@@ -26,12 +26,6 @@
     hi = x.astype(jnp.bfloat16)
     lo = (x - hi.astype(jnp.float32)).astype(jnp.bfloat16)
     return hi, lo
-
-
-def paired(blocks):
-    rows, n, _ = blocks.shape
-    view = blocks.reshape(rows, n // 2, 2, BS, BS)
-    return view.transpose(0, 1, 3, 2, 4).reshape(rows, n // 2, BS, LANES)
 
 
 def first_half(shape):
@@ -215,11 +209,28 @@
             ]
 
 
-def outgoing_kernel(pick_ref, p_ref, out_ref, sem):
+def outgoing_kernel(pick_ref, blocks_ref, ids_ref, out_ref, carried_ref, spread_ref, sem):
+    half = BS // 2
+    first = first_half((half, LANES))
+
+    def lay(r, carry):
+        for k in range(half):
+            spread_ref[pl.ds(k, KP, stride=half), :] = blocks_ref[r, :, k * LANES : (k + 1) * LANES]
+        for s in range(KP // 2):
+            even = spread_ref[2 * s * half : (2 * s + 1) * half, :]
+            odd = spread_ref[(2 * s + 1) * half : (2 * s + 2) * half, :]
+            base = r * ROW_T + s * BS
+            carried_ref[pl.ds(base, half, stride=2), :] = jnp.where(first, even, pltpu.roll(odd, BS, axis=1))
+            carried_ref[pl.ds(base + 1, half, stride=2), :] = jnp.where(first, pltpu.roll(even, BS, axis=1), odd)
+        return carry
+
+    lax.fori_loop(0, RB, lay, 0)
+    carried_ref[RB * ROW_T : RB * ROW_T + 8, :] = jnp.zeros((8, LANES), jnp.float32)
+    carried_ref[RB * ROW_T : RB * ROW_T + RB, 0:KP] = ids_ref[...].astype(jnp.float32)
     n = out_ref.shape[0]
 
     def copy(k):
-        src = p_ref.at[pl.ds(pl.multiple_of(pick_ref[k] * ROW_T, ROW_T), ROW_T)]
+        src = carried_ref.at[pl.ds(pl.multiple_of(pick_ref[k] * ROW_T, ROW_T), ROW_T)]
         return pltpu.make_async_copy(src, out_ref.at[k], sem.at[k])
 
     def start(k, carry):
@@ -277,7 +288,7 @@
                 pltpu.VMEM((KA * BS // 2, LANES), jnp.float32),
             ],
         ),
-        compiler_params=pltpu.CompilerParams(vmem_limit_bytes=40 * 2**20),
+        compiler_params=pltpu.CompilerParams(vmem_limit_bytes=60 * 2**20),
         cost_estimate=pl.CostEstimate(flops=10**10, bytes_accessed=16 * 2**20, transcendentals=0),
         name="near",
     )(cols, lists, counts, operator_blocks, *near_rows)
@@ -286,6 +297,7 @@
 def far_call(cols, lists, counts, position, operator_blocks, far_rows, matched, left, n_dom):
     far_spec = lambda m: pl.BlockSpec((1, ROW_T, LANES), lambda i, cols, *_: (cols[i * KH + m], 0, 0))
     slot_shape = (KC // 2 * BS, LANES)
+    hbm = lambda x: pltpu.with_memory_space_constraint(x, pltpu.HBM)
     return pl.pallas_call(
         far_kernel,
         out_shape=tuple(jax.ShapeDtypeStruct((n,) + slot_shape, jnp.float32) for n in (8, 8, 8, 8, 1)),
@@ -311,7 +323,7 @@
         compiler_params=pltpu.CompilerParams(vmem_limit_bytes=40 * 2**20),
         cost_estimate=pl.CostEstimate(flops=10**10, bytes_accessed=24 * 2**20, transcendentals=0),
         name="far",
-    )(cols, lists, counts, position, operator_blocks, *([far_rows] * KH), matched, left)
+    )(cols, lists, counts, position, operator_blocks, *([far_rows] * KH), hbm(matched), hbm(left))
 
 
 SIDE = 4
@@ -355,38 +367,43 @@
     d = lax.axis_index("dom")
     owner = slot_owner_row.reshape(-1)
 
-    panels = paired(prolong_blocks).reshape(RB * ROW_T, LANES)
-    outgoing = pl.pallas_call(
+    outgoing, carried = pl.pallas_call(
         outgoing_kernel,
-        out_shape=jax.ShapeDtypeStruct((n_dom, ROW_T, LANES), jnp.float32),
+        out_shape=(
+            jax.ShapeDtypeStruct((n_dom, ROW_T, LANES), jnp.float32),
+            jax.ShapeDtypeStruct((RB * ROW_T + 8, LANES), jnp.float32),
+        ),
         grid_spec=pltpu.PrefetchScalarGridSpec(
             num_scalar_prefetch=1,
             grid=(1,),
-            in_specs=[pl.BlockSpec((RB * ROW_T, LANES), lambda i, *_: (0, 0))],
-            out_specs=pl.BlockSpec(memory_space=pltpu.HBM),
-            scratch_shapes=[pltpu.SemaphoreType.DMA((n_dom,))],
-        ),
+            in_specs=[
+                pl.BlockSpec((RB, KP, BS * BS), lambda i, *_: (0, 0, 0)),
+                pl.BlockSpec((RB, KP), lambda i, *_: (0, 0)),
+            ],
+            out_specs=(
+                pl.BlockSpec(memory_space=pltpu.HBM),
+                pl.BlockSpec((RB * ROW_T + 8, LANES), lambda i, *_: (0, 0)),
+            ),
+            scratch_shapes=[pltpu.VMEM((KP * BS // 2, LANES), jnp.float32), pltpu.SemaphoreType.DMA((n_dom,))],
+        ),
+        cost_estimate=pl.CostEstimate(flops=0, bytes_accessed=6 * 2**20, transcendentals=0),
         name="outgoing",
-    )(send_lists.reshape(-1), panels)
+    )(send_lists.reshape(-1), prolong_blocks, prolong_cols)
     far_rows = lax.all_to_all(outgoing, "dom", split_axis=0, concat_axis=0, tiled=True)
 
-    id_tile = jnp.pad(prolong_cols.reshape(1, PAIRS).astype(jnp.float32), ((0, 7), (0, LANES - PAIRS)))
-    carried = jnp.concatenate([panels, id_tile], axis=0)
-    near_rows = [carried]
-    for k in range(1, n_grp):
-        near_rows.append(lax.ppermute(carried, "grp", [((z + k) % n_grp, z) for z in range(n_grp)]))
-
-    mine = jnp.concatenate(
-        [prolong_cols.reshape(-1), coarse_pattern.reshape(-1), send_lists.reshape(-1), owner.reshape(n_dom, 2)[:, 0]]
+    wide = lambda x: jnp.pad(x, ((0, 0), (0, 2 * n_dom - x.shape[1])))
+    mine = jnp.concatenate([wide(prolong_cols), wide(coarse_pattern), wide(send_lists), slot_owner_row], axis=0)
+    told = lax.all_to_all(
+        jnp.broadcast_to(mine[None], (n_dom,) + mine.shape), "dom", split_axis=0, concat_axis=0, tiled=True
     )
-    told = lax.all_to_all(
-        jnp.broadcast_to(mine[None], (n_dom, mine.shape[0])), "dom", split_axis=0, concat_axis=0, tiled=True
+    told, operator_cols, prolong_slot, halo_count, owner = lax.optimization_barrier(
+        (told, operator_cols, prolong_slot, halo_count, owner)
     )
-    all_cols = told[:, :PAIRS].reshape(n_dom, RB, KP)
-    patterns = told[:, PAIRS : 2 * PAIRS].reshape(2 * n_dom, KC)
-    here = jnp.arange(n_dom, dtype=jnp.int32)[None, :] == d
-    picked = jnp.sum(jnp.where(here, told[:, 2 * PAIRS : 2 * PAIRS + n_dom], 0), axis=1)
-    first_rows = told[:, 2 * PAIRS + n_dom :]
+    all_cols = told[:, :RB, :KP]
+    patterns = told[:, RB : RB + 2, :KC].reshape(2 * n_dom, KC)
+    here = jnp.arange(2 * n_dom, dtype=jnp.int32)[None, :] == d
+    picked = jnp.sum(jnp.where(here, told[:, RB + 2], 0), axis=1)
+    slot_rows = told[:, RB + 3]
     far_ids = jnp.sum(
         jnp.where((picked[:, None] == jnp.arange(RB, dtype=jnp.int32))[:, :, None], all_cols, 0), axis=1
     )
@@ -399,8 +416,13 @@
     position = ((to_u - u) % SIDE) * 8 + ((to_v - v) % SIDE) * 2 + (to_k - k) % 2
     position = jnp.where(slots % 2 == 1, n_dom, position)
 
+    passed, _ = lax.optimization_barrier((carried, wanted))
+    near_rows = [carried]
+    for dz in range(1, n_grp):
+        near_rows.append(lax.ppermute(passed, "grp", [((z + dz) % n_grp, z) for z in range(n_grp)]))
+
     near_ids_table = jnp.concatenate(
-        [rows[RB * ROW_T, :PAIRS].astype(jnp.int32).reshape(RB, KP) for rows in near_rows], axis=0
+        [rows[RB * ROW_T : RB * ROW_T + RB, :KP].astype(jnp.int32) for rows in near_rows], axis=0
     )
     near_slots = operator_cols[:, :KG]
     near_cols = (((near_slots // RB) - g) % n_grp * RB + near_slots % RB).reshape(-1)
@@ -416,11 +438,12 @@
     chunks = far_call(far_cols, far_list, far_count, position, operator_blocks, far_rows, matched, left, n_dom)
     slot_shape = (KC // 2 * BS, LANES)
 
-    arriving = [chunks[0]] + [lax.ppermute(chunks[t], "dom", shift_pairs(t, 0)) for t in range(1, SIDE)]
+    sent = {t: lax.ppermute(chunks[t], "dom", shift_pairs(t, 0)) for t in (2, 1, 3)}
+    *arriving, own_second = lax.optimization_barrier((chunks[0], sent[1], sent[2], sent[3], chunks[4]))
     sources = jnp.stack([device_at(u - t, v, k, d) for t in range(SIDE)])
     owners = jnp.stack([device_at(u, v + p // 2, k + p % 2, d) for p in range(8)])
-    rows_from = pick_rows(first_rows, sources)
-    row_of = pick_rows(rows_from.T, owners).T
+    rows_from = pick_rows(slot_rows, sources)
+    row_of = pick_rows(rows_from.T, 2 * owners).T
     own_first = row_of[0, 0]
 
     def owned(t2):
@@ -431,7 +454,7 @@
             total = total + jnp.where(to_row[:, :, None, None], part, 0.0)
         if t2 == 0:
             to_row = (jnp.arange(2, dtype=jnp.int32) == 1 - own_first)[None] & (jnp.arange(2) == 0)[:, None]
-            total = total + jnp.where(to_row[:, :, None, None], chunks[4][:, None], 0.0)
+            total = total + jnp.where(to_row[:, :, None, None], own_second[:, None], 0.0)
         return total
 
     sent = {t2: lax.ppermute(owned(t2), "dom", shift_pairs(t2, 1)) for t2 in (2, 1, 3)}
@@ -447,6 +470,7 @@
         in_specs=[row_spec, row_spec],
         out_specs=pl.BlockSpec((1, KC, BS * BS), lambda i: (i, 0, 0)),
         scratch_shapes=[pltpu.VMEM((KC * BS // 2, LANES), jnp.float32)],
+        compiler_params=pltpu.CompilerParams(vmem_limit_bytes=16 * 2**20),
         name="final",
     )(sums[1], swapped)
 

time: 196 us -> 177 us (0.903)
  local copies, waits for them, and re-layouts: 20.7 us -> 4.43 us
    all_to_all x1, waiting for transfers between devices: 28.9 us -> 4.99 us  [per_device(): lax.all_to_all(outgoing, 'dom', split_axis=0, concat_axis=0, tiled=True)]
    ppermute x3, waiting for transfers between devices: 0.01 us -> 21 us  [per_device(): lax.ppermute(passed, 'grp', [((z + dz) % n_grp, z) for z in range(n_grp)])]
    unnamed x37 -> x23, local copies, waits for them, and re-layouts: 12.5 us -> 0.8 us
    reshape x4 -> x0, local copies, waits for them, and re-layouts: 2.43 us -> none  [the longest x2 2.27 us: paired(): view = blocks.reshape(rows, n // 2, 2, BS, BS)]
    ppermute x3, waiting for transfers between devices: 41.1 us -> 43.1 us  [per_device(): lax.ppermute(chunks[t], 'dom', shift_pairs(t, 0))]
  transfers between devices with their start and end apart: 12 -> 12, of which waited for: 9 -> 10; matrix products, arithmetic and copies ran while one was open for 7% -> 7% of each run, Pallas kernels for 8% -> 10%
where the time goes in v2:
time: 177 us; the launch traced here: 176 us
  waiting for transfers between devices  95.5 us (54%)
  Pallas kernels  33.3 us (19%)
  starting transfers between devices  31.8 us (18%)
  other arithmetic  9.94 us (6%)
  local copies, waits for them, and re-layouts  4.43 us (3%)
    ppermute x3, waiting for transfers between devices, per_device(): lax.ppermute(chunks[t], 'dom', shift_pairs(t, 0))  43.1 us
    ppermute x3, waiting for transfers between devices, per_device(): lax.ppermute(owned(t2), 'dom', shift_pairs(t2, 1))  24.2 us
    ppermute x3, waiting for transfers between devices, per_device(): lax.ppermute(passed, 'grp', [((z + dz) % n_grp, z) for z in range(n_grp)])  21 us
    pallas_call x1, Pallas kernels, far_call(): pl.pallas_call(far_kernel, out_shape=tuple((jax.ShapeDtypeStruct((n,) + s...  14.4 us
    pallas_call x1, Pallas kernels, near_call(): pl.pallas_call(near_kernel, out_shape=(jax.ShapeDtypeStruct((RB, KP, KC /...  12.1 us
    all_to_all x1, starting transfers between devices, per_device(): lax.all_to_all(jnp.broadcast_to(mine[None], (n_dom,) + mine.shape), 'dom'...  8.59 us
    all_to_all x1, starting transfers between devices, per_device(): lax.all_to_all(outgoing, 'dom', split_axis=0, concat_axis=0, tiled=True)  7.03 us
    ppermute x3, starting transfers between devices, per_device(): lax.ppermute(passed, 'grp', [((z + dz) % n_grp, z) for z in range(n_grp)])  5.74 us
  transfers between devices with their start and end apart: 12, of which 10 were waited for; matrix products, arithmetic and copies ran while one was open for 7% of the time, Pallas kernels for 10%

profile of v2, /device:TPU:1, one launch (start us, length us, event | category | flops | bytes accessed | tf_op | source)
XLA Modules:
  0.0 176.3 jit_solution(6883323591266296340)
XLA Ops:
  0.0 0.7 fusion.8
  0.7 0.8 reshape.889
  1.5 8.6 %all-to-all-start = ((s32[32,1,512]{2,1,0:T(1,128)}), s32[32,1,512]{2,1,0:T(1,128)S(1)}, u32[]{:S(2)}, u32[]{:S(2)}) async-start(s32[32,1,512]{2,1,0:T(1,128)} %reshape.889), calls=%async_computation | async-start | bytes 131072 | tf_op jit(solution)/shard_map/all_to_all | solution.py:396
  10.6 5.5 %outgoing.1 = (f32[32,256,128]{2,1,0:T(8,128)}, f32[1032,128]{1,0:T(8,128)}) custom-call(s32[32]{0:T(128)} %bitcast.70, f32[4,8,4096]{2,1,0:T(8,128)} %blocks_ref.1, s32[4,8]{1,0:T(4,128)} %ids_ref.1), custom_call_target="tpu_custom_call" | custom-call | bytes 6291456 | tf_op jit(solution)/shard_map/outgoing/pallas_call | solution.py:370
  16.1 0.7 slice_convert_fusion.3
  16.9 0.6 all-to-all-done
  17.5 7.0 %all-to-all-start.1 = ((f32[32,256,128]{2,1,0:T(8,128)}), f32[32,256,128]{2,1,0:T(8,128)}, u32[]{:S(2)}, u32[]{:S(2)}) async-start(f32[32,256,128]{2,1,0:T(8,128)} %get-tuple-element.30), calls=%async_computation.1 | async-start | bytes 8388608 | tf_op jit(solution)/shard_map/all_to_all | solution.py:392
  24.5 0.5 broadcast.581
  25.0 0.8 reduce.5
  26.1 0.2 select_reduce_fusion.10
  27.1 0.4 select_reduce_fusion.6
  27.6 0.6 select_reduce_fusion.4
  28.2 0.2 compare_reduce_fusion.1
  28.5 1.7 collective-permute-start.2
  30.2 3.3 %collective-permute-start.1 = (f32[1032,128]{1,0:T(8,128)S(1)}, f32[1032,128]{1,0:T(8,128)S(1)}, u32[]{:S(2)}, u32[]{:S(2)}) collective-permute-start(f32[1032,128]{1,0:T(8,128)S(1)} %copy-done.6), channel_id=1, source_target_pairs={{64,0},{96,32},{0,64},{32,96},{65,1},{97,33},{1,65},{33,97},{66,2}... | collective-permute-start | bytes 1585160 | tf_op jit(solution)/shard_map/ppermute | solution.py:422
  33.5 0.7 collective-permute-start
  34.6 0.2 select_reduce_fusion.3
  34.9 0.6 select_reduce_fusion.2
  35.8 8.8 %collective-permute-done.2.p3 = f32[1032,128]{1,0:T(8,128)S(1)} collective-permute-done((f32[1032,128]{1,0:T(8,128)S(1)}, f32[1032,128]{1,0:T(8,128)S(1)}, u32[]{:S(2)}, u32[]{:S(2)}) %collective-permute-start.2) | collective-permute-done | bytes 528416 | tf_op jit(solution)/shard_map/ppermute | solution.py:422
  44.6 12.2 %collective-permute-done.1.p2 = f32[1032,128]{1,0:T(8,128)S(1)} collective-permute-done((f32[1032,128]{1,0:T(8,128)S(1)}, f32[1032,128]{1,0:T(8,128)S(1)}, u32[]{:S(2)}, u32[]{:S(2)}) %collective-permute-start.1) | collective-permute-done | bytes 528416 | tf_op jit(solution)/shard_map/ppermute | solution.py:422
  57.6 0.6 select_reduce_fusion.1
  58.2 0.6 select_reduce_fusion
  58.9 0.7 select_n.493.list_ref
  59.6 12.1 %near.1 = (f32[4,8,8,64,128]{4,3,2,1,0:T(8,128)}, bf16[4,8,128,128]{3,2,1,0:T(8,128)(2,1)}) custom-call(s32[48]{0:T(128)} %copy-done.3, s32[3072]{0:T(1024)} %select_n.493.list_ref, s32[32]{0:T(128)} %copy-done.2, f32[4,16,4096]{2,1,0:T(8,128)} %a_ref.3, f32[1032,128]{1,0:T(8,128)} %get-tuple-element.32.p0, f32[1032,128]{1,0:T(8,128)} %copy-done.9, ...), custom_call_target="tpu_custom_call" | custom-call | flops 10000000000 | bytes 16777216 | tf_op jit(solution)/shard_map/near/pallas_call | solution.py:271
  71.7 5.0 %all-to-all-done.1.f0.f1.f2.f3 = f32[32,256,128]{2,1,0:T(8,128)} async-done(((f32[32,256,128]{2,1,0:T(8,128)}), f32[32,256,128]{2,1,0:T(8,128)}, u32[]{:S(2)}, u32[]{:S(2)}) %all-to-all-start.1) | async-done | bytes 4194336 | tf_op jit(solution)/shard_map/all_to_all | solution.py:392
  76.7 14.4 %far.1 = (f32[8,512,128]{2,1,0:T(8,128)S(1)}, f32[8,512,128]{2,1,0:T(8,128)S(1)}, f32[8,512,128]{2,1,0:T(8,128)S(1)}, f32[8,512,128]{2,1,0:T(8,128)S(1)}, f32[1,512,128]{2,1,0:T(8,128)S(1)}) custom-call(s32[16]{0:T(128)S(1)} %reshape.882.cols_ref, s32[1024]{0:T(1024)S(1)} %select_n.472.list_ref, s32[32]{0:T(128)S(1)} %get-tuple-element.47.count_ref, ...), custom_call_target="tpu_custom_call" | custom-call | flops 10000000000 | bytes 25165824 | tf_op jit(solution)/shard_map/far/pallas_call | solution.py:301
  91.2 2.6 %collective-permute-start.3 = (f32[8,512,128]{2,1,0:T(8,128)S(1)}, f32[8,512,128]{2,1,0:T(8,128)S(1)}, u32[]{:S(2)}, u32[]{:S(2)}) collective-permute-start(f32[8,512,128]{2,1,0:T(8,128)S(1)} %get-tuple-element.36), channel_id=1, source_target_pairs={{0,8},{1,3},{2,10},{3,5},{4,12},{5,7},{6,14},{7,1},{8,16},{9,11},{... | collective-permute-start | bytes 6291464 | tf_op jit(solution)/shard_map/ppermute | solution.py:441
  93.8 1.8 collective-permute-start.4
  95.5 0.7 collective-permute-start.5
  96.6 0.5 slice.171
  98.3 19.8 %collective-permute-done.3 = f32[8,512,128]{2,1,0:T(8,128)S(1)} collective-permute-done((f32[8,512,128]{2,1,0:T(8,128)S(1)}, f32[8,512,128]{2,1,0:T(8,128)S(1)}, u32[]{:S(2)}, u32[]{:S(2)}) %collective-permute-start.3) | collective-permute-done | bytes 2097184 | tf_op jit(solution)/shard_map/ppermute | solution.py:441
  118.1 23.4 %collective-permute-done.4 = f32[8,512,128]{2,1,0:T(8,128)S(1)} collective-permute-done((f32[8,512,128]{2,1,0:T(8,128)S(1)}, f32[8,512,128]{2,1,0:T(8,128)S(1)}, u32[]{:S(2)}, u32[]{:S(2)}) %collective-permute-start.4) | collective-permute-done | bytes 2097184 | tf_op jit(solution)/shard_map/ppermute | solution.py:441
  141.4 0.3 fusion.25
  141.7 0.4 fusion.27
  142.1 0.3 select_add_fusion
  142.4 0.4 collective-permute-start.8
  142.9 0.3 select_add_fusion.1
  143.2 0.9 collective-permute-start.7
  144.1 0.3 select_add_fusion.2
  144.4 0.6 collective-permute-start.6
  145.3 0.4 select_add_fusion.3
  145.7 10.7 %collective-permute-done.8 = f32[2,2,512,128]{3,2,1,0:T(8,128)S(1)} collective-permute-done((f32[2,2,512,128]{3,2,1,0:T(8,128)S(1)}, f32[2,2,512,128]{3,2,1,0:T(8,128)S(1)}, u32[]{:S(2)}, u32[]{:S(2)}) %collective-permute-start.8) | collective-permute-done | bytes 1048608 | tf_op jit(solution)/shard_map/ppermute | solution.py:460
  156.5 2.3 %collective-permute-done.7 = f32[2,2,512,128]{3,2,1,0:T(8,128)S(1)} collective-permute-done((f32[2,2,512,128]{3,2,1,0:T(8,128)S(1)}, f32[2,2,512,128]{3,2,1,0:T(8,128)S(1)}, u32[]{:S(2)}, u32[]{:S(2)}) %collective-permute-start.7) | collective-permute-done | bytes 1048608 | tf_op jit(solution)/shard_map/ppermute | solution.py:460
  158.8 11.2 %collective-permute-done.6 = f32[2,2,512,128]{3,2,1,0:T(8,128)S(1)} collective-permute-done((f32[2,2,512,128]{3,2,1,0:T(8,128)S(1)}, f32[2,2,512,128]{3,2,1,0:T(8,128)S(1)}, u32[]{:S(2)}, u32[]{:S(2)}) %collective-permute-start.6) | collective-permute-done | bytes 1048608 | tf_op jit(solution)/shard_map/ppermute | solution.py:460
  170.0 0.2 fusion.1
  170.2 3.4 %collective-permute-start.9 = (f32[2,512,128]{2,1,0:T(8,128)S(1)}, f32[2,512,128]{2,1,0:T(8,128)S(1)}, u32[]{:S(2)}, u32[]{:S(2)}) collective-permute-start(f32[2,512,128]{2,1,0:T(8,128)S(1)} %get-tuple-element.49), channel_id=1, source_target_pairs={{0,1},{1,0},{2,3},{3,2},{4,5},{5,4},{6,7},{7,6},{8,9},{9,8},{10,11... | collective-permute-start | bytes 1572872 | tf_op jit(solution)/shard_map/ppermute | solution.py:463
  173.5 1.5 collective-permute-done.9.got_ref
  175.1 1.3 final.1
  (91 shorter events, 4.1 us)
Async XLA Ops:
  1.5 16.0 %all-to-all-start = ((s32[32,1,512]{2,1,0:T(1,128)}), s32[32,1,512]{2,1,0:T(1,128)S(1)}, u32[]{:S(2)}, u32[]{:S(2)}) async-start(s32[32,1,512]{2,1,0:T(1,128)} %reshape.889), calls=%async_computation | async-start | bytes 131072 | tf_op jit(solution)/shard_map/all_to_all | solution.py:396
  17.5 8.5 %copy-start.4 = (s32[4,8]{1,0:T(4,128)S(1)}, s32[4,8]{1,0:T(4,128)}, u32[]{:S(2)}) copy-start(s32[4,8]{1,0:T(4,128)} %param.14) | copy-start | bytes 388
  17.5 8.7 %copy-start.5 = (s32[1,64]{1,0:T(1,128)S(1)}, s32[1,64]{1,0:T(1,128)}, u32[]{:S(2)}) copy-start(s32[1,64]{1,0:T(1,128)} %param.16) | copy-start | bytes 772
  17.5 8.9 %copy-start.1 = (s32[4,16]{1,0:T(4,128)S(1)}, s32[4,16]{1,0:T(4,128)}, u32[]{:S(2)}) copy-start(s32[4,16]{1,0:T(4,128)} %param.10) | copy-start | bytes 772
  17.5 11.0 %copy-start.6 = (f32[1032,128]{1,0:T(8,128)S(1)}, f32[1032,128]{1,0:T(8,128)}, u32[]{:S(2)}) copy-start(f32[1032,128]{1,0:T(8,128)} %get-tuple-element.32.p0) | copy-start | bytes 1585156
  17.5 16.8 %copy-start.10 = (s32[4]{0:T(128)S(1)}, s32[4]{0:T(128)}, u32[]{:S(2)}) copy-start(s32[4]{0:T(128)} %param.11) | copy-start | bytes 52
  17.5 59.3 %all-to-all-start.1 = ((f32[32,256,128]{2,1,0:T(8,128)}), f32[32,256,128]{2,1,0:T(8,128)}, u32[]{:S(2)}, u32[]{:S(2)}) async-start(f32[32,256,128]{2,1,0:T(8,128)} %get-tuple-element.30), calls=%async_computation.1 | async-start | bytes 8388608 | tf_op jit(solution)/shard_map/all_to_all | solution.py:392
  28.5 16.1 %collective-permute-start.2 = (f32[1032,128]{1,0:T(8,128)S(1)}, f32[1032,128]{1,0:T(8,128)S(1)}, u32[]{:S(2)}, u32[]{:S(2)}) collective-permute-start(f32[1032,128]{1,0:T(8,128)S(1)} %copy-done.6), channel_id=1, source_target_pairs={{96,0},{0,32},{32,64},{64,96},{97,1},{1,33},{33,65},{65,97},{98,2}... | collective-permute-start | bytes 1585160 | tf_op jit(solution)/shard_map/ppermute | solution.py:422
  30.2 26.6 %collective-permute-start.1 = (f32[1032,128]{1,0:T(8,128)S(1)}, f32[1032,128]{1,0:T(8,128)S(1)}, u32[]{:S(2)}, u32[]{:S(2)}) collective-permute-start(f32[1032,128]{1,0:T(8,128)S(1)} %copy-done.6), channel_id=1, source_target_pairs={{64,0},{96,32},{0,64},{32,96},{65,1},{97,33},{1,65},{33,97},{66,2}... | collective-permute-start | bytes 1585160 | tf_op jit(solution)/shard_map/ppermute | solution.py:422
  33.5 23.3 %collective-permute-start = (f32[1032,128]{1,0:T(8,128)S(1)}, f32[1032,128]{1,0:T(8,128)S(1)}, u32[]{:S(2)}, u32[]{:S(2)}) collective-permute-start(f32[1032,128]{1,0:T(8,128)S(1)} %copy-done.6), channel_id=1, source_target_pairs={{32,0},{64,32},{96,64},{0,96},{33,1},{65,33},{97,65},{1,97},{34,2}... | collective-permute-start | bytes 1585160 | tf_op jit(solution)/shard_map/ppermute | solution.py:422
  35.7 23.9 %copy-start.3 = (s32[48]{0:T(128)}, s32[48]{0:T(128)S(1)}, u32[]{:S(2)}) copy-start(s32[48]{0:T(128)S(1)} %reshape.887.cols_ref) | copy-start | bytes 580
  44.6 15.0 %copy-start.7 = (f32[1032,128]{1,0:T(8,128)}, f32[1032,128]{1,0:T(8,128)S(1)}, u32[]{:S(2)}) copy-start(f32[1032,128]{1,0:T(8,128)S(1)} %collective-permute-done.2.p3) | copy-start | bytes 1585156
  56.8 2.8 %copy-start.8 = (f32[1032,128]{1,0:T(8,128)}, f32[1032,128]{1,0:T(8,128)S(1)}, u32[]{:S(2)}) copy-start(f32[1032,128]{1,0:T(8,128)S(1)} %collective-permute-done.1.p2) | copy-start | bytes 1585156
  56.8 2.8 %copy-start.9 = (f32[1032,128]{1,0:T(8,128)}, f32[1032,128]{1,0:T(8,128)S(1)}, u32[]{:S(2)}) copy-start(f32[1032,128]{1,0:T(8,128)S(1)} %collective-permute-done.p1) | copy-start | bytes 1585156
  57.4 2.2 %copy-start.2 = (s32[32]{0:T(128)}, s32[32]{0:T(128)S(1)}, u32[]{:S(2)}) copy-start(s32[32]{0:T(128)S(1)} %convert_reduce_fusion.count_ref) | copy-start | bytes 388
  59.6 17.1 %copy-start = (f32[4,16,4096]{2,1,0:T(8,128)S(1)}, f32[4,16,4096]{2,1,0:T(8,128)}, u32[]{:S(2)}) copy-start(f32[4,16,4096]{2,1,0:T(8,128)} %a_ref.3) | copy-start | bytes 3145732
  91.2 26.9 %collective-permute-start.3 = (f32[8,512,128]{2,1,0:T(8,128)S(1)}, f32[8,512,128]{2,1,0:T(8,128)S(1)}, u32[]{:S(2)}, u32[]{:S(2)}) collective-permute-start(f32[8,512,128]{2,1,0:T(8,128)S(1)} %get-tuple-element.36), channel_id=1, source_target_pairs={{0,8},{1,3},{2,10},{3,5},{4,12},{5,7},{6,14},{7,1},{8,16},{9,11},{... | collective-permute-start | bytes 6291464 | tf_op jit(solution)/shard_map/ppermute | solution.py:441
  93.8 47.6 %collective-permute-start.4 = (f32[8,512,128]{2,1,0:T(8,128)S(1)}, f32[8,512,128]{2,1,0:T(8,128)S(1)}, u32[]{:S(2)}, u32[]{:S(2)}) collective-permute-start(f32[8,512,128]{2,1,0:T(8,128)S(1)} %get-tuple-element.37), channel_id=1, source_target_pairs={{0,16},{1,5},{2,18},{3,7},{4,20},{5,1},{6,22},{7,3},{8,24},{9,13},... | collective-permute-start | bytes 6291464 | tf_op jit(solution)/shard_map/ppermute | solution.py:441
  95.5 45.9 %collective-permute-start.5 = (f32[8,512,128]{2,1,0:T(8,128)S(1)}, f32[8,512,128]{2,1,0:T(8,128)S(1)}, u32[]{:S(2)}, u32[]{:S(2)}) collective-permute-start(f32[8,512,128]{2,1,0:T(8,128)S(1)} %get-tuple-element.38), channel_id=1, source_target_pairs={{0,24},{1,7},{2,26},{3,1},{4,28},{5,3},{6,30},{7,5},{8,0},{9,15},{... | collective-permute-start | bytes 6291464 | tf_op jit(solution)/shard_map/ppermute | solution.py:441
  142.4 14.0 %collective-permute-start.8 = (f32[2,2,512,128]{3,2,1,0:T(8,128)S(1)}, f32[2,2,512,128]{3,2,1,0:T(8,128)S(1)}, u32[]{:S(2)}, u32[]{:S(2)}) collective-permute-start(f32[2,2,512,128]{3,2,1,0:T(8,128)S(1)} %select_add_fusion), channel_id=1, source_target_pairs={{0,6},{1,25},{2,0},{3,27},{4,2},{5,29},{6,4},{7,31},{8,14},{9,1},{... | collective-permute-start | bytes 3145736 | tf_op jit(solution)/shard_map/ppermute | solution.py:460
  143.2 15.6 %collective-permute-start.7 = (f32[2,2,512,128]{3,2,1,0:T(8,128)S(1)}, f32[2,2,512,128]{3,2,1,0:T(8,128)S(1)}, u32[]{:S(2)}, u32[]{:S(2)}) collective-permute-start(f32[2,2,512,128]{3,2,1,0:T(8,128)S(1)} %select_add_fusion.1), channel_id=1, source_target_pairs={{0,4},{1,17},{2,6},{3,19},{4,0},{5,21},{6,2},{7,23},{8,12},{9,25},... | collective-permute-start | bytes 3145736 | tf_op jit(solution)/shard_map/ppermute | solution.py:460
  144.4 25.5 %collective-permute-start.6 = (f32[2,2,512,128]{3,2,1,0:T(8,128)S(1)}, f32[2,2,512,128]{3,2,1,0:T(8,128)S(1)}, u32[]{:S(2)}, u32[]{:S(2)}) collective-permute-start(f32[2,2,512,128]{3,2,1,0:T(8,128)S(1)} %select_add_fusion.2), channel_id=1, source_target_pairs={{0,2},{1,9},{2,4},{3,11},{4,6},{5,13},{6,0},{7,15},{8,10},{9,17},{... | collective-permute-start | bytes 3145736 | tf_op jit(solution)/shard_map/ppermute | solution.py:460
  170.2 4.9 %collective-permute-start.9 = (f32[2,512,128]{2,1,0:T(8,128)S(1)}, f32[2,512,128]{2,1,0:T(8,128)S(1)}, u32[]{:S(2)}, u32[]{:S(2)}) collective-permute-start(f32[2,512,128]{2,1,0:T(8,128)S(1)} %get-tuple-element.49), channel_id=1, source_target_pairs={{0,1},{1,0},{2,3},{3,2},{4,5},{5,4},{6,7},{7,6},{8,9},{9,8},{10,11... | collective-permute-start | bytes 1572872 | tf_op jit(solution)/shard_map/ppermute | solution.py:463

commit v3 on v2

--- a/solution.py
+++ b/solution.py
@@ -13,6 +13,8 @@
 KA = 16
 KP = 8
 KC = 16
+HALVES = 2
+HALF_C = KC // HALVES
 RB = 4
 PAIRS = RB * KP
 NEAR_E = KG * KP
@@ -166,7 +168,7 @@
         outs = []
         for t in range(2):
             j = jj * 2 + t
-            for s in range(KC // 2):
+            for s in range(HALF_C // 2):
                 hi, lo = split(m_ref[0, j, s])
                 cols = slice(s * LANES, (s + 1) * LANES)
                 wide_ref[t, 0:64, cols] = hi
@@ -174,7 +176,7 @@
             outs.append(jnp.dot(left_ref[0, j], wide_ref[t], preferred_element_type=jnp.float32))
         for t in range(2):
             pos = pos_ref[i * KP + jj * 2 + t]
-            for s in range(KC // 2):
+            for s in range(HALF_C // 2):
                 cols = slice(s * LANES, (s + 1) * LANES)
                 acc_ref[pos, s * BS : (s + 1) * BS, :] += outs[t][0:BS, cols] + outs[t][BS : 2 * BS, cols]
         return carry
@@ -193,11 +195,13 @@
             copy.wait()
 
 
-def final_kernel(mine_ref, got_ref, out_ref, spread_ref):
+def final_kernel(*refs):
+    *parts, out_ref, spread_ref = refs
     half = BS // 2
     first = first_half((half, LANES))
     for s in range(KC // 2):
-        even, odd = (pl.ds(s * BS + o, half, stride=2) for o in range(2))
+        mine_ref, got_ref = parts[2 * (s // (HALF_C // 2)) : 2 * (s // (HALF_C // 2)) + 2]
+        even, odd = (pl.ds(s % (HALF_C // 2) * BS + o, half, stride=2) for o in range(2))
         even = mine_ref[0, even, :] + got_ref[0, even, :]
         odd = mine_ref[0, odd, :] + got_ref[0, odd, :]
         spread_ref[2 * s * half : (2 * s + 1) * half, :] = jnp.where(first, even, pltpu.roll(odd, BS, axis=1))
@@ -248,7 +252,7 @@
 def match_lists(wanted, ids, live):
     n = ids.shape[1]
     eq = wanted[:, :, None] == ids[:, None, :]
-    c_of = jnp.sum(jnp.where(eq, jnp.arange(KC, dtype=jnp.int32)[None, :, None], 0), axis=1)
+    c_of = jnp.sum(jnp.where(eq, jnp.arange(wanted.shape[1], dtype=jnp.int32)[None, :, None], 0), axis=1)
     hit = jnp.any(eq, axis=1) & live
     number = jnp.arange(n, dtype=jnp.int32)
     before = jnp.sum(jnp.where((number[:, None] < number[None, :])[None], hit[:, :, None].astype(jnp.int32), 0), axis=1)
@@ -294,9 +298,9 @@
     )(cols, lists, counts, operator_blocks, *near_rows)
 
 
-def far_call(cols, lists, counts, position, operator_blocks, far_rows, matched, left, n_dom):
+def far_call(half, cols, lists, counts, position, operator_blocks, far_rows, matched, left, n_dom):
     far_spec = lambda m: pl.BlockSpec((1, ROW_T, LANES), lambda i, cols, *_: (cols[i * KH + m], 0, 0))
-    slot_shape = (KC // 2 * BS, LANES)
+    slot_shape = (HALF_C // 2 * BS, LANES)
     hbm = lambda x: pltpu.with_memory_space_constraint(x, pltpu.HBM)
     return pl.pallas_call(
         far_kernel,
@@ -307,21 +311,21 @@
             in_specs=[pl.BlockSpec((1, 8, BS * BS), lambda i, *_: (i, 1, 0))]
             + [far_spec(m) for m in range(KH)]
             + [
-                pl.BlockSpec((1, KP, KC // 2, BS, LANES), lambda i, *_: (i, 0, 0, 0, 0)),
+                pl.BlockSpec((1, KP, HALF_C // 2, BS, LANES), lambda i, *_: (i, 0, half, 0, 0)),
                 pl.BlockSpec((1, KP, LANES, LANES), lambda i, *_: (i, 0, 0, 0)),
             ],
             out_specs=(pl.BlockSpec(memory_space=pltpu.HBM),) * 5,
             scratch_shapes=[
                 pltpu.VMEM((KH, 256, KP * BS), jnp.bfloat16),
                 pltpu.VMEM((2, FAR_E // 2 + 1, BS, LANES), jnp.float32),
-                pltpu.VMEM((2, LANES, KC * BS), jnp.bfloat16),
+                pltpu.VMEM((2, LANES, HALF_C * BS), jnp.bfloat16),
                 pltpu.VMEM((n_dom + 1,) + slot_shape, jnp.float32),
                 pltpu.VMEM((8 * BS // 2, LANES), jnp.float32),
                 pltpu.SemaphoreType.DMA((5,)),
             ],
         ),
         compiler_params=pltpu.CompilerParams(vmem_limit_bytes=40 * 2**20),
-        cost_estimate=pl.CostEstimate(flops=10**10, bytes_accessed=24 * 2**20, transcendentals=0),
+        cost_estimate=pl.CostEstimate(flops=5 * 10**9, bytes_accessed=14 * 2**20, transcendentals=0),
         name="far",
     )(cols, lists, counts, position, operator_blocks, *([far_rows] * KH), hbm(matched), hbm(left))
 
@@ -432,47 +436,63 @@
     live = jnp.arange(KH, dtype=jnp.int32)[None, :] < halo_count[:, None]
     spread = lambda x: jnp.repeat(x, KP, axis=0)
     near_list, near_count = match_lists(wanted, spread(near_ids), jnp.ones((PAIRS, NEAR_E), bool))
-    far_list, far_count = match_lists(wanted, spread(far_ids), spread(jnp.repeat(live, KP, axis=1)))
+    far_live = spread(jnp.repeat(live, KP, axis=1))
+    far_lists = [
+        match_lists(wanted[:, half * HALF_C : (half + 1) * HALF_C], spread(far_ids), far_live) for half in range(HALVES)
+    ]
 
     matched, left = near_call(near_cols, near_list, near_count, operator_blocks, near_rows)
-    chunks = far_call(far_cols, far_list, far_count, position, operator_blocks, far_rows, matched, left, n_dom)
-    slot_shape = (KC // 2 * BS, LANES)
-
-    sent = {t: lax.ppermute(chunks[t], "dom", shift_pairs(t, 0)) for t in (2, 1, 3)}
-    *arriving, own_second = lax.optimization_barrier((chunks[0], sent[1], sent[2], sent[3], chunks[4]))
+    slot_shape = (HALF_C // 2 * BS, LANES)
     sources = jnp.stack([device_at(u - t, v, k, d) for t in range(SIDE)])
     owners = jnp.stack([device_at(u, v + p // 2, k + p % 2, d) for p in range(8)])
     rows_from = pick_rows(slot_rows, sources)
     row_of = pick_rows(rows_from.T, 2 * owners).T
-    own_first = row_of[0, 0]
-
-    def owned(t2):
-        total = 0.0
-        for t in range(SIDE):
-            part = arriving[t][2 * t2 : 2 * t2 + 2][:, None]
-            to_row = row_of[t, 2 * t2 : 2 * t2 + 2][:, None] == jnp.arange(2, dtype=jnp.int32)
-            total = total + jnp.where(to_row[:, :, None, None], part, 0.0)
-        if t2 == 0:
-            to_row = (jnp.arange(2, dtype=jnp.int32) == 1 - own_first)[None] & (jnp.arange(2) == 0)[:, None]
-            total = total + jnp.where(to_row[:, :, None, None], own_second[:, None], 0.0)
-        return total
-
-    sent = {t2: lax.ppermute(owned(t2), "dom", shift_pairs(t2, 1)) for t2 in (2, 1, 3)}
-    kept = owned(0)
-    sums = [kept[kk] + sent[1][kk] + sent[2][kk] + sent[3][kk] for kk in (1, 0)]
-    swapped = lax.ppermute(sums[0], "dom", [(n, n ^ 1) for n in range(n_dom)])
+    two = jnp.arange(2, dtype=jnp.int32)
+    second_row = (two == 1 - row_of[0, 0])[None] & (two == 0)[:, None]
+
+    def first_phase(half):
+        far_list, far_count = far_lists[half]
+        chunks = far_call(
+            half, far_cols, far_list, far_count, position, operator_blocks, far_rows, matched, left, n_dom
+        )
+        sent = {t: lax.ppermute(chunks[t], "dom", shift_pairs(t, 0)) for t in (2, 1, 3)}
+        return lax.optimization_barrier((chunks[0], sent[1], sent[2], sent[3], chunks[4]))
+
+    def second_phase(here):
+        *arriving, second = here
+
+        def owned(t2):
+            total = 0.0
+            for t in range(SIDE):
+                part = arriving[t][2 * t2 : 2 * t2 + 2][:, None]
+                to_row = row_of[t, 2 * t2 : 2 * t2 + 2][:, None] == two
+                total = total + jnp.where(to_row[:, :, None, None], part, 0.0)
+            if t2 == 0:
+                total = total + jnp.where(second_row[:, :, None, None], second[:, None], 0.0)
+            return total
+
+        sent = [lax.ppermute(owned(t2), "dom", shift_pairs(t2, 1)) for t2 in (2, 1, 3)]
+        return owned(0), sent
+
+    def swap(kept, sent):
+        sums = [kept[kk] + sent[1][kk] + sent[0][kk] + sent[2][kk] for kk in (1, 0)]
+        return sums[1], lax.ppermute(sums[0], "dom", [(n, n ^ 1) for n in range(n_dom)])
+
+    arrived = [first_phase(half) for half in range(HALVES)]
+    halves = [second_phase(here) for here in arrived]
+    parts = [swap(*half) for half in halves]
 
     row_spec = pl.BlockSpec((1,) + slot_shape, lambda i: (i, 0, 0))
     return pl.pallas_call(
         final_kernel,
         out_shape=jax.ShapeDtypeStruct((2, KC, BS * BS), jnp.float32),
         grid=(2,),
-        in_specs=[row_spec, row_spec],
+        in_specs=[row_spec] * (2 * HALVES),
         out_specs=pl.BlockSpec((1, KC, BS * BS), lambda i: (i, 0, 0)),
         scratch_shapes=[pltpu.VMEM((KC * BS // 2, LANES), jnp.float32)],
         compiler_params=pltpu.CompilerParams(vmem_limit_bytes=16 * 2**20),
         name="final",
-    )(sums[1], swapped)
+    )(*[x for pair in parts for x in pair])
 
 
 def solution(mesh):

time: 177 us -> 174 us (0.983)
  waiting for transfers between devices: 95.5 us -> 72.2 us
  starting transfers between devices: 31.8 us -> 42.8 us
  Pallas kernels: 33.3 us -> 41.5 us
    ppermute x7 -> x14, waiting for transfers between devices: 68.9 us -> 47.3 us  [the longest x6 28.8 us: first_phase(): lax.ppermute(chunks[t], 'dom', shift_pairs(t, 0))]
    ppermute x7 -> x14, starting transfers between devices: 10.5 us -> 21.4 us  [the longest x6 8.3 us: first_phase(): lax.ppermute(chunks[t], 'dom', shift_pairs(t, 0))]
    pallas_call x1 -> x2, Pallas kernels: 14.4 us -> 22.4 us  [far_call(): pl.pallas_call(far_kernel, out_shape=tuple((jax.ShapeDtypeStruct((n,) + s...]
  transfers between devices with their start and end apart: 12 -> 19, of which waited for: 10 -> 13; matrix products, arithmetic and copies ran while one was open for 7% -> 7% of each run, Pallas kernels for 10% -> 17%
where the time goes in v3:
time: 174 us; the launch traced here: 173 us
  waiting for transfers between devices  72.2 us (41%)
  starting transfers between devices  42.8 us (25%)
  Pallas kernels  41.5 us (24%)
  other arithmetic  10.9 us (6%)
  local copies, waits for them, and re-layouts  4.62 us (3%)
    ppermute x6, waiting for transfers between devices, first_phase(): lax.ppermute(chunks[t], 'dom', shift_pairs(t, 0))  28.8 us
    pallas_call x2, Pallas kernels, far_call(): pl.pallas_call(far_kernel, out_shape=tuple((jax.ShapeDtypeStruct((n,) + s...  22.4 us
    ppermute x3, waiting for transfers between devices, per_device(): lax.ppermute(passed, 'grp', [((z + dz) % n_grp, z) for z in range(n_grp)])  19.8 us
    ppermute x6, waiting for transfers between devices, second_phase(): lax.ppermute(owned(t2), 'dom', shift_pairs(t2, 1))  17.3 us
    pallas_call x1, Pallas kernels, near_call(): pl.pallas_call(near_kernel, out_shape=(jax.ShapeDtypeStruct((RB, KP, KC /...  12.4 us
    all_to_all x1, starting transfers between devices, per_device(): lax.all_to_all(jnp.broadcast_to(mine[None], (n_dom,) + mine.shape), 'dom'...  8.59 us
    ppermute x6, starting transfers between devices, first_phase(): lax.ppermute(chunks[t], 'dom', shift_pairs(t, 0))  8.3 us
    ppermute x2, starting transfers between devices, swap(): lax.ppermute(sums[0], 'dom', [(n, n ^ 1) for n in range(n_dom)])  7.76 us
  transfers between devices with their start and end apart: 19, of which 13 were waited for; matrix products, arithmetic and copies ran while one was open for 7% of the time, Pallas kernels for 17%

profile of v3, /device:TPU:1, one launch (start us, length us, event | category | flops | bytes accessed | tf_op | source)
XLA Modules:
  0.0 173.4 jit_solution(11562074013995076441)
XLA Ops:
  0.0 0.7 fusion.13
  0.7 0.8 reshape.964
  1.5 8.6 %all-to-all-start = ((s32[32,1,512]{2,1,0:T(1,128)}), s32[32,1,512]{2,1,0:T(1,128)S(1)}, u32[]{:S(2)}, u32[]{:S(2)}) async-start(s32[32,1,512]{2,1,0:T(1,128)} %reshape.964), calls=%async_computation | async-start | bytes 131072 | tf_op jit(solution)/shard_map/all_to_all | solution.py:400
  10.8 5.5 %outgoing.1 = (f32[32,256,128]{2,1,0:T(8,128)}, f32[1032,128]{1,0:T(8,128)}) custom-call(s32[32]{0:T(128)} %bitcast.78, f32[4,8,4096]{2,1,0:T(8,128)} %blocks_ref.1, s32[4,8]{1,0:T(4,128)} %ids_ref.1), custom_call_target="tpu_custom_call" | custom-call | bytes 6291456 | tf_op jit(solution)/shard_map/outgoing/pallas_call | solution.py:374
  16.3 0.7 slice_convert_fusion.3
  17.0 0.5 all-to-all-done
  17.5 7.1 %all-to-all-start.1 = ((f32[32,256,128]{2,1,0:T(8,128)}), f32[32,256,128]{2,1,0:T(8,128)}, u32[]{:S(2)}, u32[]{:S(2)}) async-start(f32[32,256,128]{2,1,0:T(8,128)} %get-tuple-element.40), calls=%async_computation.1 | async-start | bytes 8388608 | tf_op jit(solution)/shard_map/all_to_all | solution.py:396
  24.6 0.5 broadcast.621
  25.1 0.8 reduce.9
  26.8 0.6 select_reduce_fusion.6
  28.7 1.7 collective-permute-start.2
  30.4 3.3 %collective-permute-start.1 = (f32[1032,128]{1,0:T(8,128)S(1)}, f32[1032,128]{1,0:T(8,128)S(1)}, u32[]{:S(2)}, u32[]{:S(2)}) collective-permute-start(f32[1032,128]{1,0:T(8,128)S(1)} %copy-done.6), channel_id=1, source_target_pairs={{64,0},{96,32},{0,64},{32,96},{65,1},{97,33},{1,65},{33,97},{66,2}... | collective-permute-start | bytes 1585160 | tf_op jit(solution)/shard_map/ppermute | solution.py:426
  33.7 0.7 collective-permute-start
  35.4 0.6 select_reduce_fusion.4
  36.1 0.6 select_reduce_fusion.2
  37.2 7.6 %collective-permute-done.2.p3 = f32[1032,128]{1,0:T(8,128)S(1)} collective-permute-done((f32[1032,128]{1,0:T(8,128)S(1)}, f32[1032,128]{1,0:T(8,128)S(1)}, u32[]{:S(2)}, u32[]{:S(2)}) %collective-permute-start.2) | collective-permute-done | bytes 528416 | tf_op jit(solution)/shard_map/ppermute | solution.py:426
  44.8 12.2 %collective-permute-done.1.p2 = f32[1032,128]{1,0:T(8,128)S(1)} collective-permute-done((f32[1032,128]{1,0:T(8,128)S(1)}, f32[1032,128]{1,0:T(8,128)S(1)}, u32[]{:S(2)}, u32[]{:S(2)}) %collective-permute-start.1) | collective-permute-done | bytes 528416 | tf_op jit(solution)/shard_map/ppermute | solution.py:426
  57.7 0.6 select_reduce_fusion.1
  58.3 0.6 select_reduce_fusion
  59.1 0.7 select_n.560.list_ref
  59.8 12.4 %near.1 = (f32[4,8,8,64,128]{4,3,2,1,0:T(8,128)}, bf16[4,8,128,128]{3,2,1,0:T(8,128)(2,1)}) custom-call(s32[48]{0:T(128)} %copy-done.3, s32[3072]{0:T(1024)} %select_n.560.list_ref, s32[32]{0:T(128)} %copy-done.2, f32[4,16,4096]{2,1,0:T(8,128)} %a_ref.5, f32[1032,128]{1,0:T(8,128)} %get-tuple-element.42.p0, f32[1032,128]{1,0:T(8,128)} %copy-done.9, ...), custom_call_target="tpu_custom_call" | custom-call | flops 10000000000 | bytes 16777216 | tf_op jit(solution)/shard_map/near/pallas_call | solution.py:275
  72.1 4.7 %all-to-all-done.1.f0.f1.f2.f3 = f32[32,256,128]{2,1,0:T(8,128)} async-done(((f32[32,256,128]{2,1,0:T(8,128)}), f32[32,256,128]{2,1,0:T(8,128)}, u32[]{:S(2)}, u32[]{:S(2)}) %all-to-all-start.1) | async-done | bytes 4194336 | tf_op jit(solution)/shard_map/all_to_all | solution.py:396
  76.8 10.9 %far.3 = (f32[8,256,128]{2,1,0:T(8,128)S(1)}, f32[8,256,128]{2,1,0:T(8,128)S(1)}, f32[8,256,128]{2,1,0:T(8,128)S(1)}, f32[8,256,128]{2,1,0:T(8,128)S(1)}, f32[1,256,128]{2,1,0:T(8,128)S(1)}) custom-call(s32[16]{0:T(128)S(1)} %reshape.957.cols_ref, s32[1024]{0:T(1024)S(1)} %select_n.582.list_ref, s32[32]{0:T(128)S(1)} %get-tuple-element.143.count_ref, ...), custom_call_target="tpu_custom_call" | custom-call | flops 5000000000 | bytes 14680064 | tf_op jit(solution)/shard_map/far/pallas_call | solution.py:305
  87.8 3.1 %collective-permute-start.10 = (f32[8,256,128]{2,1,0:T(8,128)S(1)}, f32[8,256,128]{2,1,0:T(8,128)S(1)}, u32[]{:S(2)}, u32[]{:S(2)}) collective-permute-start(f32[8,256,128]{2,1,0:T(8,128)S(1)} %get-tuple-element.56), channel_id=1, source_target_pairs={{0,8},{1,3},{2,10},{3,5},{4,12},{5,7},{6,14},{7,1},{8,16},{9,11},{... | collective-permute-start | bytes 3145736 | tf_op jit(solution)/shard_map/ppermute | solution.py:458
  91.1 1.3 collective-permute-start.11
  92.4 1.1 collective-permute-start.12
  93.5 11.5 %far.2 = (f32[8,256,128]{2,1,0:T(8,128)S(1)}, f32[8,256,128]{2,1,0:T(8,128)S(1)}, f32[8,256,128]{2,1,0:T(8,128)S(1)}, f32[8,256,128]{2,1,0:T(8,128)S(1)}, f32[1,256,128]{2,1,0:T(8,128)S(1)}) custom-call(s32[16]{0:T(128)S(1)} %reshape.957.cols_ref, s32[1024]{0:T(1024)S(1)} %select_n.539.list_ref, s32[32]{0:T(128)S(1)} %get-tuple-element.75.count_ref, ...), custom_call_target="tpu_custom_call" | custom-call | flops 5000000000 | bytes 14680064 | tf_op jit(solution)/shard_map/far/pallas_call | solution.py:305
  105.1 1.7 collective-permute-start.4
  106.8 1.0 collective-permute-start.5
  107.8 0.5 slice.266
  109.3 6.4 %collective-permute-done.11 = f32[8,256,128]{2,1,0:T(8,128)S(1)} collective-permute-done((f32[8,256,128]{2,1,0:T(8,128)S(1)}, f32[8,256,128]{2,1,0:T(8,128)S(1)}, u32[]{:S(2)}, u32[]{:S(2)}) %collective-permute-start.11) | collective-permute-done | bytes 1048608 | tf_op jit(solution)/shard_map/ppermute | solution.py:458
  115.7 11.4 %collective-permute-done.3 = f32[8,256,128]{2,1,0:T(8,128)S(1)} collective-permute-done((f32[8,256,128]{2,1,0:T(8,128)S(1)}, f32[8,256,128]{2,1,0:T(8,128)S(1)}, u32[]{:S(2)}, u32[]{:S(2)}) %collective-permute-start.3) | collective-permute-done | bytes 1048608 | tf_op jit(solution)/shard_map/ppermute | solution.py:458
  127.1 11.0 %collective-permute-done.4 = f32[8,256,128]{2,1,0:T(8,128)S(1)} collective-permute-done((f32[8,256,128]{2,1,0:T(8,128)S(1)}, f32[8,256,128]{2,1,0:T(8,128)S(1)}, u32[]{:S(2)}, u32[]{:S(2)}) %collective-permute-start.4) | collective-permute-done | bytes 1048608 | tf_op jit(solution)/shard_map/ppermute | solution.py:458
  139.2 0.7 collective-permute-start.15
  140.2 0.8 collective-permute-start.14
  141.3 0.7 collective-permute-start.13
  142.1 2.1 %collective-permute-start.8 = (f32[2,2,256,128]{3,2,1,0:T(8,128)S(1)}, f32[2,2,256,128]{3,2,1,0:T(8,128)S(1)}, u32[]{:S(2)}, u32[]{:S(2)}) collective-permute-start(f32[2,2,256,128]{3,2,1,0:T(8,128)S(1)} %get-tuple-element.124), channel_id=1, source_target_pairs={{0,6},{1,25},{2,0},{3,27},{4,2},{5,29},{6,4},{7,31},{8,14},{9,1},{... | collective-permute-start | bytes 1572872 | tf_op jit(solution)/shard_map/ppermute | solution.py:474
  144.1 1.1 collective-permute-start.7
  145.2 2.4 %collective-permute-done.15 = f32[2,2,256,128]{3,2,1,0:T(8,128)S(1)} collective-permute-done((f32[2,2,256,128]{3,2,1,0:T(8,128)S(1)}, f32[2,2,256,128]{3,2,1,0:T(8,128)S(1)}, u32[]{:S(2)}, u32[]{:S(2)}) %collective-permute-start.15) | collective-permute-done | bytes 524320 | tf_op jit(solution)/shard_map/ppermute | solution.py:474
  147.6 0.4 select_add_fusion.3
  148.0 2.2 %collective-permute-done.14 = f32[2,2,256,128]{3,2,1,0:T(8,128)S(1)} collective-permute-done((f32[2,2,256,128]{3,2,1,0:T(8,128)S(1)}, f32[2,2,256,128]{3,2,1,0:T(8,128)S(1)}, u32[]{:S(2)}, u32[]{:S(2)}) %collective-permute-start.14) | collective-permute-done | bytes 524320 | tf_op jit(solution)/shard_map/ppermute | solution.py:474
  150.1 5.6 %collective-permute-done.13 = f32[2,2,256,128]{3,2,1,0:T(8,128)S(1)} collective-permute-done((f32[2,2,256,128]{3,2,1,0:T(8,128)S(1)}, f32[2,2,256,128]{3,2,1,0:T(8,128)S(1)}, u32[]{:S(2)}, u32[]{:S(2)}) %collective-permute-start.13) | collective-permute-done | bytes 524320 | tf_op jit(solution)/shard_map/ppermute | solution.py:474
  155.9 3.9 %collective-permute-start.16 = (f32[2,256,128]{2,1,0:T(8,128)S(1)}, f32[2,256,128]{2,1,0:T(8,128)S(1)}, u32[]{:S(2)}, u32[]{:S(2)}) collective-permute-start(f32[2,256,128]{2,1,0:T(8,128)S(1)} %get-tuple-element.77), channel_id=1, source_target_pairs={{0,1},{1,0},{2,3},{3,2},{4,5},{5,4},{6,7},{7,6},{8,9},{9,8},{10,11... | collective-permute-start | bytes 786440 | tf_op jit(solution)/shard_map/ppermute | solution.py:479
  159.7 1.7 collective-permute-done.7
  161.4 5.5 %collective-permute-done.6 = f32[2,2,256,128]{3,2,1,0:T(8,128)S(1)} collective-permute-done((f32[2,2,256,128]{3,2,1,0:T(8,128)S(1)}, f32[2,2,256,128]{3,2,1,0:T(8,128)S(1)}, u32[]{:S(2)}, u32[]{:S(2)}) %collective-permute-start.6) | collective-permute-done | bytes 524320 | tf_op jit(solution)/shard_map/ppermute | solution.py:474
  167.1 3.9 %collective-permute-start.9 = (f32[2,256,128]{2,1,0:T(8,128)S(1)}, f32[2,256,128]{2,1,0:T(8,128)S(1)}, u32[]{:S(2)}, u32[]{:S(2)}) collective-permute-start(f32[2,256,128]{2,1,0:T(8,128)S(1)} %get-tuple-element.79), channel_id=1, source_target_pairs={{0,1},{1,0},{2,3},{3,2},{4,5},{5,4},{6,7},{7,6},{8,9},{9,8},{10,11... | collective-permute-start | bytes 786440 | tf_op jit(solution)/shard_map/ppermute | solution.py:479
  171.0 1.2 collective-permute-done.9.refs_1_
  172.1 1.3 final.1
  (114 shorter events, 7.4 us)
Async XLA Ops:
  1.5 16.0 %all-to-all-start = ((s32[32,1,512]{2,1,0:T(1,128)}), s32[32,1,512]{2,1,0:T(1,128)S(1)}, u32[]{:S(2)}, u32[]{:S(2)}) async-start(s32[32,1,512]{2,1,0:T(1,128)} %reshape.964), calls=%async_computation | async-start | bytes 131072 | tf_op jit(solution)/shard_map/all_to_all | solution.py:400
  17.5 8.6 %copy-start.4 = (s32[4,8]{1,0:T(4,128)S(1)}, s32[4,8]{1,0:T(4,128)}, u32[]{:S(2)}) copy-start(s32[4,8]{1,0:T(4,128)} %param.14) | copy-start | bytes 388
  17.5 8.7 %copy-start.5 = (s32[1,64]{1,0:T(1,128)S(1)}, s32[1,64]{1,0:T(1,128)}, u32[]{:S(2)}) copy-start(s32[1,64]{1,0:T(1,128)} %param.16) | copy-start | bytes 772
  17.5 8.9 %copy-start.1 = (s32[4,16]{1,0:T(4,128)S(1)}, s32[4,16]{1,0:T(4,128)}, u32[]{:S(2)}) copy-start(s32[4,16]{1,0:T(4,128)} %param.10) | copy-start | bytes 772
  17.5 11.2 %copy-start.6 = (f32[1032,128]{1,0:T(8,128)S(1)}, f32[1032,128]{1,0:T(8,128)}, u32[]{:S(2)}) copy-start(f32[1032,128]{1,0:T(8,128)} %get-tuple-element.42.p0) | copy-start | bytes 1585156
  17.5 16.9 %copy-start.10 = (s32[4]{0:T(128)S(1)}, s32[4]{0:T(128)}, u32[]{:S(2)}) copy-start(s32[4]{0:T(128)} %param.11) | copy-start | bytes 52
  17.5 59.3 %all-to-all-start.1 = ((f32[32,256,128]{2,1,0:T(8,128)}), f32[32,256,128]{2,1,0:T(8,128)}, u32[]{:S(2)}, u32[]{:S(2)}) async-start(f32[32,256,128]{2,1,0:T(8,128)} %get-tuple-element.40), calls=%async_computation.1 | async-start | bytes 8388608 | tf_op jit(solution)/shard_map/all_to_all | solution.py:396
  28.7 16.1 %collective-permute-start.2 = (f32[1032,128]{1,0:T(8,128)S(1)}, f32[1032,128]{1,0:T(8,128)S(1)}, u32[]{:S(2)}, u32[]{:S(2)}) collective-permute-start(f32[1032,128]{1,0:T(8,128)S(1)} %copy-done.6), channel_id=1, source_target_pairs={{96,0},{0,32},{32,64},{64,96},{97,1},{1,33},{33,65},{65,97},{98,2}... | collective-permute-start | bytes 1585160 | tf_op jit(solution)/shard_map/ppermute | solution.py:426
  30.4 26.6 %collective-permute-start.1 = (f32[1032,128]{1,0:T(8,128)S(1)}, f32[1032,128]{1,0:T(8,128)S(1)}, u32[]{:S(2)}, u32[]{:S(2)}) collective-permute-start(f32[1032,128]{1,0:T(8,128)S(1)} %copy-done.6), channel_id=1, source_target_pairs={{64,0},{96,32},{0,64},{32,96},{65,1},{97,33},{1,65},{33,97},{66,2}... | collective-permute-start | bytes 1585160 | tf_op jit(solution)/shard_map/ppermute | solution.py:426
  33.7 23.3 %collective-permute-start = (f32[1032,128]{1,0:T(8,128)S(1)}, f32[1032,128]{1,0:T(8,128)S(1)}, u32[]{:S(2)}, u32[]{:S(2)}) collective-permute-start(f32[1032,128]{1,0:T(8,128)S(1)} %copy-done.6), channel_id=1, source_target_pairs={{32,0},{64,32},{96,64},{0,96},{33,1},{65,33},{97,65},{1,97},{34,2}... | collective-permute-start | bytes 1585160 | tf_op jit(solution)/shard_map/ppermute | solution.py:426
  37.0 22.7 %copy-start.3 = (s32[48]{0:T(128)}, s32[48]{0:T(128)S(1)}, u32[]{:S(2)}) copy-start(s32[48]{0:T(128)S(1)} %reshape.962.cols_ref) | copy-start | bytes 580
  44.8 15.0 %copy-start.7 = (f32[1032,128]{1,0:T(8,128)}, f32[1032,128]{1,0:T(8,128)S(1)}, u32[]{:S(2)}) copy-start(f32[1032,128]{1,0:T(8,128)S(1)} %collective-permute-done.2.p3) | copy-start | bytes 1585156
  56.9 2.8 %copy-start.8 = (f32[1032,128]{1,0:T(8,128)}, f32[1032,128]{1,0:T(8,128)S(1)}, u32[]{:S(2)}) copy-start(f32[1032,128]{1,0:T(8,128)S(1)} %collective-permute-done.1.p2) | copy-start | bytes 1585156
  56.9 2.8 %copy-start.9 = (f32[1032,128]{1,0:T(8,128)}, f32[1032,128]{1,0:T(8,128)S(1)}, u32[]{:S(2)}) copy-start(f32[1032,128]{1,0:T(8,128)S(1)} %collective-permute-done.p1) | copy-start | bytes 1585156
  57.5 2.2 %copy-start.2 = (s32[32]{0:T(128)}, s32[32]{0:T(128)S(1)}, u32[]{:S(2)}) copy-start(s32[32]{0:T(128)S(1)} %convert_reduce_fusion.1.count_ref) | copy-start | bytes 388
  59.8 17.1 %copy-start = (f32[4,16,4096]{2,1,0:T(8,128)S(1)}, f32[4,16,4096]{2,1,0:T(8,128)}, u32[]{:S(2)}) copy-start(f32[4,16,4096]{2,1,0:T(8,128)} %a_ref.5) | copy-start | bytes 3145732
  87.8 19.0 %collective-permute-start.10 = (f32[8,256,128]{2,1,0:T(8,128)S(1)}, f32[8,256,128]{2,1,0:T(8,128)S(1)}, u32[]{:S(2)}, u32[]{:S(2)}) collective-permute-start(f32[8,256,128]{2,1,0:T(8,128)S(1)} %get-tuple-element.56), channel_id=1, source_target_pairs={{0,8},{1,3},{2,10},{3,5},{4,12},{5,7},{6,14},{7,1},{8,16},{9,11},{... | collective-permute-start | bytes 3145736 | tf_op jit(solution)/shard_map/ppermute | solution.py:458
  91.1 24.6 %collective-permute-start.11 = (f32[8,256,128]{2,1,0:T(8,128)S(1)}, f32[8,256,128]{2,1,0:T(8,128)S(1)}, u32[]{:S(2)}, u32[]{:S(2)}) collective-permute-start(f32[8,256,128]{2,1,0:T(8,128)S(1)} %get-tuple-element.57), channel_id=1, source_target_pairs={{0,16},{1,5},{2,18},{3,7},{4,20},{5,1},{6,22},{7,3},{8,24},{9,13},... | collective-permute-start | bytes 3145736 | tf_op jit(solution)/shard_map/ppermute | solution.py:458
  92.4 23.3 %collective-permute-start.12 = (f32[8,256,128]{2,1,0:T(8,128)S(1)}, f32[8,256,128]{2,1,0:T(8,128)S(1)}, u32[]{:S(2)}, u32[]{:S(2)}) collective-permute-start(f32[8,256,128]{2,1,0:T(8,128)S(1)} %get-tuple-element.58), channel_id=1, source_target_pairs={{0,24},{1,7},{2,26},{3,1},{4,28},{5,3},{6,30},{7,5},{8,0},{9,15},{... | collective-permute-start | bytes 3145736 | tf_op jit(solution)/shard_map/ppermute | solution.py:458
  105.0 22.1 %collective-permute-start.3 = (f32[8,256,128]{2,1,0:T(8,128)S(1)}, f32[8,256,128]{2,1,0:T(8,128)S(1)}, u32[]{:S(2)}, u32[]{:S(2)}) collective-permute-start(f32[8,256,128]{2,1,0:T(8,128)S(1)} %get-tuple-element.46), channel_id=1, source_target_pairs={{0,8},{1,3},{2,10},{3,5},{4,12},{5,7},{6,14},{7,1},{8,16},{9,11},{... | collective-permute-start | bytes 3145736 | tf_op jit(solution)/shard_map/ppermute | solution.py:458
  105.1 33.0 %collective-permute-start.4 = (f32[8,256,128]{2,1,0:T(8,128)S(1)}, f32[8,256,128]{2,1,0:T(8,128)S(1)}, u32[]{:S(2)}, u32[]{:S(2)}) collective-permute-start(f32[8,256,128]{2,1,0:T(8,128)S(1)} %get-tuple-element.47), channel_id=1, source_target_pairs={{0,16},{1,5},{2,18},{3,7},{4,20},{5,1},{6,22},{7,3},{8,24},{9,13},... | collective-permute-start | bytes 3145736 | tf_op jit(solution)/shard_map/ppermute | solution.py:458
  106.8 31.3 %collective-permute-start.5 = (f32[8,256,128]{2,1,0:T(8,128)S(1)}, f32[8,256,128]{2,1,0:T(8,128)S(1)}, u32[]{:S(2)}, u32[]{:S(2)}) collective-permute-start(f32[8,256,128]{2,1,0:T(8,128)S(1)} %get-tuple-element.48), channel_id=1, source_target_pairs={{0,24},{1,7},{2,26},{3,1},{4,28},{5,3},{6,30},{7,5},{8,0},{9,15},{... | collective-permute-start | bytes 3145736 | tf_op jit(solution)/shard_map/ppermute | solution.py:458
  139.2 8.4 %collective-permute-start.15 = (f32[2,2,256,128]{3,2,1,0:T(8,128)S(1)}, f32[2,2,256,128]{3,2,1,0:T(8,128)S(1)}, u32[]{:S(2)}, u32[]{:S(2)}) collective-permute-start(f32[2,2,256,128]{3,2,1,0:T(8,128)S(1)} %get-tuple-element.123), channel_id=1, source_target_pairs={{0,6},{1,25},{2,0},{3,27},{4,2},{5,29},{6,4},{7,31},{8,14},{9,1},{... | collective-permute-start | bytes 1572872 | tf_op jit(solution)/shard_map/ppermute | solution.py:474
  140.2 10.0 %collective-permute-start.14 = (f32[2,2,256,128]{3,2,1,0:T(8,128)S(1)}, f32[2,2,256,128]{3,2,1,0:T(8,128)S(1)}, u32[]{:S(2)}, u32[]{:S(2)}) collective-permute-start(f32[2,2,256,128]{3,2,1,0:T(8,128)S(1)} %get-tuple-element.121), channel_id=1, source_target_pairs={{0,4},{1,17},{2,6},{3,19},{4,0},{5,21},{6,2},{7,23},{8,12},{9,25},... | collective-permute-start | bytes 1572872 | tf_op jit(solution)/shard_map/ppermute | solution.py:474
  141.3 14.4 %collective-permute-start.13 = (f32[2,2,256,128]{3,2,1,0:T(8,128)S(1)}, f32[2,2,256,128]{3,2,1,0:T(8,128)S(1)}, u32[]{:S(2)}, u32[]{:S(2)}) collective-permute-start(f32[2,2,256,128]{3,2,1,0:T(8,128)S(1)} %get-tuple-element.119), channel_id=1, source_target_pairs={{0,2},{1,9},{2,4},{3,11},{4,6},{5,13},{6,0},{7,15},{8,10},{9,17},{... | collective-permute-start | bytes 1572872 | tf_op jit(solution)/shard_map/ppermute | solution.py:474
  142.1 17.7 %collective-permute-start.8 = (f32[2,2,256,128]{3,2,1,0:T(8,128)S(1)}, f32[2,2,256,128]{3,2,1,0:T(8,128)S(1)}, u32[]{:S(2)}, u32[]{:S(2)}) collective-permute-start(f32[2,2,256,128]{3,2,1,0:T(8,128)S(1)} %get-tuple-element.124), channel_id=1, source_target_pairs={{0,6},{1,25},{2,0},{3,27},{4,2},{5,29},{6,4},{7,31},{8,14},{9,1},{... | collective-permute-start | bytes 1572872 | tf_op jit(solution)/shard_map/ppermute | solution.py:474
  144.1 17.3 %collective-permute-start.7 = (f32[2,2,256,128]{3,2,1,0:T(8,128)S(1)}, f32[2,2,256,128]{3,2,1,0:T(8,128)S(1)}, u32[]{:S(2)}, u32[]{:S(2)}) collective-permute-start(f32[2,2,256,128]{3,2,1,0:T(8,128)S(1)} %get-tuple-element.122), channel_id=1, source_target_pairs={{0,4},{1,17},{2,6},{3,19},{4,0},{5,21},{6,2},{7,23},{8,12},{9,25},... | collective-permute-start | bytes 1572872 | tf_op jit(solution)/shard_map/ppermute | solution.py:474
  147.6 19.4 %collective-permute-start.6 = (f32[2,2,256,128]{3,2,1,0:T(8,128)S(1)}, f32[2,2,256,128]{3,2,1,0:T(8,128)S(1)}, u32[]{:S(2)}, u32[]{:S(2)}) collective-permute-start(f32[2,2,256,128]{3,2,1,0:T(8,128)S(1)} %get-tuple-element.120), channel_id=1, source_target_pairs={{0,2},{1,9},{2,4},{3,11},{4,6},{5,13},{6,0},{7,15},{8,10},{9,17},{... | collective-permute-start | bytes 1572872 | tf_op jit(solution)/shard_map/ppermute | solution.py:474
  155.9 15.1 %collective-permute-start.16 = (f32[2,256,128]{2,1,0:T(8,128)S(1)}, f32[2,256,128]{2,1,0:T(8,128)S(1)}, u32[]{:S(2)}, u32[]{:S(2)}) collective-permute-start(f32[2,256,128]{2,1,0:T(8,128)S(1)} %get-tuple-element.77), channel_id=1, source_target_pairs={{0,1},{1,0},{2,3},{3,2},{4,5},{5,4},{6,7},{7,6},{8,9},{9,8},{10,11... | collective-permute-start | bytes 786440 | tf_op jit(solution)/shard_map/ppermute | solution.py:479
  167.1 5.0 %collective-permute-start.9 = (f32[2,256,128]{2,1,0:T(8,128)S(1)}, f32[2,256,128]{2,1,0:T(8,128)S(1)}, u32[]{:S(2)}, u32[]{:S(2)}) collective-permute-start(f32[2,256,128]{2,1,0:T(8,128)S(1)} %get-tuple-element.79), channel_id=1, source_target_pairs={{0,1},{1,0},{2,3},{3,2},{4,5},{5,4},{6,7},{7,6},{8,9},{9,8},{10,11... | collective-permute-start | bytes 786440 | tf_op jit(solution)/shard_map/ppermute | solution.py:479

commit v4 on v3

--- a/solution.py
+++ b/solution.py
@@ -39,9 +39,7 @@
         hi, lo = split(table(s))
         cols = slice(s * LANES, (s + 1) * LANES)
         right_ref[slot, 0:64, cols] = hi
-        right_ref[slot, 64:128, cols] = hi
-        right_ref[slot, 128:192, cols] = lo
-        right_ref[slot, 192:256, cols] = lo
+        right_ref[slot, 64:128, cols] = lo
 
 
 def spread_rows(a_ref, spread_ref):
@@ -52,11 +50,15 @@
 
 
 def left_of(two):
-    hi = two.astype(jnp.bfloat16).astype(jnp.float32)
-    lo = pltpu.roll(two - hi, BS, axis=1)
+    other = pltpu.roll(two, BS, axis=1)
     first = first_half(two.shape)
-    rows = jnp.concatenate([jnp.where(first, hi, lo), jnp.where(first, lo, hi)], axis=0).astype(jnp.bfloat16)
-    return jnp.concatenate([rows, rows], axis=1)
+    rows = jnp.concatenate([jnp.where(first, two, other), jnp.where(first, other, two)], axis=0)
+    return jnp.concatenate(split(rows), axis=0)
+
+
+def weights_of(left, right):
+    both = jnp.dot(left, right, preferred_element_type=jnp.float32)
+    return both[0:BS] + both[BS : 2 * BS]
 
 
 def put_weights(w_ref, m, w):
@@ -119,7 +121,7 @@
     spread_rows(a_ref, spread_ref)
     for m in range(KG):
         left = left_of(spread_ref[m * (BS // 2) : (m + 1) * (BS // 2), :])
-        w = jnp.dot(left, right_ref[cols_ref[i * KG + m]], preferred_element_type=jnp.float32)
+        w = weights_of(left, right_ref[cols_ref[i * KG + m]])
         put_weights(w_ref, m, w)
 
     def per_target(j, carry):
@@ -157,7 +159,7 @@
             return far[m][0, s * BS : (s + 1) * BS, :]
 
         put_right(right_ref, m, table)
-        w = jnp.dot(left, right_ref[m], preferred_element_type=jnp.float32)
+        w = weights_of(left, right_ref[m])
         put_weights(w_ref, m, w)
 
     def per_two(jj, carry):
@@ -287,7 +289,7 @@
                 pl.BlockSpec((1, KP, LANES, LANES), lambda i, *_: (i, 0, 0, 0)),
             ),
             scratch_shapes=[
-                pltpu.VMEM((4 * RB, 256, KP * BS), jnp.bfloat16),
+                pltpu.VMEM((4 * RB, LANES, KP * BS), jnp.bfloat16),
                 pltpu.VMEM((2, NEAR_E // 2 + 1, BS, LANES), jnp.float32),
                 pltpu.VMEM((KA * BS // 2, LANES), jnp.float32),
             ],
@@ -316,7 +318,7 @@
             ],
             out_specs=(pl.BlockSpec(memory_space=pltpu.HBM),) * 5,
             scratch_shapes=[
-                pltpu.VMEM((KH, 256, KP * BS), jnp.bfloat16),
+                pltpu.VMEM((KH, LANES, KP * BS), jnp.bfloat16),
                 pltpu.VMEM((2, FAR_E // 2 + 1, BS, LANES), jnp.float32),
                 pltpu.VMEM((2, LANES, HALF_C * BS), jnp.bfloat16),
                 pltpu.VMEM((n_dom + 1,) + slot_shape, jnp.float32),
@@ -455,7 +457,7 @@
         chunks = far_call(
             half, far_cols, far_list, far_count, position, operator_blocks, far_rows, matched, left, n_dom
         )
-        sent = {t: lax.ppermute(chunks[t], "dom", shift_pairs(t, 0)) for t in (2, 1, 3)}
+        sent = {t: lax.ppermute(chunks[t], "dom", shift_pairs(t, 0)) for t in (1, 3, 2)}
         return lax.optimization_barrier((chunks[0], sent[1], sent[2], sent[3], chunks[4]))
 
     def second_phase(here):

time: 174 us -> 174 us (level)
  no operation moved by 1% of the time
where the time goes in v4:
time: 174 us; the launch traced here: 173 us
  waiting for transfers between devices  71.9 us (41%)
  starting transfers between devices  43.3 us (25%)
  Pallas kernels  41.1 us (24%)
  other arithmetic  10.9 us (6%)
  local copies, waits for them, and re-layouts  4.62 us (3%)
    ppermute x6, waiting for transfers between devices, first_phase(): lax.ppermute(chunks[t], 'dom', shift_pairs(t, 0))  28.7 us
    pallas_call x2, Pallas kernels, far_call(): pl.pallas_call(far_kernel, out_shape=tuple((jax.ShapeDtypeStruct((n,) + s...  21.6 us
    ppermute x3, waiting for transfers between devices, per_device(): lax.ppermute(passed, 'grp', [((z + dz) % n_grp, z) for z in range(n_grp)])  19.8 us
    ppermute x6, waiting for transfers between devices, second_phase(): lax.ppermute(owned(t2), 'dom', shift_pairs(t2, 1))  17.5 us
    pallas_call x1, Pallas kernels, near_call(): pl.pallas_call(near_kernel, out_shape=(jax.ShapeDtypeStruct((RB, KP, KC /...  12.8 us
    ppermute x6, starting transfers between devices, first_phase(): lax.ppermute(chunks[t], 'dom', shift_pairs(t, 0))  8.88 us
    all_to_all x1, starting transfers between devices, per_device(): lax.all_to_all(jnp.broadcast_to(mine[None], (n_dom,) + mine.shape), 'dom'...  8.59 us
    ppermute x2, starting transfers between devices, swap(): lax.ppermute(sums[0], 'dom', [(n, n ^ 1) for n in range(n_dom)])  7.53 us
  transfers between devices with their start and end apart: 19, of which 13 were waited for; matrix products, arithmetic and copies ran while one was open for 7% of the time, Pallas kernels for 17%

profile of v4, /device:TPU:1, one launch (start us, length us, event | category | flops | bytes accessed | tf_op | source)
XLA Modules:
  0.0 173.2 jit_solution(1153337731015649294)
XLA Ops:
  0.0 0.7 fusion.13
  0.7 0.8 reshape.964
  1.5 8.6 %all-to-all-start = ((s32[32,1,512]{2,1,0:T(1,128)}), s32[32,1,512]{2,1,0:T(1,128)S(1)}, u32[]{:S(2)}, u32[]{:S(2)}) async-start(s32[32,1,512]{2,1,0:T(1,128)} %reshape.964), calls=%async_computation | async-start | bytes 131072 | tf_op jit(solution)/shard_map/all_to_all | solution.py:402
  10.8 5.5 %outgoing.1 = (f32[32,256,128]{2,1,0:T(8,128)}, f32[1032,128]{1,0:T(8,128)}) custom-call(s32[32]{0:T(128)} %bitcast.78, f32[4,8,4096]{2,1,0:T(8,128)} %blocks_ref.1, s32[4,8]{1,0:T(4,128)} %ids_ref.1), custom_call_target="tpu_custom_call" | custom-call | bytes 6291456 | tf_op jit(solution)/shard_map/outgoing/pallas_call | solution.py:376
  16.3 0.7 slice_convert_fusion.3
  17.0 0.5 all-to-all-done
  17.5 7.1 %all-to-all-start.1 = ((f32[32,256,128]{2,1,0:T(8,128)}), f32[32,256,128]{2,1,0:T(8,128)}, u32[]{:S(2)}, u32[]{:S(2)}) async-start(f32[32,256,128]{2,1,0:T(8,128)} %get-tuple-element.40), calls=%async_computation.1 | async-start | bytes 8388608 | tf_op jit(solution)/shard_map/all_to_all | solution.py:398
  24.6 0.5 broadcast.621
  25.1 0.8 reduce.9
  26.8 0.6 select_reduce_fusion.6
  28.7 1.7 collective-permute-start.2
  30.4 3.3 %collective-permute-start.1 = (f32[1032,128]{1,0:T(8,128)S(1)}, f32[1032,128]{1,0:T(8,128)S(1)}, u32[]{:S(2)}, u32[]{:S(2)}) collective-permute-start(f32[1032,128]{1,0:T(8,128)S(1)} %copy-done.6), channel_id=1, source_target_pairs={{64,0},{96,32},{0,64},{32,96},{65,1},{97,33},{1,65},{33,97},{66,2}... | collective-permute-start | bytes 1585160 | tf_op jit(solution)/shard_map/ppermute | solution.py:428
  33.7 0.7 collective-permute-start
  35.4 0.6 select_reduce_fusion.4
  36.1 0.6 select_reduce_fusion.2
  37.2 7.6 %collective-permute-done.2.p3 = f32[1032,128]{1,0:T(8,128)S(1)} collective-permute-done((f32[1032,128]{1,0:T(8,128)S(1)}, f32[1032,128]{1,0:T(8,128)S(1)}, u32[]{:S(2)}, u32[]{:S(2)}) %collective-permute-start.2) | collective-permute-done | bytes 528416 | tf_op jit(solution)/shard_map/ppermute | solution.py:428
  44.8 12.2 %collective-permute-done.1.p2 = f32[1032,128]{1,0:T(8,128)S(1)} collective-permute-done((f32[1032,128]{1,0:T(8,128)S(1)}, f32[1032,128]{1,0:T(8,128)S(1)}, u32[]{:S(2)}, u32[]{:S(2)}) %collective-permute-start.1) | collective-permute-done | bytes 528416 | tf_op jit(solution)/shard_map/ppermute | solution.py:428
  57.7 0.6 select_reduce_fusion.1
  58.3 0.6 select_reduce_fusion
  59.1 0.7 select_n.560.list_ref
  59.8 12.8 %near.1 = (f32[4,8,8,64,128]{4,3,2,1,0:T(8,128)}, bf16[4,8,128,128]{3,2,1,0:T(8,128)(2,1)}) custom-call(s32[48]{0:T(128)} %copy-done.3, s32[3072]{0:T(1024)} %select_n.560.list_ref, s32[32]{0:T(128)} %copy-done.2, f32[4,16,4096]{2,1,0:T(8,128)} %a_ref.5, f32[1032,128]{1,0:T(8,128)} %get-tuple-element.42.p0, f32[1032,128]{1,0:T(8,128)} %copy-done.9, ...), custom_call_target="tpu_custom_call" | custom-call | flops 10000000000 | bytes 16777216 | tf_op jit(solution)/shard_map/near/pallas_call | solution.py:277
  72.5 4.3 %all-to-all-done.1.f0.f1.f2.f3 = f32[32,256,128]{2,1,0:T(8,128)} async-done(((f32[32,256,128]{2,1,0:T(8,128)}), f32[32,256,128]{2,1,0:T(8,128)}, u32[]{:S(2)}, u32[]{:S(2)}) %all-to-all-start.1) | async-done | bytes 4194336 | tf_op jit(solution)/shard_map/all_to_all | solution.py:398
  76.8 10.7 %far.3 = (f32[8,256,128]{2,1,0:T(8,128)S(1)}, f32[8,256,128]{2,1,0:T(8,128)S(1)}, f32[8,256,128]{2,1,0:T(8,128)S(1)}, f32[8,256,128]{2,1,0:T(8,128)S(1)}, f32[1,256,128]{2,1,0:T(8,128)S(1)}) custom-call(s32[16]{0:T(128)S(1)} %reshape.957.cols_ref, s32[1024]{0:T(1024)S(1)} %select_n.582.list_ref, s32[32]{0:T(128)S(1)} %get-tuple-element.143.count_ref, ...), custom_call_target="tpu_custom_call" | custom-call | flops 5000000000 | bytes 14680064 | tf_op jit(solution)/shard_map/far/pallas_call | solution.py:307
  87.5 3.3 %collective-permute-start.10 = (f32[8,256,128]{2,1,0:T(8,128)S(1)}, f32[8,256,128]{2,1,0:T(8,128)S(1)}, u32[]{:S(2)}, u32[]{:S(2)}) collective-permute-start(f32[8,256,128]{2,1,0:T(8,128)S(1)} %get-tuple-element.56), channel_id=1, source_target_pairs={{0,8},{1,3},{2,10},{3,5},{4,12},{5,7},{6,14},{7,1},{8,16},{9,11},{... | collective-permute-start | bytes 3145736 | tf_op jit(solution)/shard_map/ppermute | solution.py:460
  91.1 1.0 collective-permute-start.11
  92.1 1.4 collective-permute-start.12
  93.5 10.9 %far.2 = (f32[8,256,128]{2,1,0:T(8,128)S(1)}, f32[8,256,128]{2,1,0:T(8,128)S(1)}, f32[8,256,128]{2,1,0:T(8,128)S(1)}, f32[8,256,128]{2,1,0:T(8,128)S(1)}, f32[1,256,128]{2,1,0:T(8,128)S(1)}) custom-call(s32[16]{0:T(128)S(1)} %reshape.957.cols_ref, s32[1024]{0:T(1024)S(1)} %select_n.539.list_ref, s32[32]{0:T(128)S(1)} %get-tuple-element.75.count_ref, ...), custom_call_target="tpu_custom_call" | custom-call | flops 5000000000 | bytes 14680064 | tf_op jit(solution)/shard_map/far/pallas_call | solution.py:307
  104.4 0.4 collective-permute-start.3
  104.8 1.8 %collective-permute-start.4 = (f32[8,256,128]{2,1,0:T(8,128)S(1)}, f32[8,256,128]{2,1,0:T(8,128)S(1)}, u32[]{:S(2)}, u32[]{:S(2)}) collective-permute-start(f32[8,256,128]{2,1,0:T(8,128)S(1)} %get-tuple-element.47), channel_id=1, source_target_pairs={{0,16},{1,5},{2,18},{3,7},{4,20},{5,1},{6,22},{7,3},{8,24},{9,13},... | collective-permute-start | bytes 3145736 | tf_op jit(solution)/shard_map/ppermute | solution.py:460
  106.6 1.0 collective-permute-start.5
  107.6 0.5 slice.266
  109.1 6.3 %collective-permute-done.11 = f32[8,256,128]{2,1,0:T(8,128)S(1)} collective-permute-done((f32[8,256,128]{2,1,0:T(8,128)S(1)}, f32[8,256,128]{2,1,0:T(8,128)S(1)}, u32[]{:S(2)}, u32[]{:S(2)}) %collective-permute-start.11) | collective-permute-done | bytes 1048608 | tf_op jit(solution)/shard_map/ppermute | solution.py:460
  115.4 11.4 %collective-permute-done.3 = f32[8,256,128]{2,1,0:T(8,128)S(1)} collective-permute-done((f32[8,256,128]{2,1,0:T(8,128)S(1)}, f32[8,256,128]{2,1,0:T(8,128)S(1)}, u32[]{:S(2)}, u32[]{:S(2)}) %collective-permute-start.3) | collective-permute-done | bytes 1048608 | tf_op jit(solution)/shard_map/ppermute | solution.py:460
  126.8 11.0 %collective-permute-done.4 = f32[8,256,128]{2,1,0:T(8,128)S(1)} collective-permute-done((f32[8,256,128]{2,1,0:T(8,128)S(1)}, f32[8,256,128]{2,1,0:T(8,128)S(1)}, u32[]{:S(2)}, u32[]{:S(2)}) %collective-permute-start.4) | collective-permute-done | bytes 1048608 | tf_op jit(solution)/shard_map/ppermute | solution.py:460
  138.9 0.9 collective-permute-start.15
  140.1 0.7 collective-permute-start.14
  141.1 0.9 collective-permute-start.13
  142.1 1.8 %collective-permute-start.8 = (f32[2,2,256,128]{3,2,1,0:T(8,128)S(1)}, f32[2,2,256,128]{3,2,1,0:T(8,128)S(1)}, u32[]{:S(2)}, u32[]{:S(2)}) collective-permute-start(f32[2,2,256,128]{3,2,1,0:T(8,128)S(1)} %get-tuple-element.124), channel_id=1, source_target_pairs={{0,6},{1,25},{2,0},{3,27},{4,2},{5,29},{6,4},{7,31},{8,14},{9,1},{... | collective-permute-start | bytes 1572872 | tf_op jit(solution)/shard_map/ppermute | solution.py:476
  143.9 1.1 collective-permute-start.7
  145.0 2.2 %collective-permute-done.15 = f32[2,2,256,128]{3,2,1,0:T(8,128)S(1)} collective-permute-done((f32[2,2,256,128]{3,2,1,0:T(8,128)S(1)}, f32[2,2,256,128]{3,2,1,0:T(8,128)S(1)}, u32[]{:S(2)}, u32[]{:S(2)}) %collective-permute-start.15) | collective-permute-done | bytes 524320 | tf_op jit(solution)/shard_map/ppermute | solution.py:476
  147.7 2.3 %collective-permute-done.14 = f32[2,2,256,128]{3,2,1,0:T(8,128)S(1)} collective-permute-done((f32[2,2,256,128]{3,2,1,0:T(8,128)S(1)}, f32[2,2,256,128]{3,2,1,0:T(8,128)S(1)}, u32[]{:S(2)}, u32[]{:S(2)}) %collective-permute-start.14) | collective-permute-done | bytes 524320 | tf_op jit(solution)/shard_map/ppermute | solution.py:476
  150.0 5.6 %collective-permute-done.13 = f32[2,2,256,128]{3,2,1,0:T(8,128)S(1)} collective-permute-done((f32[2,2,256,128]{3,2,1,0:T(8,128)S(1)}, f32[2,2,256,128]{3,2,1,0:T(8,128)S(1)}, u32[]{:S(2)}, u32[]{:S(2)}) %collective-permute-start.13) | collective-permute-done | bytes 524320 | tf_op jit(solution)/shard_map/ppermute | solution.py:476
  155.7 3.8 %collective-permute-start.16 = (f32[2,256,128]{2,1,0:T(8,128)S(1)}, f32[2,256,128]{2,1,0:T(8,128)S(1)}, u32[]{:S(2)}, u32[]{:S(2)}) collective-permute-start(f32[2,256,128]{2,1,0:T(8,128)S(1)} %get-tuple-element.77), channel_id=1, source_target_pairs={{0,1},{1,0},{2,3},{3,2},{4,5},{5,4},{6,7},{7,6},{8,9},{9,8},{10,11... | collective-permute-start | bytes 786440 | tf_op jit(solution)/shard_map/ppermute | solution.py:481
  159.5 1.8 %collective-permute-done.7 = f32[2,2,256,128]{3,2,1,0:T(8,128)S(1)} collective-permute-done((f32[2,2,256,128]{3,2,1,0:T(8,128)S(1)}, f32[2,2,256,128]{3,2,1,0:T(8,128)S(1)}, u32[]{:S(2)}, u32[]{:S(2)}) %collective-permute-start.7) | collective-permute-done | bytes 524320 | tf_op jit(solution)/shard_map/ppermute | solution.py:476
  161.3 5.5 %collective-permute-done.6 = f32[2,2,256,128]{3,2,1,0:T(8,128)S(1)} collective-permute-done((f32[2,2,256,128]{3,2,1,0:T(8,128)S(1)}, f32[2,2,256,128]{3,2,1,0:T(8,128)S(1)}, u32[]{:S(2)}, u32[]{:S(2)}) %collective-permute-start.6) | collective-permute-done | bytes 524320 | tf_op jit(solution)/shard_map/ppermute | solution.py:476
  166.9 3.8 %collective-permute-start.9 = (f32[2,256,128]{2,1,0:T(8,128)S(1)}, f32[2,256,128]{2,1,0:T(8,128)S(1)}, u32[]{:S(2)}, u32[]{:S(2)}) collective-permute-start(f32[2,256,128]{2,1,0:T(8,128)S(1)} %get-tuple-element.79), channel_id=1, source_target_pairs={{0,1},{1,0},{2,3},{3,2},{4,5},{5,4},{6,7},{7,6},{8,9},{9,8},{10,11... | collective-permute-start | bytes 786440 | tf_op jit(solution)/shard_map/ppermute | solution.py:481
  170.7 1.2 collective-permute-done.9.refs_1_
  171.9 1.3 final.1
  (114 shorter events, 7.7 us)
Async XLA Ops:
  1.5 16.0 %all-to-all-start = ((s32[32,1,512]{2,1,0:T(1,128)}), s32[32,1,512]{2,1,0:T(1,128)S(1)}, u32[]{:S(2)}, u32[]{:S(2)}) async-start(s32[32,1,512]{2,1,0:T(1,128)} %reshape.964), calls=%async_computation | async-start | bytes 131072 | tf_op jit(solution)/shard_map/all_to_all | solution.py:402
  17.5 8.6 %copy-start.4 = (s32[4,8]{1,0:T(4,128)S(1)}, s32[4,8]{1,0:T(4,128)}, u32[]{:S(2)}) copy-start(s32[4,8]{1,0:T(4,128)} %param.14) | copy-start | bytes 388
  17.5 8.7 %copy-start.5 = (s32[1,64]{1,0:T(1,128)S(1)}, s32[1,64]{1,0:T(1,128)}, u32[]{:S(2)}) copy-start(s32[1,64]{1,0:T(1,128)} %param.16) | copy-start | bytes 772
  17.5 8.9 %copy-start.1 = (s32[4,16]{1,0:T(4,128)S(1)}, s32[4,16]{1,0:T(4,128)}, u32[]{:S(2)}) copy-start(s32[4,16]{1,0:T(4,128)} %param.10) | copy-start | bytes 772
  17.5 11.2 %copy-start.6 = (f32[1032,128]{1,0:T(8,128)S(1)}, f32[1032,128]{1,0:T(8,128)}, u32[]{:S(2)}) copy-start(f32[1032,128]{1,0:T(8,128)} %get-tuple-element.42.p0) | copy-start | bytes 1585156
  17.5 16.9 %copy-start.10 = (s32[4]{0:T(128)S(1)}, s32[4]{0:T(128)}, u32[]{:S(2)}) copy-start(s32[4]{0:T(128)} %param.11) | copy-start | bytes 52
  17.5 59.3 %all-to-all-start.1 = ((f32[32,256,128]{2,1,0:T(8,128)}), f32[32,256,128]{2,1,0:T(8,128)}, u32[]{:S(2)}, u32[]{:S(2)}) async-start(f32[32,256,128]{2,1,0:T(8,128)} %get-tuple-element.40), calls=%async_computation.1 | async-start | bytes 8388608 | tf_op jit(solution)/shard_map/all_to_all | solution.py:398
  28.7 16.1 %collective-permute-start.2 = (f32[1032,128]{1,0:T(8,128)S(1)}, f32[1032,128]{1,0:T(8,128)S(1)}, u32[]{:S(2)}, u32[]{:S(2)}) collective-permute-start(f32[1032,128]{1,0:T(8,128)S(1)} %copy-done.6), channel_id=1, source_target_pairs={{96,0},{0,32},{32,64},{64,96},{97,1},{1,33},{33,65},{65,97},{98,2}... | collective-permute-start | bytes 1585160 | tf_op jit(solution)/shard_map/ppermute | solution.py:428
  30.4 26.6 %collective-permute-start.1 = (f32[1032,128]{1,0:T(8,128)S(1)}, f32[1032,128]{1,0:T(8,128)S(1)}, u32[]{:S(2)}, u32[]{:S(2)}) collective-permute-start(f32[1032,128]{1,0:T(8,128)S(1)} %copy-done.6), channel_id=1, source_target_pairs={{64,0},{96,32},{0,64},{32,96},{65,1},{97,33},{1,65},{33,97},{66,2}... | collective-permute-start | bytes 1585160 | tf_op jit(solution)/shard_map/ppermute | solution.py:428
  33.7 23.3 %collective-permute-start = (f32[1032,128]{1,0:T(8,128)S(1)}, f32[1032,128]{1,0:T(8,128)S(1)}, u32[]{:S(2)}, u32[]{:S(2)}) collective-permute-start(f32[1032,128]{1,0:T(8,128)S(1)} %copy-done.6), channel_id=1, source_target_pairs={{32,0},{64,32},{96,64},{0,96},{33,1},{65,33},{97,65},{1,97},{34,2}... | collective-permute-start | bytes 1585160 | tf_op jit(solution)/shard_map/ppermute | solution.py:428
  37.0 22.7 %copy-start.3 = (s32[48]{0:T(128)}, s32[48]{0:T(128)S(1)}, u32[]{:S(2)}) copy-start(s32[48]{0:T(128)S(1)} %reshape.962.cols_ref) | copy-start | bytes 580
  44.8 15.0 %copy-start.7 = (f32[1032,128]{1,0:T(8,128)}, f32[1032,128]{1,0:T(8,128)S(1)}, u32[]{:S(2)}) copy-start(f32[1032,128]{1,0:T(8,128)S(1)} %collective-permute-done.2.p3) | copy-start | bytes 1585156
  56.9 2.8 %copy-start.8 = (f32[1032,128]{1,0:T(8,128)}, f32[1032,128]{1,0:T(8,128)S(1)}, u32[]{:S(2)}) copy-start(f32[1032,128]{1,0:T(8,128)S(1)} %collective-permute-done.1.p2) | copy-start | bytes 1585156
  56.9 2.8 %copy-start.9 = (f32[1032,128]{1,0:T(8,128)}, f32[1032,128]{1,0:T(8,128)S(1)}, u32[]{:S(2)}) copy-start(f32[1032,128]{1,0:T(8,128)S(1)} %collective-permute-done.p1) | copy-start | bytes 1585156
  57.5 2.2 %copy-start.2 = (s32[32]{0:T(128)}, s32[32]{0:T(128)S(1)}, u32[]{:S(2)}) copy-start(s32[32]{0:T(128)S(1)} %convert_reduce_fusion.1.count_ref) | copy-start | bytes 388
  59.8 17.1 %copy-start = (f32[4,16,4096]{2,1,0:T(8,128)S(1)}, f32[4,16,4096]{2,1,0:T(8,128)}, u32[]{:S(2)}) copy-start(f32[4,16,4096]{2,1,0:T(8,128)} %a_ref.5) | copy-start | bytes 3145732
  87.5 19.0 %collective-permute-start.10 = (f32[8,256,128]{2,1,0:T(8,128)S(1)}, f32[8,256,128]{2,1,0:T(8,128)S(1)}, u32[]{:S(2)}, u32[]{:S(2)}) collective-permute-start(f32[8,256,128]{2,1,0:T(8,128)S(1)} %get-tuple-element.56), channel_id=1, source_target_pairs={{0,8},{1,3},{2,10},{3,5},{4,12},{5,7},{6,14},{7,1},{8,16},{9,11},{... | collective-permute-start | bytes 3145736 | tf_op jit(solution)/shard_map/ppermute | solution.py:460
  91.1 24.3 %collective-permute-start.11 = (f32[8,256,128]{2,1,0:T(8,128)S(1)}, f32[8,256,128]{2,1,0:T(8,128)S(1)}, u32[]{:S(2)}, u32[]{:S(2)}) collective-permute-start(f32[8,256,128]{2,1,0:T(8,128)S(1)} %get-tuple-element.57), channel_id=1, source_target_pairs={{0,16},{1,5},{2,18},{3,7},{4,20},{5,1},{6,22},{7,3},{8,24},{9,13},... | collective-permute-start | bytes 3145736 | tf_op jit(solution)/shard_map/ppermute | solution.py:460
  92.1 23.3 %collective-permute-start.12 = (f32[8,256,128]{2,1,0:T(8,128)S(1)}, f32[8,256,128]{2,1,0:T(8,128)S(1)}, u32[]{:S(2)}, u32[]{:S(2)}) collective-permute-start(f32[8,256,128]{2,1,0:T(8,128)S(1)} %get-tuple-element.58), channel_id=1, source_target_pairs={{0,24},{1,7},{2,26},{3,1},{4,28},{5,3},{6,30},{7,5},{8,0},{9,15},{... | collective-permute-start | bytes 3145736 | tf_op jit(solution)/shard_map/ppermute | solution.py:460
  104.4 22.4 %collective-permute-start.3 = (f32[8,256,128]{2,1,0:T(8,128)S(1)}, f32[8,256,128]{2,1,0:T(8,128)S(1)}, u32[]{:S(2)}, u32[]{:S(2)}) collective-permute-start(f32[8,256,128]{2,1,0:T(8,128)S(1)} %get-tuple-element.46), channel_id=1, source_target_pairs={{0,8},{1,3},{2,10},{3,5},{4,12},{5,7},{6,14},{7,1},{8,16},{9,11},{... | collective-permute-start | bytes 3145736 | tf_op jit(solution)/shard_map/ppermute | solution.py:460
  104.8 33.0 %collective-permute-start.4 = (f32[8,256,128]{2,1,0:T(8,128)S(1)}, f32[8,256,128]{2,1,0:T(8,128)S(1)}, u32[]{:S(2)}, u32[]{:S(2)}) collective-permute-start(f32[8,256,128]{2,1,0:T(8,128)S(1)} %get-tuple-element.47), channel_id=1, source_target_pairs={{0,16},{1,5},{2,18},{3,7},{4,20},{5,1},{6,22},{7,3},{8,24},{9,13},... | collective-permute-start | bytes 3145736 | tf_op jit(solution)/shard_map/ppermute | solution.py:460
  106.6 31.2 %collective-permute-start.5 = (f32[8,256,128]{2,1,0:T(8,128)S(1)}, f32[8,256,128]{2,1,0:T(8,128)S(1)}, u32[]{:S(2)}, u32[]{:S(2)}) collective-permute-start(f32[8,256,128]{2,1,0:T(8,128)S(1)} %get-tuple-element.48), channel_id=1, source_target_pairs={{0,24},{1,7},{2,26},{3,1},{4,28},{5,3},{6,30},{7,5},{8,0},{9,15},{... | collective-permute-start | bytes 3145736 | tf_op jit(solution)/shard_map/ppermute | solution.py:460
  138.9 8.4 %collective-permute-start.15 = (f32[2,2,256,128]{3,2,1,0:T(8,128)S(1)}, f32[2,2,256,128]{3,2,1,0:T(8,128)S(1)}, u32[]{:S(2)}, u32[]{:S(2)}) collective-permute-start(f32[2,2,256,128]{3,2,1,0:T(8,128)S(1)} %get-tuple-element.123), channel_id=1, source_target_pairs={{0,6},{1,25},{2,0},{3,27},{4,2},{5,29},{6,4},{7,31},{8,14},{9,1},{... | collective-permute-start | bytes 1572872 | tf_op jit(solution)/shard_map/ppermute | solution.py:476
  140.1 10.0 %collective-permute-start.14 = (f32[2,2,256,128]{3,2,1,0:T(8,128)S(1)}, f32[2,2,256,128]{3,2,1,0:T(8,128)S(1)}, u32[]{:S(2)}, u32[]{:S(2)}) collective-permute-start(f32[2,2,256,128]{3,2,1,0:T(8,128)S(1)} %get-tuple-element.121), channel_id=1, source_target_pairs={{0,4},{1,17},{2,6},{3,19},{4,0},{5,21},{6,2},{7,23},{8,12},{9,25},... | collective-permute-start | bytes 1572872 | tf_op jit(solution)/shard_map/ppermute | solution.py:476
  141.1 14.5 %collective-permute-start.13 = (f32[2,2,256,128]{3,2,1,0:T(8,128)S(1)}, f32[2,2,256,128]{3,2,1,0:T(8,128)S(1)}, u32[]{:S(2)}, u32[]{:S(2)}) collective-permute-start(f32[2,2,256,128]{3,2,1,0:T(8,128)S(1)} %get-tuple-element.119), channel_id=1, source_target_pairs={{0,2},{1,9},{2,4},{3,11},{4,6},{5,13},{6,0},{7,15},{8,10},{9,17},{... | collective-permute-start | bytes 1572872 | tf_op jit(solution)/shard_map/ppermute | solution.py:476
  142.1 17.4 %collective-permute-start.8 = (f32[2,2,256,128]{3,2,1,0:T(8,128)S(1)}, f32[2,2,256,128]{3,2,1,0:T(8,128)S(1)}, u32[]{:S(2)}, u32[]{:S(2)}) collective-permute-start(f32[2,2,256,128]{3,2,1,0:T(8,128)S(1)} %get-tuple-element.124), channel_id=1, source_target_pairs={{0,6},{1,25},{2,0},{3,27},{4,2},{5,29},{6,4},{7,31},{8,14},{9,1},{... | collective-permute-start | bytes 1572872 | tf_op jit(solution)/shard_map/ppermute | solution.py:476
  143.9 17.3 %collective-permute-start.7 = (f32[2,2,256,128]{3,2,1,0:T(8,128)S(1)}, f32[2,2,256,128]{3,2,1,0:T(8,128)S(1)}, u32[]{:S(2)}, u32[]{:S(2)}) collective-permute-start(f32[2,2,256,128]{3,2,1,0:T(8,128)S(1)} %get-tuple-element.122), channel_id=1, source_target_pairs={{0,4},{1,17},{2,6},{3,19},{4,0},{5,21},{6,2},{7,23},{8,12},{9,25},... | collective-permute-start | bytes 1572872 | tf_op jit(solution)/shard_map/ppermute | solution.py:476
  147.3 19.6 %collective-permute-start.6 = (f32[2,2,256,128]{3,2,1,0:T(8,128)S(1)}, f32[2,2,256,128]{3,2,1,0:T(8,128)S(1)}, u32[]{:S(2)}, u32[]{:S(2)}) collective-permute-start(f32[2,2,256,128]{3,2,1,0:T(8,128)S(1)} %get-tuple-element.120), channel_id=1, source_target_pairs={{0,2},{1,9},{2,4},{3,11},{4,6},{5,13},{6,0},{7,15},{8,10},{9,17},{... | collective-permute-start | bytes 1572872 | tf_op jit(solution)/shard_map/ppermute | solution.py:476
  155.7 15.0 %collective-permute-start.16 = (f32[2,256,128]{2,1,0:T(8,128)S(1)}, f32[2,256,128]{2,1,0:T(8,128)S(1)}, u32[]{:S(2)}, u32[]{:S(2)}) collective-permute-start(f32[2,256,128]{2,1,0:T(8,128)S(1)} %get-tuple-element.77), channel_id=1, source_target_pairs={{0,1},{1,0},{2,3},{3,2},{4,5},{5,4},{6,7},{7,6},{8,9},{9,8},{10,11... | collective-permute-start | bytes 786440 | tf_op jit(solution)/shard_map/ppermute | solution.py:481
  166.9 4.9 %collective-permute-start.9 = (f32[2,256,128]{2,1,0:T(8,128)S(1)}, f32[2,256,128]{2,1,0:T(8,128)S(1)}, u32[]{:S(2)}, u32[]{:S(2)}) collective-permute-start(f32[2,256,128]{2,1,0:T(8,128)S(1)} %get-tuple-element.79), channel_id=1, source_target_pairs={{0,1},{1,0},{2,3},{3,2},{4,5},{5,4},{6,7},{7,6},{8,9},{9,8},{10,11... | collective-permute-start | bytes 786440 | tf_op jit(solution)/shard_map/ppermute | solution.py:481
